TPU v7x, 32 devices: a whole 2x2x4 slice. The times are simulated.
32 devices in a mesh: band: 4 (over x, core), col: 8 (over z, y).
Axes of the slice: x: 2, y: 2, z: 4, core: 2. Of those that a mesh axis runs over, the one named last changes fastest.
Arguments:
- adjoint_tend: bfloat16 [8, 40, 4, 5120], P('col', None, 'band'), may hold values from -6 to 6
- trajectory: bfloat16 [40, 4, 5120], P(None, 'band', 'col'), may hold values from -3 to 3
- coupling: bfloat16 [40, 40], replicated, may hold values from -1 to 1
- row_lat: int32 [4], P('band'), may hold values from 0 to 2559, as said below
- row_points: int32 [4], P('band'), may hold values from 20 to 5120, as said below
- wave_order: int32 [768], replicated, may hold values from 0 to 767, each once
Outputs:
- spectra: bfloat16 [8, 2, 40, 4, 768], P('col', None, None, None, 'band')
Inputs may be any that keep to these rules, and one draw needn't show every extreme that they name: `row_lat`: latitude rows are counted from the north pole. `row_points`: the row of latitude index i has min(20 + 4 d, 5120) points, d = min(i, 2559 - i), placed at point indices 0 to that number minus one; the rest of the row slot is unused.
All inputs are finite; a program needn't handle non-finite values.
Results may differ from a plain program's by a relative error of at most 0.0055.
Values may be sent and summed in bfloat16 or wider, within the bound.
No kernel may reach another device: no remote copies, remote signals or barrier semaphores. Data moves between devices by JAX's collectives and lax.ppermute only.
A program may use at most 64 MiB of HBM per device.

v0:
```python
import math

import jax
import jax.numpy as jnp
from jax import lax
from jax.sharding import PartitionSpec as P

LEVELS = 8
LATITUDES = 2560


def latitude_factor(row_lat):
    ratio = (2.0 * row_lat.astype(jnp.float32) + 1.0) / LATITUDES
    return jnp.sin(0.5 * math.pi * (1.0 - ratio))


def grid_adjoint(tend_block, traj_block, coupling, coriolis, row_points, first_point):
    width = tend_block.shape[3]
    driven = jnp.einsum("ab,brp->arp", coupling, traj_block, preferred_element_type=jnp.float32)
    tend_wide = tend_block.astype(jnp.float32)
    weighted = tend_wide * (1.0 + traj_block.astype(jnp.float32))[None]
    backed = jnp.einsum(
        "ab,karp->kbrp", coupling.astype(jnp.float32), weighted, precision=lax.Precision.HIGHEST
    )
    total = backed + tend_wide * driven[None]
    turning = coriolis[None, None, :, None]
    eastward = tend_wide[:, :LEVELS]
    northward = tend_wide[:, LEVELS : 2 * LEVELS]
    total = jnp.concatenate(
        [
            total[:, :LEVELS] - turning * northward,
            total[:, LEVELS : 2 * LEVELS] + turning * eastward,
            total[:, 2 * LEVELS :],
        ],
        axis=1,
    )
    places = first_point + jnp.arange(width, dtype=jnp.int32)
    keep = places[None, :] < row_points[:, None]
    return jnp.where(keep[None, None], total, 0.0).astype(jnp.bfloat16)


def wave_table(points, waves, width):
    places = jnp.arange(width, dtype=jnp.int32)
    phase = places[:, None] * waves[None, :] % points
    angle = phase.astype(jnp.float32) * (2.0 * math.pi) / points.astype(jnp.float32)
    keep = (2 * waves < points)[None, :]
    cosine = jnp.where(keep, jnp.cos(angle), 0.0)
    sine = jnp.where(keep, -jnp.sin(angle), 0.0)
    return jnp.concatenate([cosine, sine], axis=1).astype(jnp.bfloat16)


def body(adjoint_tend, trajectory, coupling, row_lat, row_points, wave_order):
    coriolis = latitude_factor(row_lat)
    members = adjoint_tend.shape[0]
    column_vars = adjoint_tend.shape[1]
    spread = lax.all_to_all(adjoint_tend, "col", split_axis=3, concat_axis=0, tiled=True)
    first_point = lax.axis_index("col") * trajectory.shape[2]
    grid_local = grid_adjoint(spread, trajectory, coupling, coriolis, row_points, first_point)
    grid = lax.all_to_all(grid_local, "col", split_axis=0, concat_axis=3, tiled=True)
    width = grid.shape[3]
    waves_total = wave_order.shape[0]
    block = math.gcd(waves_total, 256)
    points = row_points[0]
    flat = grid[:, :, 0, :].reshape(members * column_vars, width)
    root = jnp.sqrt(points.astype(jnp.float32))
    cosines = []
    sines = []
    for first_wave in range(0, waves_total, block):
        table = wave_table(points, wave_order[first_wave : first_wave + block], width)
        coeffs = jnp.dot(flat, table, preferred_element_type=jnp.float32) / root
        cosines.append(coeffs[:, :block])
        sines.append(coeffs[:, block:])
    real_part = (
        jnp.concatenate(cosines, axis=1)
        .astype(jnp.bfloat16)
        .reshape(members, column_vars, waves_total)
    )
    imag_part = (
        jnp.concatenate(sines, axis=1)
        .astype(jnp.bfloat16)
        .reshape(members, column_vars, waves_total)
    )
    per_row = [jnp.stack([real_part, imag_part], axis=1)]
    spectra = jnp.stack(per_row, axis=3)
    return lax.all_to_all(spectra, "band", split_axis=4, concat_axis=3, tiled=True)


def solution(mesh):
    return jax.shard_map(
        body,
        mesh=mesh,
        in_specs=(
            P("col", None, "band", None),
            P(None, "band", "col"),
            P(),
            P("band"),
            P("band"),
            P(),
        ),
        out_specs=P("col", None, None, None, "band"),
        check_vma=False,
    )
```

profile of v0, /device:TPU:0, one launch (start us, length us, event | category | flops | bytes accessed | tf_op | source)
XLA Modules:
  0.0 291.2 jit_solution(207323912714518692)
XLA Ops:
  0.0 4.3 %copy.19 = bf16[1,40,1,5120]{1,2,0,3:T(2,128)(2,1)S(1)} copy(bf16[1,40,1,5120]{3,1,2,0:T(8,128)(2,1)} %param.6) | data formatting | bytes 819200 | tf_op args[0]
  4.3 0.5 broadcast.80
  4.8 28.9 %reduce = bf16[5120,40]{1,0:T(8,128)(2,1)} reduce(bf16[5120,1,1,40]{3,2,1,0:T(2,128)(2,1)S(1)} %bitcast.78, bf16[]{:T(256)} %broadcast.80), dimensions={1,2}, to_apply=%bitcast.63.reduce_sub_computation | reduce | bytes 819202
  33.8 4.2 %reshape.209 = bf16[8,2,12800]{2,1,0:T(2,128)(2,1)} reshape(bf16[5120,40]{1,0:T(8,128)(2,1)} %reduce) | data formatting | bytes 819200
  38.0 7.3 %all-to-all-start = ((bf16[8,2,12800]{2,1,0:T(2,128)(2,1)}), bf16[8,2,12800]{2,1,0:T(2,128)(2,1)S(1)}, u32[]{:S(2)}, u32[]{:S(2)}) async-start(bf16[8,2,12800]{2,1,0:T(2,128)(2,1)} %reshape.209), calls=%async_computation | async-start | bytes 819200 | tf_op jit(solution)/shard_map/all_to_all | solution.py:56
  46.0 143.3 %select_convert_fusion.1 = (bf16[5120,256]{1,0:T(8,128)(2,1)}, bf16[5120,256]{1,0:T(8,128)(2,1)}, bf16[5120,256]{1,0:T(8,128)(2,1)}, bf16[5120,256]{1,0:T(8,128)(2,1)}) fusion(pred[256]{0:T(512)(128)(4,1)S(1)} %get-tuple-element.15, f32[]{:T(128)S(6)} %convert_element_type.95, pred[]{:T(512)S(6)} %lt.52, s32[]{:T(128)S(6)} %select_n.49, ...), kind=kLoop, calls=%fused_computation.25 | loop fusion | flops 41943040 | bytes 10488329 | tf_op jit(solution)/shard_map/convert.24
  190.1 0.1 fusion.60
  190.3 3.6 %reshape.210 = bf16[5120,1,1,40]{3,2,1,0:T(2,128)(2,1)S(1)} reshape(bf16[8,2,12800]{2,1,0:T(2,128)(2,1)S(1)} %all-to-all-done) | data formatting | bytes 819200
  193.9 1.4 copy.20
  195.3 0.1 convert_element_type.102
  195.4 0.6 fusion.33
  196.1 0.8 fusion.56
  196.9 6.0 %all-to-all-start.1 = ((bf16[8,40,1,640]{3,1,2,0:T(8,128)(2,1)}), bf16[8,40,1,640]{3,1,2,0:T(8,128)(2,1)S(1)}, u32[]{:S(2)}, u32[]{:S(2)}) async-start(bf16[8,40,1,640]{3,1,2,0:T(8,128)(2,1)} %fusion.56), calls=%async_computation.1 | async-start | bytes 819200 | tf_op jit(solution)/shard_map/all_to_all | solution.py:59
  202.9 71.6 %select_convert_fusion.5 = (bf16[5120,256]{1,0:T(8,128)(2,1)S(1)}, bf16[5120,256]{1,0:T(8,128)(2,1)}) fusion(f32[]{:T(128)S(6)} %convert_element_type.95, pred[]{:T(512)S(6)} %lt.52, s32[]{:T(128)S(6)} %select_n.49, s32[256]{0:T(256)S(1)} %get-tuple-element.16, pred[256]{0:T(512)(128)(4,1)S(1)} %get-tuple-element.13), kind=kLoop, calls=%fused_computation.35 | loop fusion | flops 20971520 | bytes 5244169 | tf_op jit(solution)/shard_map/convert.28
  274.6 3.6 %fusion.37 = bf16[40,512]{1,0:T(8,128)(2,1)S(1)} fusion(bf16[40,5120]{1,0:T(8,128)(2,1)S(1)} %bitcast.86, bf16[5120,256]{1,0:T(8,128)(2,1)} %get-tuple-element.24, bf16[5120,256]{1,0:T(8,128)(2,1)} %get-tuple-element.23, f32[]{:T(128)S(6)} %sqrt.3), kind=kOutput, calls=%fused_computation.48 | convolution fusion | flops 220241920 | bytes 5693444 | tf_op jit(solution)/shard_map/dot_general | solution.py:70
  278.2 0.4 copy-done.3
  278.7 1.0 fusion.43
  279.7 0.7 copy-done.1
  280.4 1.0 fusion.49
  281.4 0.4 copy.25
  281.8 0.6 reshape.211
  282.4 7.1 %all_to_all.36 = bf16[4,2,7680]{2,1,0:T(2,128)(2,1)S(1)} all-to-all(bf16[4,2,7680]{2,1,0:T(2,128)(2,1)S(1)} %reshape.211), channel_id=1, replica_groups=mesh['band'=4,'col'=8] {'band'}, dimensions={0} | all-to-all | bytes 245760 | tf_op jit(solution)/shard_map/all_to_all | solution.py:85
  289.5 0.6 reshape.212
  290.1 1.1 copy.26
  (24 shorter events, 0.2 us)
Async XLA Ops:
  0.0 190.1 %copy-start = (bf16[40,40]{1,0:T(8,128)(2,1)S(1)}, bf16[40,40]{1,0:T(8,128)(2,1)}, u32[]{:S(2)}) copy-start(bf16[40,40]{1,0:T(8,128)(2,1)} %param.8) | copy-start | bytes 9604
  4.8 41.1 %copy-start.5 = (s32[768]{0:T(1024)S(1)}, s32[768]{0:T(1024)}, u32[]{:S(2)}) copy-start(s32[768]{0:T(1024)} %param.11) | copy-start | bytes 9220
  38.0 152.3 %all-to-all-start = ((bf16[8,2,12800]{2,1,0:T(2,128)(2,1)}), bf16[8,2,12800]{2,1,0:T(2,128)(2,1)S(1)}, u32[]{:S(2)}, u32[]{:S(2)}) async-start(bf16[8,2,12800]{2,1,0:T(2,128)(2,1)} %reshape.209), calls=%async_computation | async-start | bytes 819200 | tf_op jit(solution)/shard_map/all_to_all | solution.py:56
  46.0 144.1 %copy-start.4 = (bf16[40,1,640]{2,0,1:T(8,128)(2,1)S(1)}, bf16[40,1,640]{2,0,1:T(8,128)(2,1)}, u32[]{:S(2)}) copy-start(bf16[40,1,640]{2,0,1:T(8,128)(2,1)} %param.7) | copy-start | bytes 153604
  196.9 77.6 %all-to-all-start.1 = ((bf16[8,40,1,640]{3,1,2,0:T(8,128)(2,1)}), bf16[8,40,1,640]{3,1,2,0:T(8,128)(2,1)S(1)}, u32[]{:S(2)}, u32[]{:S(2)}) async-start(bf16[8,40,1,640]{3,1,2,0:T(8,128)(2,1)} %fusion.56), calls=%async_computation.1 | async-start | bytes 819200 | tf_op jit(solution)/shard_map/all_to_all | solution.py:59
  274.6 3.7 %copy-start.2 = (bf16[5120,256]{1,0:T(8,128)(2,1)S(1)}, bf16[5120,256]{1,0:T(8,128)(2,1)}, u32[]{:S(2)}) copy-start(bf16[5120,256]{1,0:T(8,128)(2,1)} %get-tuple-element.25) | copy-start | bytes 7864324
  274.6 4.1 %copy-start.3 = (bf16[5120,256]{1,0:T(8,128)(2,1)S(1)}, bf16[5120,256]{1,0:T(8,128)(2,1)}, u32[]{:S(2)}) copy-start(bf16[5120,256]{1,0:T(8,128)(2,1)} %get-tuple-element.26) | copy-start | bytes 7864324
  278.7 1.7 copy-start.1
where the time goes:
time: 292 us; the launch traced here: 291 us
  other arithmetic  245 us (84%)
  local copies, waits for them, and re-layouts  18 us (6%)
  starting transfers between devices  13.3 us (5%)
  blocking collectives  7.11 us (2%)
  matrix products  6.36 us (2%)
    another operation x2, other arithmetic  215 us
    unnamed x1, other arithmetic  28.9 us
    unnamed x19, local copies, waits for them, and re-layouts  15 us
    all_to_all x1, starting transfers between devices, body(): lax.all_to_all(adjoint_tend, 'col', split_axis=3, concat_axis=0, tiled=True)  7.28 us
    all_to_all x1, blocking collectives, body(): lax.all_to_all(spectra, 'band', split_axis=4, concat_axis=3, tiled=True)  7.11 us
    all_to_all x1, starting transfers between devices, body(): lax.all_to_all(grid_local, 'col', split_axis=0, concat_axis=3, tiled=True)  6 us
  transfers between devices with their start and end apart: 2, of which 0 were waited for; matrix products, arithmetic and copies ran while one was open for 74% of the time, Pallas kernels for 0%

commit v1 on v0

v1 whole, which is shorter than its diff:
```python
import functools
import math

import jax
import jax.numpy as jnp
from jax import lax
from jax.experimental import pallas as pl
from jax.experimental.pallas import tpu as pltpu
from jax.sharding import PartitionSpec as P

LEVELS = 8
LATITUDES = 2560
LANES = 128
SUB = 32


def partner(place, step, count):
    if count & (count - 1) == 0:
        return place ^ step
    return (place + step) % count


def source(place, step, count):
    if count & (count - 1) == 0:
        return place ^ step
    return (place - step) % count


def turn(places, waves, points):
    product = places * waves
    whole = jnp.floor(product * (1.0 / points) + 0.5)
    quarter = (product - whole * points) * 4.0 / points
    nearest = jnp.floor(quarter + 0.5)
    angle = (quarter - nearest) * (0.5 * math.pi)
    square = angle * angle
    sine = angle + angle * square * (
        -1.6666654611e-1 + square * (8.3321608736e-3 - square * 1.9515295891e-4)
    )
    cosine = (
        1.0
        - 0.5 * square
        + square
        * square
        * (4.166664568298827e-2 + square * (-1.388731625493765e-3 + square * 2.443315711809948e-5))
    )
    odd = jnp.abs(nearest) == 1.0
    first = jnp.where(odd, sine, cosine)
    second = jnp.where(odd, cosine, sine)
    first = jnp.where((nearest == 1.0) | (jnp.abs(nearest) >= 2.0), -first, first)
    second = jnp.where((nearest == -1.0) | (jnp.abs(nearest) >= 2.0), -second, second)
    return first, -second


def main_kernel(blocks, block, parts, *refs):
    index_ref, lat_ref, points_ref, waves_ref, mix_ref, tend_ref = refs[:6]
    traj_refs = refs[6 : 6 + blocks]
    out_refs = refs[6 + blocks : 6 + blocks + parts]
    table_ref, grid_ref = refs[6 + blocks + parts :]
    column_vars = tend_ref.shape[0]
    waves_total = waves_ref.shape[1]
    share = waves_total // parts
    count = points_ref[0]
    points = jnp.full((1, 1), count, jnp.int32).astype(jnp.float32)
    waves = waves_ref[...].astype(jnp.float32)

    coarse_rows = block // SUB
    coarse_pad = -(-coarse_rows // 8) * 8
    fine = lax.broadcasted_iota(jnp.int32, (SUB, 1), 0).astype(jnp.float32)
    coarse = lax.broadcasted_iota(jnp.int32, (coarse_pad, 1), 0).astype(jnp.float32) * SUB
    fine_cos, fine_sin = turn(fine, waves, points)
    coarse_cos, coarse_sin = turn(coarse, waves, points)
    for row in range(coarse_rows):
        here_cos = coarse_cos[row : row + 1]
        here_sin = coarse_sin[row : row + 1]
        rows = pl.ds(row * SUB, SUB)
        table_ref[rows, :waves_total] = (here_cos * fine_cos - here_sin * fine_sin).astype(
            jnp.bfloat16
        )
        table_ref[rows, waves_total:] = (here_cos * fine_sin + here_sin * fine_cos).astype(
            jnp.bfloat16
        )

    slot = lax.broadcasted_iota(jnp.int32, (blocks, 1), 0)
    first = jnp.zeros((blocks, 1), jnp.int32)
    for i in range(blocks):
        first = jnp.where(slot == i, index_ref[i] * block, first)
    phase_cos, phase_sin = turn(first.astype(jnp.float32), waves, points)
    scale = jnp.where(2.0 * waves < points, 1.0 / jnp.sqrt(points), 0.0)
    phase_cos = phase_cos * scale
    phase_sin = phase_sin * scale

    latitude = jnp.full((1, 1), lat_ref[0], jnp.int32).astype(jnp.float32)
    ratio = (2.0 * latitude + 1.0) / LATITUDES
    _, coriolis = turn(0.25 * (ratio - 1.0), jnp.ones((1, LANES), jnp.float32), 1.0)
    coriolis = coriolis[:, :1]

    mix = mix_ref[...]
    for i in range(blocks):
        start = index_ref[i] * block
        traj = traj_refs[i][...].astype(jnp.float32)
        tend = tend_ref[:, pl.ds(pl.multiple_of(start, LANES), block)].astype(jnp.float32)
        stacked = jnp.concatenate([traj, tend, tend * traj], axis=0).astype(jnp.bfloat16)
        mixed = jnp.dot(mix, stacked, preferred_element_type=jnp.float32)
        total = mixed[column_vars:] + tend * mixed[:column_vars]
        total = jnp.concatenate(
            [
                total[:LEVELS] - coriolis * tend[LEVELS : 2 * LEVELS],
                total[LEVELS : 2 * LEVELS] + coriolis * tend[:LEVELS],
                total[2 * LEVELS :],
            ],
            axis=0,
        )
        place = start + lax.broadcasted_iota(jnp.int32, (1, block), 1)
        grid_ref[pl.ds(i * column_vars, column_vars), :] = jnp.where(place < count, total, 0.0)

    flat = grid_ref[...].astype(jnp.bfloat16)
    reals = []
    imags = []
    width = math.gcd(waves_total, 256)
    for first_wave in range(0, waves_total, width):
        cols = slice(first_wave, first_wave + width)
        near_cos = jnp.dot(flat, table_ref[:, cols], preferred_element_type=jnp.float32)
        near_sin = jnp.dot(
            flat,
            table_ref[:, waves_total + first_wave : waves_total + first_wave + width],
            preferred_element_type=jnp.float32,
        )
        real = jnp.zeros((column_vars, width), jnp.float32)
        imag = jnp.zeros((column_vars, width), jnp.float32)
        for i in range(blocks):
            rows = slice(i * column_vars, (i + 1) * column_vars)
            far_cos = phase_cos[i : i + 1, cols]
            far_sin = phase_sin[i : i + 1, cols]
            real = real + (far_cos * near_cos[rows] - far_sin * near_sin[rows])
            imag = imag + (far_cos * near_sin[rows] + far_sin * near_cos[rows])
        reals.append(real)
        imags.append(imag)
    both = jnp.concatenate(
        [jnp.concatenate(reals, axis=1), jnp.concatenate(imags, axis=1)], axis=0
    )
    for k in range(parts):
        out_refs[k][...] = both[:, k * share : (k + 1) * share].astype(jnp.bfloat16)


def place_kernel(parts, *refs):
    target_ref = refs[0]
    in_refs = refs[1 : 1 + parts]
    out_ref = refs[1 + parts]
    total = target_ref.shape[0]
    column_vars = total // parts
    choose = (
        target_ref[...] == lax.broadcasted_iota(jnp.int32, (total, total), 1)
    ).astype(jnp.bfloat16)
    wide = [ref[...].astype(jnp.float32) for ref in in_refs]
    for half in range(2):
        rows = slice(half * column_vars, (half + 1) * column_vars)
        stacked = jnp.concatenate([w[rows] for w in wide], axis=0).astype(jnp.bfloat16)
        out_ref[half] = jnp.dot(
            choose, stacked, preferred_element_type=jnp.float32
        ).astype(jnp.bfloat16)


VMEM_SPEC = pl.BlockSpec(memory_space=pltpu.VMEM)
SMEM_SPEC = pl.BlockSpec(memory_space=pltpu.SMEM)


def body(cols, bands, adjoint_tend, trajectory, coupling, row_lat, row_points, wave_order):
    column_vars = adjoint_tend.shape[1]
    width = adjoint_tend.shape[3]
    own = trajectory.shape[2]
    waves_total = wave_order.shape[0]
    share = waves_total // bands
    my_col = lax.axis_index("col")
    my_band = lax.axis_index("band")
    tend = adjoint_tend.reshape(column_vars, width)
    traj = trajectory.reshape(column_vars, own)

    if own % LANES == 0:
        block = own
        pieces = [traj]
        indices = [my_col]
        for step in range(1, cols):
            pairs = [(i, partner(i, step, cols)) for i in range(cols)]
            pieces.append(lax.ppermute(traj, "col", pairs))
            indices.append(source(my_col, step, cols))
        indices = jnp.stack(indices)
    else:
        block = width // 8
        whole = lax.all_gather(traj, "col", axis=1, tiled=True)
        pieces = [whole[:, i * block : (i + 1) * block] for i in range(8)]
        indices = jnp.arange(8, dtype=jnp.int32)
    blocks = len(pieces)

    waves = jnp.concatenate(
        [
            lax.dynamic_slice_in_dim(wave_order, partner(my_band, k, bands) * share, share)
            for k in range(bands)
        ]
    ).reshape(1, waves_total)
    none = jnp.zeros_like(coupling)
    mix = jnp.concatenate(
        [
            jnp.concatenate([coupling, none, none], axis=1),
            jnp.concatenate([none, coupling.T, coupling.T], axis=1),
        ],
        axis=0,
    )
    flops = 2 * column_vars * width * 2 * waves_total
    parts = pl.pallas_call(
        functools.partial(main_kernel, blocks, block, bands),
        out_shape=[jax.ShapeDtypeStruct((2 * column_vars, share), jnp.bfloat16)] * bands,
        in_specs=[SMEM_SPEC] * 3 + [VMEM_SPEC] * (3 + blocks),
        out_specs=[VMEM_SPEC] * bands,
        scratch_shapes=[
            pltpu.VMEM((block, 2 * waves_total), jnp.bfloat16),
            pltpu.VMEM((blocks * column_vars, block), jnp.float32),
        ],
        compiler_params=pltpu.CompilerParams(vmem_limit_bytes=40 * 1024 * 1024),
        cost_estimate=pl.CostEstimate(
            flops=flops, bytes_accessed=4 * column_vars * width, transcendentals=0
        ),
        name="column_and_waves",
    )(indices, row_lat, row_points, waves, mix, tend, *pieces)

    arrived = [parts[0]]
    for step in range(1, bands):
        pairs = [(i, partner(i, step, bands)) for i in range(bands)]
        arrived.append(lax.ppermute(parts[step], "band", pairs))
    row = jnp.arange(column_vars * bands, dtype=jnp.int32)
    variable, slot = row // bands, row % bands
    step_of = slot ^ my_band if bands & (bands - 1) == 0 else (my_band - slot) % bands
    target = (step_of * column_vars + variable).reshape(-1, 1)
    spectra = pl.pallas_call(
        functools.partial(place_kernel, bands),
        out_shape=jax.ShapeDtypeStruct((2, column_vars * bands, share), jnp.bfloat16),
        in_specs=[VMEM_SPEC] * (1 + bands),
        out_specs=VMEM_SPEC,
        name="row_slots",
    )(target, *arrived)
    return spectra.reshape(1, 2, column_vars, bands, share)


def solution(mesh):
    return jax.shard_map(
        functools.partial(body, mesh.shape["col"], mesh.shape["band"]),
        mesh=mesh,
        in_specs=(
            P("col", None, "band", None),
            P(None, "band", "col"),
            P(),
            P("band"),
            P("band"),
            P(),
        ),
        out_specs=P("col", None, None, None, "band"),
        check_vma=False,
    )
```

time: 292 us -> 30.7 us (0.11)
  other arithmetic: 245 us -> 0.81 us
  local copies, waits for them, and re-layouts: 18 us -> 4.82 us
  blocking collectives: 7.11 us -> 0 us
  matrix products: 6.36 us -> 0 us
  waiting for transfers between devices: 0.01 us -> 4.82 us
  Pallas kernels: 0 us -> 4.15 us
    another operation x3 -> x0, other arithmetic: 215 us -> none
    unnamed x1 -> x0, other arithmetic: 28.9 us -> none
    ppermute x0 -> x10, starting transfers between devices: none -> 14.4 us  [the longest x7 12.5 us: body(): pieces.append(lax.ppermute(traj, 'col', pairs))]
    all_to_all x2 -> x0, starting transfers between devices: 13.3 us -> none  [the longest x1 7.28 us: body(): lax.all_to_all(adjoint_tend, 'col', split_axis=3, concat_axis=0, tiled=True)]
    unnamed x19 -> x17, local copies, waits for them, and re-layouts: 15 us -> 3.01 us
    all_to_all x1 -> x0, blocking collectives: 7.11 us -> none  [body(): lax.all_to_all(spectra, 'band', split_axis=4, concat_axis=3, tiled=True)]
    dot_general x5 -> x0, matrix products: 6.36 us -> none  [the longest x3 5.66 us: body(): coeffs = jnp.dot(flat, table, preferred_element_type=jnp.float32) / root]
    ppermute x0 -> x10, waiting for transfers between devices: none -> 4.82 us  [the longest x3 2.55 us: body(): arrived.append(lax.ppermute(parts[step], 'band', pairs))]
  transfers between devices with their start and end apart: 2 -> 10, of which waited for: 0 -> 4; matrix products, arithmetic and copies ran while one was open for 74% -> 4% of each run, Pallas kernels for 0% -> 0%
where the time goes in v1:
time: 30.7 us; the launch traced here: 30.4 us
  starting transfers between devices  14.4 us (47%)
  local copies, waits for them, and re-layouts  4.82 us (16%)
  waiting for transfers between devices  4.82 us (16%)
  Pallas kernels  4.15 us (14%)
  between operations  1.38 us (4%)
  other arithmetic  0.81 us (3%)
    ppermute x7, starting transfers between devices, body(): pieces.append(lax.ppermute(traj, 'col', pairs))  12.5 us
    unnamed x17, local copies, waits for them, and re-layouts  3.01 us
    ppermute x3, waiting for transfers between devices, body(): arrived.append(lax.ppermute(parts[step], 'band', pairs))  2.55 us
    pallas_call x1, Pallas kernels, body(): pl.pallas_call(functools.partial(main_kernel, blocks, block, bands), out_...  2.32 us
    ppermute x7, waiting for transfers between devices, body(): pieces.append(lax.ppermute(traj, 'col', pairs))  2.28 us
    ppermute x3, starting transfers between devices, body(): arrived.append(lax.ppermute(parts[step], 'band', pairs))  1.93 us
    pallas_call x1, Pallas kernels, body(): pl.pallas_call(functools.partial(place_kernel, bands), out_shape=jax.Shap...  1.83 us
    reshape x1, local copies, waits for them, and re-layouts, body(): return spectra.reshape(1, 2, column_vars, bands, share)  1.64 us
  transfers between devices with their start and end apart: 10, of which 4 were waited for; matrix products, arithmetic and copies ran while one was open for 4% of the time, Pallas kernels for 0%

profile of v1, /device:TPU:0, one launch (start us, length us, event | category | flops | bytes accessed | tf_op | source)
XLA Modules:
  0.0 30.4 jit_solution(7727313354267029730)
XLA Ops:
  0.0 6.0 %collective-permute-start.6 = (bf16[40,640]{1,0:T(8,128)(2,1)}, bf16[40,640]{1,0:T(8,128)(2,1)S(1)}, u32[]{:S(2)}, u32[]{:S(2)}) collective-permute-start(bf16[40,640]{1,0:T(8,128)(2,1)} %bitcast.12), channel_id=1, source_target_pairs={{0,7},{1,6},{2,5},{3,4},{4,3},{5,2},{6,1},{7,0},{8,15},{9,14},{10,... | collective-permute-start | bytes 153608 | tf_op jit(solution)/shard_map/ppermute | solution.py:184
  6.0 0.2 collective-permute-start.5
  6.2 0.7 %collective-permute-start.4 = (bf16[40,640]{1,0:T(8,128)(2,1)}, bf16[40,640]{1,0:T(8,128)(2,1)S(1)}, u32[]{:S(2)}, u32[]{:S(2)}) collective-permute-start(bf16[40,640]{1,0:T(8,128)(2,1)} %bitcast.14), channel_id=1, source_target_pairs={{0,5},{1,4},{2,7},{3,6},{4,1},{5,0},{6,3},{7,2},{8,13},{9,12},{10,... | collective-permute-start | bytes 153608 | tf_op jit(solution)/shard_map/ppermute | solution.py:184
  7.0 2.0 %collective-permute-start.3 = (bf16[40,640]{1,0:T(8,128)(2,1)}, bf16[40,640]{1,0:T(8,128)(2,1)S(1)}, u32[]{:S(2)}, u32[]{:S(2)}) collective-permute-start(bf16[40,640]{1,0:T(8,128)(2,1)} %bitcast.15), channel_id=1, source_target_pairs={{0,4},{1,5},{2,6},{3,7},{4,0},{5,1},{6,2},{7,3},{8,12},{9,13},{10,... | collective-permute-start | bytes 153608 | tf_op jit(solution)/shard_map/ppermute | solution.py:184
  8.9 2.4 %collective-permute-start.2 = (bf16[40,640]{1,0:T(8,128)(2,1)}, bf16[40,640]{1,0:T(8,128)(2,1)S(1)}, u32[]{:S(2)}, u32[]{:S(2)}) collective-permute-start(bf16[40,640]{1,0:T(8,128)(2,1)} %bitcast.16), channel_id=1, source_target_pairs={{0,3},{1,2},{2,1},{3,0},{4,7},{5,6},{6,5},{7,4},{8,11},{9,10},{10,... | collective-permute-start | bytes 153608 | tf_op jit(solution)/shard_map/ppermute | solution.py:184
  11.3 0.7 %copy-done.6 = bf16[40,40]{1,0:T(8,128)(2,1)S(1)} copy-done((bf16[40,40]{1,0:T(8,128)(2,1)S(1)}, bf16[40,40]{1,0:T(8,128)(2,1)}, u32[]{:S(2)}) %copy-start.6) | copy-done | bytes 3224
  12.0 0.1 copy.7
  12.1 0.1 fusion.9.refs_4_
  12.2 0.6 %copy-done.7 = s32[768]{0:T(1024)S(1)} copy-done((s32[768]{0:T(1024)S(1)}, s32[768]{0:T(1024)}, u32[]{:S(2)}) %copy-start.7) | copy-done | bytes 3096
  12.9 0.8 %collective-permute-start.1 = (bf16[40,640]{1,0:T(8,128)(2,1)S(1)}, bf16[40,640]{1,0:T(8,128)(2,1)S(1)}, u32[]{:S(2)}, u32[]{:S(2)}) collective-permute-start(bf16[40,640]{1,0:T(8,128)(2,1)S(1)} %bitcast.17), channel_id=1, source_target_pairs={{0,2},{1,3},{2,0},{3,1},{4,6},{5,7},{6,4},{7,5},{8,10},{9,11},{10,... | collective-permute-start | bytes 153608 | tf_op jit(solution)/shard_map/ppermute | solution.py:184
  13.7 0.3 %collective-permute-start = (bf16[40,640]{1,0:T(8,128)(2,1)S(1)}, bf16[40,640]{1,0:T(8,128)(2,1)S(1)}, u32[]{:S(2)}, u32[]{:S(2)}) collective-permute-start(bf16[40,640]{1,0:T(8,128)(2,1)S(1)} %bitcast.18), channel_id=1, source_target_pairs={{0,1},{1,0},{2,3},{3,2},{4,5},{5,4},{6,7},{7,6},{8,9},{9,8},{10,11... | collective-permute-start | bytes 153608 | tf_op jit(solution)/shard_map/ppermute | solution.py:184
  15.5 0.1 stack.35.refs_0_
  15.6 1.5 %collective-permute-done.1.refs_8_ = bf16[40,640]{1,0:T(8,128)(2,1)S(1)} collective-permute-done((bf16[40,640]{1,0:T(8,128)(2,1)S(1)}, bf16[40,640]{1,0:T(8,128)(2,1)S(1)}, u32[]{:S(2)}, u32[]{:S(2)}) %collective-permute-start.1) | collective-permute-done | bytes 51232 | tf_op jit(solution)/shard_map/ppermute | solution.py:184
  17.1 0.8 %collective-permute-done.refs_7_ = bf16[40,640]{1,0:T(8,128)(2,1)S(1)} collective-permute-done((bf16[40,640]{1,0:T(8,128)(2,1)S(1)}, bf16[40,640]{1,0:T(8,128)(2,1)S(1)}, u32[]{:S(2)}, u32[]{:S(2)}) %collective-permute-start) | collective-permute-done | bytes 51232 | tf_op jit(solution)/shard_map/ppermute | solution.py:184
  17.8 1.0 %copy-done.1 = bf16[1,40,1,5120]{3,1,2,0:T(8,128)(2,1)S(1)} copy-done((bf16[1,40,1,5120]{3,1,2,0:T(8,128)(2,1)S(1)}, bf16[1,40,1,5120]{3,1,2,0:T(8,128)(2,1)}, u32[]{:S(2)}) %copy-start.1) | copy-done | bytes 409624
  18.8 2.3 %column_and_waves.1 = (bf16[80,192]{1,0:T(8,128)(2,1)S(1)}, bf16[80,192]{1,0:T(8,128)(2,1)S(1)}, bf16[80,192]{1,0:T(8,128)(2,1)S(1)}, bf16[80,192]{1,0:T(8,128)(2,1)S(1)}) custom-call(s32[8]{0:T(128)S(1)} %stack.35.refs_0_, s32[1]{0:T(128)S(6)} %copy.8.refs_1_, s32[1]{0:T(128)S(6)} %copy.9.refs_2_, s32[1,768]{1,0:T(1,128)S(1)} %reshape.71.refs_3_, ...), custom_call_target="tpu_custom_call" | custom-call | flops 629145600 | bytes 819200 | tf_op jit(solution)/shard_map/column_and_waves/pallas_call | solution.py:209
  21.3 1.6 %collective-permute-start.8 = (bf16[80,192]{1,0:T(8,128)(2,1)S(1)}, bf16[80,192]{1,0:T(8,128)(2,1)S(1)}, u32[]{:S(2)}, u32[]{:S(2)}) collective-permute-start(bf16[80,192]{1,0:T(8,128)(2,1)S(1)} %get-tuple-element.11), channel_id=1, source_target_pairs={{0,16},{8,24},{16,0},{24,8},{1,17},{9,25},{17,1},{25,9},{2,18},{10... | collective-permute-start | bytes 92168 | tf_op jit(solution)/shard_map/ppermute | solution.py:228
  22.8 0.3 %collective-permute-start.9 = (bf16[80,192]{1,0:T(8,128)(2,1)S(1)}, bf16[80,192]{1,0:T(8,128)(2,1)S(1)}, u32[]{:S(2)}, u32[]{:S(2)}) collective-permute-start(bf16[80,192]{1,0:T(8,128)(2,1)S(1)} %get-tuple-element.12), channel_id=1, source_target_pairs={{0,24},{8,16},{16,8},{24,0},{1,25},{9,17},{17,9},{25,1},{2,26},{10... | collective-permute-start | bytes 92168 | tf_op jit(solution)/shard_map/ppermute | solution.py:228
  23.1 0.7 %fusion.2.refs_0_ = s32[160,1]{1,0:T(8,128)} fusion(s32[]{:T(128)S(6)} %axis_index.23), kind=kLoop, calls=%fused_computation.6 | loop fusion | flops 2400 | bytes 644 | tf_op jit(solution)/shard_map/add | solution.py:232
  23.8 1.5 %collective-permute-done.8.refs_3_ = bf16[80,192]{1,0:T(8,128)(2,1)S(1)} collective-permute-done((bf16[80,192]{1,0:T(8,128)(2,1)S(1)}, bf16[80,192]{1,0:T(8,128)(2,1)S(1)}, u32[]{:S(2)}, u32[]{:S(2)}) %collective-permute-start.8) | collective-permute-done | bytes 30752 | tf_op jit(solution)/shard_map/ppermute | solution.py:228
  25.3 1.0 %collective-permute-done.9.refs_4_ = bf16[80,192]{1,0:T(8,128)(2,1)S(1)} collective-permute-done((bf16[80,192]{1,0:T(8,128)(2,1)S(1)}, bf16[80,192]{1,0:T(8,128)(2,1)S(1)}, u32[]{:S(2)}, u32[]{:S(2)}) %collective-permute-start.9) | collective-permute-done | bytes 30752 | tf_op jit(solution)/shard_map/ppermute | solution.py:228
  26.3 0.6 %copy-done.5 = bf16[80,192]{1,0:T(8,128)(2,1)} copy-done((bf16[80,192]{1,0:T(8,128)(2,1)}, bf16[80,192]{1,0:T(8,128)(2,1)S(1)}, u32[]{:S(2)}) %copy-start.5) | copy-done | bytes 30744
  26.9 1.8 %row_slots.1 = bf16[2,160,192]{2,1,0:T(8,128)(2,1)} custom-call(s32[160,1]{1,0:T(8,128)} %fusion.2.refs_0_, bf16[80,192]{1,0:T(8,128)(2,1)} %copy-done, bf16[80,192]{1,0:T(8,128)(2,1)} %copy-done.3, bf16[80,192]{1,0:T(8,128)(2,1)} %copy-done.4, bf16[80,192]{1,0:T(8,128)(2,1)} %copy-done.5), custom_call_target="tpu_custom_call" | custom-call | tf_op jit(solution)/shard_map/row_slots/pallas_call | solution.py:233
  28.8 1.6 %reshape.74 = bf16[1,2,40,4,192]{4,3,2,1,0:T(4,128)(2,1)} reshape(bf16[2,160,192]{2,1,0:T(8,128)(2,1)} %row_slots.1) | data formatting | bytes 245760 | tf_op jit(solution)/shard_map/reshape | solution.py:240
  (23 shorter events, 0.3 us)
Async XLA Ops:
  0.0 12.9 %collective-permute-start.6 = (bf16[40,640]{1,0:T(8,128)(2,1)}, bf16[40,640]{1,0:T(8,128)(2,1)S(1)}, u32[]{:S(2)}, u32[]{:S(2)}) collective-permute-start(bf16[40,640]{1,0:T(8,128)(2,1)} %bitcast.12), channel_id=1, source_target_pairs={{0,7},{1,6},{2,5},{3,4},{4,3},{5,2},{6,1},{7,0},{8,15},{9,14},{10,... | collective-permute-start | bytes 153608 | tf_op jit(solution)/shard_map/ppermute | solution.py:184
  6.0 7.7 %collective-permute-start.5 = (bf16[40,640]{1,0:T(8,128)(2,1)}, bf16[40,640]{1,0:T(8,128)(2,1)S(1)}, u32[]{:S(2)}, u32[]{:S(2)}) collective-permute-start(bf16[40,640]{1,0:T(8,128)(2,1)} %bitcast.13), channel_id=1, source_target_pairs={{0,6},{1,7},{2,4},{3,5},{4,2},{5,3},{6,0},{7,1},{8,14},{9,15},{10,... | collective-permute-start | bytes 153608 | tf_op jit(solution)/shard_map/ppermute | solution.py:184
  6.2 9.3 %collective-permute-start.4 = (bf16[40,640]{1,0:T(8,128)(2,1)}, bf16[40,640]{1,0:T(8,128)(2,1)S(1)}, u32[]{:S(2)}, u32[]{:S(2)}) collective-permute-start(bf16[40,640]{1,0:T(8,128)(2,1)} %bitcast.14), channel_id=1, source_target_pairs={{0,5},{1,4},{2,7},{3,6},{4,1},{5,0},{6,3},{7,2},{8,13},{9,12},{10,... | collective-permute-start | bytes 153608 | tf_op jit(solution)/shard_map/ppermute | solution.py:184
  7.0 8.6 %collective-permute-start.3 = (bf16[40,640]{1,0:T(8,128)(2,1)}, bf16[40,640]{1,0:T(8,128)(2,1)S(1)}, u32[]{:S(2)}, u32[]{:S(2)}) collective-permute-start(bf16[40,640]{1,0:T(8,128)(2,1)} %bitcast.15), channel_id=1, source_target_pairs={{0,4},{1,5},{2,6},{3,7},{4,0},{5,1},{6,2},{7,3},{8,12},{9,13},{10,... | collective-permute-start | bytes 153608 | tf_op jit(solution)/shard_map/ppermute | solution.py:184
  8.9 6.6 %collective-permute-start.2 = (bf16[40,640]{1,0:T(8,128)(2,1)}, bf16[40,640]{1,0:T(8,128)(2,1)S(1)}, u32[]{:S(2)}, u32[]{:S(2)}) collective-permute-start(bf16[40,640]{1,0:T(8,128)(2,1)} %bitcast.16), channel_id=1, source_target_pairs={{0,3},{1,2},{2,1},{3,0},{4,7},{5,6},{6,5},{7,4},{8,11},{9,10},{10,... | collective-permute-start | bytes 153608 | tf_op jit(solution)/shard_map/ppermute | solution.py:184
  11.3 0.7 %copy-start.6 = (bf16[40,40]{1,0:T(8,128)(2,1)S(1)}, bf16[40,40]{1,0:T(8,128)(2,1)}, u32[]{:S(2)}) copy-start(bf16[40,40]{1,0:T(8,128)(2,1)} %param.8) | copy-start | bytes 9604
  12.0 0.9 %copy-start.2 = (bf16[40,1,640]{2,0,1:T(8,128)(2,1)S(1)}, bf16[40,1,640]{2,0,1:T(8,128)(2,1)}, u32[]{:S(2)}) copy-start(bf16[40,1,640]{2,0,1:T(8,128)(2,1)} %param.7) | copy-start | bytes 153604
  12.1 0.7 %copy-start.7 = (s32[768]{0:T(1024)S(1)}, s32[768]{0:T(1024)}, u32[]{:S(2)}) copy-start(s32[768]{0:T(1024)} %param.11) | copy-start | bytes 9220
  12.9 4.2 %collective-permute-start.1 = (bf16[40,640]{1,0:T(8,128)(2,1)S(1)}, bf16[40,640]{1,0:T(8,128)(2,1)S(1)}, u32[]{:S(2)}, u32[]{:S(2)}) collective-permute-start(bf16[40,640]{1,0:T(8,128)(2,1)S(1)} %bitcast.17), channel_id=1, source_target_pairs={{0,2},{1,3},{2,0},{3,1},{4,6},{5,7},{6,4},{7,5},{8,10},{9,11},{10,... | collective-permute-start | bytes 153608 | tf_op jit(solution)/shard_map/ppermute | solution.py:184
  13.7 4.1 %collective-permute-start = (bf16[40,640]{1,0:T(8,128)(2,1)S(1)}, bf16[40,640]{1,0:T(8,128)(2,1)S(1)}, u32[]{:S(2)}, u32[]{:S(2)}) collective-permute-start(bf16[40,640]{1,0:T(8,128)(2,1)S(1)} %bitcast.18), channel_id=1, source_target_pairs={{0,1},{1,0},{2,3},{3,2},{4,5},{5,4},{6,7},{7,6},{8,9},{9,8},{10,11... | collective-permute-start | bytes 153608 | tf_op jit(solution)/shard_map/ppermute | solution.py:184
  17.8 1.0 %copy-start.1 = (bf16[1,40,1,5120]{3,1,2,0:T(8,128)(2,1)S(1)}, bf16[1,40,1,5120]{3,1,2,0:T(8,128)(2,1)}, u32[]{:S(2)}) copy-start(bf16[1,40,1,5120]{3,1,2,0:T(8,128)(2,1)} %param.6) | copy-start | bytes 1228804
  21.2 2.6 %copy-start = (bf16[80,192]{1,0:T(8,128)(2,1)}, bf16[80,192]{1,0:T(8,128)(2,1)S(1)}, u32[]{:S(2)}) copy-start(bf16[80,192]{1,0:T(8,128)(2,1)S(1)} %get-tuple-element.9.refs_1_) | copy-start | bytes 92164
  21.2 2.6 %collective-permute-start.7 = (bf16[80,192]{1,0:T(8,128)(2,1)S(1)}, bf16[80,192]{1,0:T(8,128)(2,1)S(1)}, u32[]{:S(2)}, u32[]{:S(2)}) collective-permute-start(bf16[80,192]{1,0:T(8,128)(2,1)S(1)} %get-tuple-element.10), channel_id=1, source_target_pairs={{0,8},{8,0},{16,24},{24,16},{1,9},{9,1},{17,25},{25,17},{2,10},{10... | collective-permute-start | bytes 92168 | tf_op jit(solution)/shard_map/ppermute | solution.py:228
  21.3 4.1 %collective-permute-start.8 = (bf16[80,192]{1,0:T(8,128)(2,1)S(1)}, bf16[80,192]{1,0:T(8,128)(2,1)S(1)}, u32[]{:S(2)}, u32[]{:S(2)}) collective-permute-start(bf16[80,192]{1,0:T(8,128)(2,1)S(1)} %get-tuple-element.11), channel_id=1, source_target_pairs={{0,16},{8,24},{16,0},{24,8},{1,17},{9,25},{17,1},{25,9},{2,18},{10... | collective-permute-start | bytes 92168 | tf_op jit(solution)/shard_map/ppermute | solution.py:228
  22.8 3.5 %collective-permute-start.9 = (bf16[80,192]{1,0:T(8,128)(2,1)S(1)}, bf16[80,192]{1,0:T(8,128)(2,1)S(1)}, u32[]{:S(2)}, u32[]{:S(2)}) collective-permute-start(bf16[80,192]{1,0:T(8,128)(2,1)S(1)} %get-tuple-element.12), channel_id=1, source_target_pairs={{0,24},{8,16},{16,8},{24,0},{1,25},{9,17},{17,9},{25,1},{2,26},{10... | collective-permute-start | bytes 92168 | tf_op jit(solution)/shard_map/ppermute | solution.py:228
  23.8 2.6 %copy-start.3 = (bf16[80,192]{1,0:T(8,128)(2,1)}, bf16[80,192]{1,0:T(8,128)(2,1)S(1)}, u32[]{:S(2)}) copy-start(bf16[80,192]{1,0:T(8,128)(2,1)S(1)} %collective-permute-done.7.refs_2_) | copy-start | bytes 92164
  25.3 1.0 %copy-start.4 = (bf16[80,192]{1,0:T(8,128)(2,1)}, bf16[80,192]{1,0:T(8,128)(2,1)S(1)}, u32[]{:S(2)}) copy-start(bf16[80,192]{1,0:T(8,128)(2,1)S(1)} %collective-permute-done.8.refs_3_) | copy-start | bytes 92164
  26.3 0.6 %copy-start.5 = (bf16[80,192]{1,0:T(8,128)(2,1)}, bf16[80,192]{1,0:T(8,128)(2,1)S(1)}, u32[]{:S(2)}) copy-start(bf16[80,192]{1,0:T(8,128)(2,1)S(1)} %collective-permute-done.9.refs_4_) | copy-start | bytes 92164

commit v2 on v1

v2 whole, which is shorter than its diff:
```python
import functools
import math

import jax
import jax.numpy as jnp
from jax import lax
from jax.experimental import pallas as pl
from jax.experimental.pallas import tpu as pltpu
from jax.sharding import PartitionSpec as P

LEVELS = 8
LATITUDES = 2560
LANES = 128
SUB = 32


def partner(place, step, count):
    if count & (count - 1) == 0:
        return place ^ step
    return (place + step) % count


def source(place, step, count):
    if count & (count - 1) == 0:
        return place ^ step
    return (place - step) % count


def turn(places, waves, points):
    product = places * waves
    whole = jnp.floor(product * (1.0 / points) + 0.5)
    quarter = (product - whole * points) * 4.0 / points
    nearest = jnp.floor(quarter + 0.5)
    angle = (quarter - nearest) * (0.5 * math.pi)
    square = angle * angle
    sine = angle + angle * square * (
        -1.6666654611e-1 + square * (8.3321608736e-3 - square * 1.9515295891e-4)
    )
    cosine = (
        1.0
        - 0.5 * square
        + square
        * square
        * (4.166664568298827e-2 + square * (-1.388731625493765e-3 + square * 2.443315711809948e-5))
    )
    odd = jnp.abs(nearest) == 1.0
    first = jnp.where(odd, sine, cosine)
    second = jnp.where(odd, cosine, sine)
    first = jnp.where((nearest == 1.0) | (jnp.abs(nearest) >= 2.0), -first, first)
    second = jnp.where((nearest == -1.0) | (jnp.abs(nearest) >= 2.0), -second, second)
    return first, -second


def tables_kernel(
    blocks, block, index_of, lat_ref, waves_hbm, coupling_hbm, tend_hbm, traj_hbm, *refs
):
    table_ref, phase_ref, mix_ref, kept_ref, own_ref, coriolis_ref = refs[:6]
    waves_ref, coupling_ref, tend_ref, sems = refs[6:]
    copies = [
        pltpu.make_async_copy(source_ref, target_ref, sems.at[i])
        for i, (source_ref, target_ref) in enumerate(
            [
                (waves_hbm, waves_ref),
                (coupling_hbm, coupling_ref),
                (tend_hbm, tend_ref),
                (traj_hbm, own_ref),
            ]
        )
    ]
    for copy in copies:
        copy.start()
    index = lat_ref[0]
    count = jnp.minimum(20 + 4 * jnp.minimum(index, LATITUDES - 1 - index), tend_ref.shape[1])
    copies[0].wait()
    waves_total = waves_ref.shape[0]
    points = jnp.full((1, 1), count, jnp.int32).astype(jnp.float32)
    waves = waves_ref[...].reshape(1, waves_total).astype(jnp.float32)

    coarse_rows = block // SUB
    coarse_pad = -(-coarse_rows // 8) * 8
    fine = lax.broadcasted_iota(jnp.int32, (SUB, 1), 0).astype(jnp.float32)
    coarse = lax.broadcasted_iota(jnp.int32, (coarse_pad, 1), 0).astype(jnp.float32) * SUB
    fine_cos, fine_sin = turn(fine, waves, points)
    coarse_cos, coarse_sin = turn(coarse, waves, points)
    for row in range(coarse_rows):
        here_cos = coarse_cos[row : row + 1]
        here_sin = coarse_sin[row : row + 1]
        rows = pl.ds(row * SUB, SUB)
        table_ref[rows, :waves_total] = (here_cos * fine_cos - here_sin * fine_sin).astype(
            jnp.bfloat16
        )
        table_ref[rows, waves_total:] = (here_cos * fine_sin + here_sin * fine_cos).astype(
            jnp.bfloat16
        )

    slot = lax.broadcasted_iota(jnp.int32, (blocks, 1), 0)
    first = jnp.zeros((blocks, 1), jnp.int32)
    for i, of_row in enumerate(index_of()):
        first = jnp.where(slot == i, of_row * block, first)
    phase_cos, phase_sin = turn(first.astype(jnp.float32), waves, points)
    scale = jnp.where(2.0 * waves < points, 1.0 / jnp.sqrt(points), 0.0)
    phase_ref[0] = phase_cos * scale
    phase_ref[1] = phase_sin * scale

    latitude = jnp.full((1, LANES), index, jnp.int32).astype(jnp.float32)
    ratio = (2.0 * latitude + 1.0) / LATITUDES
    coriolis_ref[...] = turn(0.25 * (ratio - 1.0), jnp.ones((1, LANES), jnp.float32), 1.0)[1]

    copies[1].wait()
    column_vars = coupling_ref.shape[0]
    coupling = coupling_ref[...]
    row = lax.broadcasted_iota(jnp.int32, (column_vars, 3 * column_vars), 0)
    col = lax.broadcasted_iota(jnp.int32, (column_vars, 3 * column_vars), 1)
    near = (col == row).astype(jnp.bfloat16)
    far = ((col == row + column_vars) | (col == row + 2 * column_vars)).astype(jnp.bfloat16)
    mix_ref[...] = jnp.concatenate(
        [
            jnp.dot(coupling, near, preferred_element_type=jnp.float32),
            lax.dot_general(
                coupling, far, (((0,), (0,)), ((), ())), preferred_element_type=jnp.float32
            ),
        ],
        axis=0,
    ).astype(jnp.bfloat16)

    copies[2].wait()
    for i in range(blocks):
        cols = slice(i * block, (i + 1) * block)
        place = i * block + lax.broadcasted_iota(jnp.int32, (1, block), 1)
        kept_ref[:, cols] = jnp.where(
            place < count, tend_ref[:, cols].astype(jnp.float32), 0.0
        ).astype(jnp.bfloat16)
    copies[3].wait()


def main_kernel(blocks, block, parts, index_of, *refs):
    coriolis_ref, mix_ref, table_ref, phase_ref, tend_ref = refs[:5]
    traj_refs = refs[5 : 5 + blocks]
    out_refs = refs[5 + blocks : 5 + blocks + parts]
    grid_ref = refs[5 + blocks + parts]
    column_vars = tend_ref.shape[0]
    waves_total = phase_ref.shape[2]
    share = waves_total // parts

    coriolis = coriolis_ref[:, :1]
    mix = mix_ref[...]
    for i, index in enumerate(index_of()):
        start = pl.multiple_of(index * block, LANES)
        traj = traj_refs[i][...].astype(jnp.float32)
        tend = tend_ref[:, pl.ds(start, block)].astype(jnp.float32)
        stacked = jnp.concatenate([traj, tend, tend * traj], axis=0).astype(jnp.bfloat16)
        mixed = jnp.dot(mix, stacked, preferred_element_type=jnp.float32)
        total = mixed[column_vars:] + tend * mixed[:column_vars]
        grid_ref[pl.ds(i * column_vars, column_vars), :] = jnp.concatenate(
            [
                total[:LEVELS] - coriolis * tend[LEVELS : 2 * LEVELS],
                total[LEVELS : 2 * LEVELS] + coriolis * tend[:LEVELS],
                total[2 * LEVELS :],
            ],
            axis=0,
        )

    flat = grid_ref[...].astype(jnp.bfloat16)
    reals = []
    imags = []
    width = math.gcd(waves_total, 256)
    for first_wave in range(0, waves_total, width):
        cols = slice(first_wave, first_wave + width)
        near_cos = jnp.dot(flat, table_ref[:, cols], preferred_element_type=jnp.float32)
        near_sin = jnp.dot(
            flat,
            table_ref[:, waves_total + first_wave : waves_total + first_wave + width],
            preferred_element_type=jnp.float32,
        )
        real = jnp.zeros((column_vars, width), jnp.float32)
        imag = jnp.zeros((column_vars, width), jnp.float32)
        for i in range(blocks):
            rows = slice(i * column_vars, (i + 1) * column_vars)
            far_cos = phase_ref[0, i : i + 1, cols]
            far_sin = phase_ref[1, i : i + 1, cols]
            real = real + (far_cos * near_cos[rows] - far_sin * near_sin[rows])
            imag = imag + (far_cos * near_sin[rows] + far_sin * near_cos[rows])
        reals.append(real)
        imags.append(imag)
    both = jnp.concatenate(
        [jnp.concatenate(reals, axis=1), jnp.concatenate(imags, axis=1)], axis=0
    )
    shares = [both[:, d * share : (d + 1) * share] for d in range(parts)]
    my_band = lax.axis_index("band")
    for k in range(parts):
        goal = partner(my_band, k, parts)
        chosen = shares[0]
        for d in range(1, parts):
            chosen = jnp.where(goal == d, shares[d], chosen)
        out_refs[k][...] = chosen.astype(jnp.bfloat16)


def place_kernel(parts, *refs):
    in_refs = refs[:parts]
    out_ref = refs[parts]
    column_vars = out_ref.shape[2]
    share = out_ref.shape[4]
    total = parts * column_vars
    row = lax.broadcasted_iota(jnp.int32, (total, 1), 0)
    variable = jnp.floor((row.astype(jnp.float32) + 0.5) * (1.0 / parts)).astype(jnp.int32)
    slot = row - variable * parts
    if parts & (parts - 1) == 0:
        step = slot ^ lax.axis_index("band")
    else:
        step = lax.axis_index("band") - slot
        step = jnp.where(step < 0, step + parts, step)
    target = step * column_vars + variable
    choose = (target == lax.broadcasted_iota(jnp.int32, (total, total), 1)).astype(jnp.bfloat16)
    wide = [ref[...].astype(jnp.float32) for ref in in_refs]
    for half in range(2):
        rows = slice(half * column_vars, (half + 1) * column_vars)
        stacked = jnp.concatenate([w[rows] for w in wide], axis=0).astype(jnp.bfloat16)
        placed = jnp.dot(choose, stacked, preferred_element_type=jnp.float32)
        out_ref[0, half] = placed.reshape(column_vars, parts, share).astype(jnp.bfloat16)


VMEM_SPEC = pl.BlockSpec(memory_space=pltpu.VMEM)
SMEM_SPEC = pl.BlockSpec(memory_space=pltpu.SMEM)
HBM_SPEC = pl.BlockSpec(memory_space=pltpu.HBM)


def body(cols, bands, adjoint_tend, trajectory, coupling, row_lat, row_points, wave_order):
    column_vars = adjoint_tend.shape[1]
    width = adjoint_tend.shape[3]
    own = trajectory.shape[2]
    waves_total = wave_order.shape[0]
    share = waves_total // bands
    tend = adjoint_tend.reshape(column_vars, width)
    traj = trajectory.reshape(column_vars, own)

    inner = 2 if cols % 2 == 0 else 1
    outer = cols // inner
    direct = own % LANES == 0
    blocks = cols if direct else 8
    block = width // blocks

    def index_of():
        if not direct:
            return list(range(blocks))
        my_col = lax.axis_index("col")
        far, near = my_col // inner, my_col % inner
        indices = [source(far, step, outer) * inner + near for step in range(outer)]
        return indices + [index ^ 1 for index in indices] if inner == 2 else indices

    operands = [wave_order, coupling, tend, traj]
    table, phase, mix, kept, own_piece, coriolis = pl.pallas_call(
        functools.partial(tables_kernel, blocks, block, index_of),
        out_shape=[
            jax.ShapeDtypeStruct((block, 2 * waves_total), jnp.bfloat16),
            jax.ShapeDtypeStruct((2, blocks, waves_total), jnp.float32),
            jax.ShapeDtypeStruct((2 * column_vars, 3 * column_vars), jnp.bfloat16),
            jax.ShapeDtypeStruct((column_vars, width), jnp.bfloat16),
            jax.ShapeDtypeStruct((column_vars, own), jnp.bfloat16),
            jax.ShapeDtypeStruct((1, LANES), jnp.float32),
        ],
        in_specs=[SMEM_SPEC] + [HBM_SPEC] * len(operands),
        out_specs=[VMEM_SPEC] * 6,
        scratch_shapes=[
            pltpu.VMEM((waves_total,), jnp.int32),
            pltpu.VMEM((column_vars, column_vars), jnp.bfloat16),
            pltpu.VMEM((column_vars, width), jnp.bfloat16),
            pltpu.SemaphoreType.DMA((len(operands),)),
        ],
        compiler_params=pltpu.CompilerParams(vmem_limit_bytes=16 * 1024 * 1024),
        cost_estimate=pl.CostEstimate(
            flops=1024 * column_vars * width, bytes_accessed=4 * column_vars * width, transcendentals=0
        ),
        name="tables",
    )(row_lat, *[pltpu.with_memory_space_constraint(x, pltpu.HBM) for x in operands])

    if direct:
        places = [(i // inner, i % inner) for i in range(cols)]
        arrived = []
        for step in range(1, outer):
            pairs = [(f * inner + n, partner(f, step, outer) * inner + n) for f, n in places]
            arrived.append(lax.ppermute(traj, "col", pairs))
        if inner == 2:
            pairs = [(i, i ^ 1) for i in range(cols)]
            passed = [lax.optimization_barrier((piece, coriolis))[0] for piece in arrived]
            arrived += [lax.ppermute(piece, "col", pairs) for piece in [traj] + passed]
    else:
        whole = lax.all_gather(traj, "col", axis=1, tiled=True)
        arrived = [whole[:, i * block : (i + 1) * block] for i in range(8)]

    pieces = [own_piece] + arrived if direct else arrived
    parts = pl.pallas_call(
        functools.partial(main_kernel, blocks, block, bands, index_of),
        out_shape=[jax.ShapeDtypeStruct((2 * column_vars, share), jnp.bfloat16)] * bands,
        in_specs=[VMEM_SPEC] * (5 + blocks),
        out_specs=[VMEM_SPEC] * bands,
        scratch_shapes=[pltpu.VMEM((blocks * column_vars, block), jnp.float32)],
        compiler_params=pltpu.CompilerParams(vmem_limit_bytes=24 * 1024 * 1024),
        cost_estimate=pl.CostEstimate(
            flops=4 * column_vars * width * waves_total,
            bytes_accessed=4 * column_vars * width,
            transcendentals=0,
        ),
        name="column_and_waves",
    )(coriolis, mix, table, phase, kept, *pieces)

    ready = [parts[0]]
    for step in range(1, bands):
        pairs = [(i, partner(i, step, bands)) for i in range(bands)]
        ready.append(lax.ppermute(parts[step], "band", pairs))
    return pl.pallas_call(
        functools.partial(place_kernel, bands),
        out_shape=jax.ShapeDtypeStruct((1, 2, column_vars, bands, share), jnp.bfloat16),
        in_specs=[VMEM_SPEC] * bands,
        out_specs=VMEM_SPEC,
        compiler_params=pltpu.CompilerParams(vmem_limit_bytes=16 * 1024 * 1024),
        name="row_slots",
    )(*ready)


def solution(mesh):
    return jax.shard_map(
        functools.partial(body, mesh.shape["col"], mesh.shape["band"]),
        mesh=mesh,
        in_specs=(
            P("col", None, "band", None),
            P(None, "band", "col"),
            P(),
            P("band"),
            P("band"),
            P(),
        ),
        out_specs=P("col", None, None, None, "band"),
        check_vma=False,
    )
```

time: 30.7 us -> 24.1 us (0.79)
  local copies, waits for them, and re-layouts: 4.82 us -> 0 us
  starting transfers between devices: 14.4 us -> 12.8 us
  waiting for transfers between devices: 4.82 us -> 6.34 us
  other arithmetic: 0.81 us -> 0 us
  between operations: 1.38 us -> 0.69 us
    unnamed x17 -> x0, local copies, waits for them, and re-layouts: 3.01 us -> none
    reshape x2 -> x0, local copies, waits for them, and re-layouts: 1.64 us -> none  [the longest x1 1.64 us: body(): return spectra.reshape(1, 2, column_vars, bands, share)]
    ppermute x10, starting transfers between devices: 14.4 us -> 12.8 us  [the longest x3 5.62 us: body(): arrived.append(lax.ppermute(traj, 'col', pairs))]
    ppermute x10, waiting for transfers between devices: 4.82 us -> 6.34 us  [the longest x3 3.22 us: body(): ready.append(lax.ppermute(parts[step], 'band', pairs))]
    pallas_call x1, Pallas kernels: 1.83 us -> 0.87 us  [body(): pl.pallas_call(functools.partial(place_kernel, bands), out_shape=jax.Shap...]
    pallas_call x1 -> x2, Pallas kernels: 2.32 us -> 3.17 us  [the longest x1 1.76 us: body(): pl.pallas_call(functools.partial(tables_kernel, blocks, block, index_of),...]
    add x1 -> x0, other arithmetic: 0.66 us -> none  [body(): target = (step_of * column_vars + variable).reshape(-1, 1)]
  transfers between devices with their start and end apart: 10 -> 10, of which waited for: 4 -> 6; matrix products, arithmetic and copies ran while one was open for 4% -> 0% of each run, Pallas kernels for 0% -> 7%
where the time goes in v2:
time: 24.1 us; the launch traced here: 23.9 us
  starting transfers between devices  12.8 us (53%)
  waiting for transfers between devices  6.34 us (26%)
  Pallas kernels  4.04 us (17%)
  between operations  0.69 us (3%)
    ppermute x3, starting transfers between devices, body(): arrived.append(lax.ppermute(traj, 'col', pairs))  5.62 us
    ppermute x4, starting transfers between devices, body(): arrived += [lax.ppermute(piece, 'col', pairs) for piece in [traj] + passed]  5.29 us
    ppermute x3, waiting for transfers between devices, body(): ready.append(lax.ppermute(parts[step], 'band', pairs))  3.22 us
    ppermute x4, waiting for transfers between devices, body(): arrived += [lax.ppermute(piece, 'col', pairs) for piece in [traj] + passed]  2.63 us
    ppermute x3, starting transfers between devices, body(): ready.append(lax.ppermute(parts[step], 'band', pairs))  1.93 us
    pallas_call x1, Pallas kernels, body(): pl.pallas_call(functools.partial(tables_kernel, blocks, block, index_of),...  1.76 us
    pallas_call x1, Pallas kernels, body(): pl.pallas_call(functools.partial(main_kernel, blocks, block, bands, index...  1.4 us
    pallas_call x1, Pallas kernels, body(): pl.pallas_call(functools.partial(place_kernel, bands), out_shape=jax.Shap...  0.87 us
  transfers between devices with their start and end apart: 10, of which 6 were waited for; matrix products, arithmetic and copies ran while one was open for 0% of the time, Pallas kernels for 7%

profile of v2, /device:TPU:0, one launch (start us, length us, event | category | flops | bytes accessed | tf_op | source)
XLA Modules:
  0.0 23.9 jit_solution(13084467045847118171)
XLA Ops:
  0.0 5.0 %collective-permute-start.2 = (bf16[40,640]{1,0:T(8,128)(2,1)}, bf16[40,640]{1,0:T(8,128)(2,1)S(1)}, u32[]{:S(2)}, u32[]{:S(2)}) collective-permute-start(bf16[40,640]{1,0:T(8,128)(2,1)} %bitcast.3), channel_id=1, source_target_pairs={{0,6},{1,7},{2,4},{3,5},{4,2},{5,3},{6,0},{7,1},{8,14},{9,15},{10,... | collective-permute-start | bytes 153608 | tf_op jit(solution)/shard_map/ppermute | solution.py:281
  5.0 0.0 collective-permute-start.1
  5.1 0.6 %collective-permute-start = (bf16[40,640]{1,0:T(8,128)(2,1)}, bf16[40,640]{1,0:T(8,128)(2,1)S(1)}, u32[]{:S(2)}, u32[]{:S(2)}) collective-permute-start(bf16[40,640]{1,0:T(8,128)(2,1)} %bitcast.5), channel_id=1, source_target_pairs={{0,2},{1,3},{2,0},{3,1},{4,6},{5,7},{6,4},{7,5},{8,10},{9,11},{10,... | collective-permute-start | bytes 153608 | tf_op jit(solution)/shard_map/ppermute | solution.py:281
  5.6 1.7 %collective-permute-start.3 = (bf16[40,640]{1,0:T(8,128)(2,1)}, bf16[40,640]{1,0:T(8,128)(2,1)S(1)}, u32[]{:S(2)}, u32[]{:S(2)}) collective-permute-start(bf16[40,640]{1,0:T(8,128)(2,1)} %bitcast.6), channel_id=1, source_target_pairs={{0,1},{1,0},{2,3},{3,2},{4,5},{5,4},{6,7},{7,6},{8,9},{9,8},{10,11... | collective-permute-start | bytes 153608 | tf_op jit(solution)/shard_map/ppermute | solution.py:285
  8.0 1.8 %tables.1 = (bf16[640,1536]{1,0:T(8,128)(2,1)S(1)}, f32[2,8,768]{2,1,0:T(8,128)S(1)}, bf16[80,120]{1,0:T(8,128)(2,1)S(1)}, bf16[40,5120]{1,0:T(8,128)(2,1)S(1)},...) custom-call(s32[1]{0:T(128)S(6)} %copy.6.lat_ref, s32[768]{0:T(1024)} %waves_hbm.1, bf16[40,40]{1,0:T(8,128)(2,1)} %coupling_hbm.1, ...), custom_call_target="tpu_custom_call" | custom-call | flops 209715200 | bytes 819200 | tf_op jit(solution)/shard_map/tables/pallas_call | solution.py:251
  9.8 0.0 collective-permute-done.2.refs_8_
  9.8 0.5 %collective-permute-done.1.refs_7_ = bf16[40,640]{1,0:T(8,128)(2,1)S(1)} collective-permute-done((bf16[40,640]{1,0:T(8,128)(2,1)}, bf16[40,640]{1,0:T(8,128)(2,1)S(1)}, u32[]{:S(2)}, u32[]{:S(2)}) %collective-permute-start.1) | collective-permute-done | bytes 51232 | tf_op jit(solution)/shard_map/ppermute | solution.py:281
  10.3 0.0 collective-permute-done.refs_6_
  10.3 1.5 %collective-permute-start.4 = (bf16[40,640]{1,0:T(8,128)(2,1)S(1)}, bf16[40,640]{1,0:T(8,128)(2,1)S(1)}, u32[]{:S(2)}, u32[]{:S(2)}) collective-permute-start(bf16[40,640]{1,0:T(8,128)(2,1)S(1)} %collective-permute-done.refs_6_), channel_id=1, source_target_pairs={{0,1},{1,0},{2,3},{3,2},{4,5},{5,4},{6,7},{7,6},{8,9},{9,8},{10,11... | collective-permute-start | bytes 153608 | tf_op jit(solution)/shard_map/ppermute | solution.py:285
  11.8 0.5 %collective-permute-start.5 = (bf16[40,640]{1,0:T(8,128)(2,1)S(1)}, bf16[40,640]{1,0:T(8,128)(2,1)S(1)}, u32[]{:S(2)}, u32[]{:S(2)}) collective-permute-start(bf16[40,640]{1,0:T(8,128)(2,1)S(1)} %collective-permute-done.1.refs_7_), channel_id=1, source_target_pairs={{0,1},{1,0},{2,3},{3,2},{4,5},{5,4},{6,7},{7,6},{8,9},{9,8},{10,11... | collective-permute-start | bytes 153608 | tf_op jit(solution)/shard_map/ppermute | solution.py:285
  12.3 1.5 %collective-permute-start.6 = (bf16[40,640]{1,0:T(8,128)(2,1)S(1)}, bf16[40,640]{1,0:T(8,128)(2,1)S(1)}, u32[]{:S(2)}, u32[]{:S(2)}) collective-permute-start(bf16[40,640]{1,0:T(8,128)(2,1)S(1)} %collective-permute-done.2.refs_8_), channel_id=1, source_target_pairs={{0,1},{1,0},{2,3},{3,2},{4,5},{5,4},{6,7},{7,6},{8,9},{9,8},{10,11... | collective-permute-start | bytes 153608 | tf_op jit(solution)/shard_map/ppermute | solution.py:285
  13.8 0.0 collective-permute-done.3.refs_9_
  13.8 0.9 %collective-permute-done.4.refs_10_ = bf16[40,640]{1,0:T(8,128)(2,1)S(1)} collective-permute-done((bf16[40,640]{1,0:T(8,128)(2,1)S(1)}, bf16[40,640]{1,0:T(8,128)(2,1)S(1)}, u32[]{:S(2)}, u32[]{:S(2)}) %collective-permute-start.4) | collective-permute-done | bytes 51232 | tf_op jit(solution)/shard_map/ppermute | solution.py:285
  14.7 1.2 %collective-permute-done.5.refs_11_ = bf16[40,640]{1,0:T(8,128)(2,1)S(1)} collective-permute-done((bf16[40,640]{1,0:T(8,128)(2,1)S(1)}, bf16[40,640]{1,0:T(8,128)(2,1)S(1)}, u32[]{:S(2)}, u32[]{:S(2)}) %collective-permute-start.5) | collective-permute-done | bytes 51232 | tf_op jit(solution)/shard_map/ppermute | solution.py:285
  15.9 0.5 %collective-permute-done.6.refs_12_ = bf16[40,640]{1,0:T(8,128)(2,1)S(1)} collective-permute-done((bf16[40,640]{1,0:T(8,128)(2,1)S(1)}, bf16[40,640]{1,0:T(8,128)(2,1)S(1)}, u32[]{:S(2)}, u32[]{:S(2)}) %collective-permute-start.6) | collective-permute-done | bytes 51232 | tf_op jit(solution)/shard_map/ppermute | solution.py:285
  16.5 1.4 %column_and_waves.1 = (bf16[80,192]{1,0:T(8,128)(2,1)S(1)}, bf16[80,192]{1,0:T(8,128)(2,1)S(1)}, bf16[80,192]{1,0:T(8,128)(2,1)S(1)}, bf16[80,192]{1,0:T(8,128)(2,1)S(1)}) custom-call(f32[1,128]{1,0:T(1,128)S(1)} %get-tuple-element.18.refs_0_, bf16[80,120]{1,0:T(8,128)(2,1)S(1)} %get-tuple-element.19.refs_1_, ...), custom_call_target="tpu_custom_call" | custom-call | flops 629145600 | bytes 819200 | tf_op jit(solution)/shard_map/column_and_waves/pallas_call | solution.py:291
  17.9 0.1 collective-permute-start.7
  17.9 1.6 %collective-permute-start.8 = (bf16[80,192]{1,0:T(8,128)(2,1)S(1)}, bf16[80,192]{1,0:T(8,128)(2,1)S(1)}, u32[]{:S(2)}, u32[]{:S(2)}) collective-permute-start(bf16[80,192]{1,0:T(8,128)(2,1)S(1)} %get-tuple-element.29), channel_id=1, source_target_pairs={{0,16},{8,24},{16,0},{24,8},{1,17},{9,25},{17,1},{25,9},{2,18},{10... | collective-permute-start | bytes 92168 | tf_op jit(solution)/shard_map/ppermute | solution.py:309
  19.5 0.3 %collective-permute-start.9 = (bf16[80,192]{1,0:T(8,128)(2,1)S(1)}, bf16[80,192]{1,0:T(8,128)(2,1)S(1)}, u32[]{:S(2)}, u32[]{:S(2)}) collective-permute-start(bf16[80,192]{1,0:T(8,128)(2,1)S(1)} %get-tuple-element.30), channel_id=1, source_target_pairs={{0,24},{8,16},{16,8},{24,0},{1,25},{9,17},{17,9},{25,1},{2,26},{10... | collective-permute-start | bytes 92168 | tf_op jit(solution)/shard_map/ppermute | solution.py:309
  19.8 0.0 collective-permute-done.7.refs_1_
  19.8 2.2 %collective-permute-done.8.refs_2_ = bf16[80,192]{1,0:T(8,128)(2,1)S(1)} collective-permute-done((bf16[80,192]{1,0:T(8,128)(2,1)S(1)}, bf16[80,192]{1,0:T(8,128)(2,1)S(1)}, u32[]{:S(2)}, u32[]{:S(2)}) %collective-permute-start.8) | collective-permute-done | bytes 30752 | tf_op jit(solution)/shard_map/ppermute | solution.py:309
  22.0 1.0 %collective-permute-done.9.refs_3_ = bf16[80,192]{1,0:T(8,128)(2,1)S(1)} collective-permute-done((bf16[80,192]{1,0:T(8,128)(2,1)S(1)}, bf16[80,192]{1,0:T(8,128)(2,1)S(1)}, u32[]{:S(2)}, u32[]{:S(2)}) %collective-permute-start.9) | collective-permute-done | bytes 30752 | tf_op jit(solution)/shard_map/ppermute | solution.py:309
  23.0 0.9 %row_slots.1 = bf16[1,2,40,4,192]{4,3,2,1,0:T(4,128)(2,1)} custom-call(bf16[80,192]{1,0:T(8,128)(2,1)S(1)} %get-tuple-element.27.refs_0_, bf16[80,192]{1,0:T(8,128)(2,1)S(1)} %collective-permute-done.7.refs_1_, bf16[80,192]{1,0:T(8,128)(2,1)S(1)} %collective-permute-done.8.refs_2_, bf16[80,192]{1,0:T(8,128)(2,1)S(1)} %collective-permute-done.9.refs_3_), custom_call_target="tpu_custom_call" | custom-call | tf_op jit(solution)/shard_map/row_slots/pallas_call | solution.py:310
Async XLA Ops:
  0.0 9.8 %collective-permute-start.2 = (bf16[40,640]{1,0:T(8,128)(2,1)}, bf16[40,640]{1,0:T(8,128)(2,1)S(1)}, u32[]{:S(2)}, u32[]{:S(2)}) collective-permute-start(bf16[40,640]{1,0:T(8,128)(2,1)} %bitcast.3), channel_id=1, source_target_pairs={{0,6},{1,7},{2,4},{3,5},{4,2},{5,3},{6,0},{7,1},{8,14},{9,15},{10,... | collective-permute-start | bytes 153608 | tf_op jit(solution)/shard_map/ppermute | solution.py:281
  5.0 5.2 %collective-permute-start.1 = (bf16[40,640]{1,0:T(8,128)(2,1)}, bf16[40,640]{1,0:T(8,128)(2,1)S(1)}, u32[]{:S(2)}, u32[]{:S(2)}) collective-permute-start(bf16[40,640]{1,0:T(8,128)(2,1)} %bitcast.4), channel_id=1, source_target_pairs={{0,4},{1,5},{2,6},{3,7},{4,0},{5,1},{6,2},{7,3},{8,12},{9,13},{10,... | collective-permute-start | bytes 153608 | tf_op jit(solution)/shard_map/ppermute | solution.py:281
  5.1 5.2 %collective-permute-start = (bf16[40,640]{1,0:T(8,128)(2,1)}, bf16[40,640]{1,0:T(8,128)(2,1)S(1)}, u32[]{:S(2)}, u32[]{:S(2)}) collective-permute-start(bf16[40,640]{1,0:T(8,128)(2,1)} %bitcast.5), channel_id=1, source_target_pairs={{0,2},{1,3},{2,0},{3,1},{4,6},{5,7},{6,4},{7,5},{8,10},{9,11},{10,... | collective-permute-start | bytes 153608 | tf_op jit(solution)/shard_map/ppermute | solution.py:281
  5.6 8.2 %collective-permute-start.3 = (bf16[40,640]{1,0:T(8,128)(2,1)}, bf16[40,640]{1,0:T(8,128)(2,1)S(1)}, u32[]{:S(2)}, u32[]{:S(2)}) collective-permute-start(bf16[40,640]{1,0:T(8,128)(2,1)} %bitcast.6), channel_id=1, source_target_pairs={{0,1},{1,0},{2,3},{3,2},{4,5},{5,4},{6,7},{7,6},{8,9},{9,8},{10,11... | collective-permute-start | bytes 153608 | tf_op jit(solution)/shard_map/ppermute | solution.py:285
  10.3 4.4 %collective-permute-start.4 = (bf16[40,640]{1,0:T(8,128)(2,1)S(1)}, bf16[40,640]{1,0:T(8,128)(2,1)S(1)}, u32[]{:S(2)}, u32[]{:S(2)}) collective-permute-start(bf16[40,640]{1,0:T(8,128)(2,1)S(1)} %collective-permute-done.refs_6_), channel_id=1, source_target_pairs={{0,1},{1,0},{2,3},{3,2},{4,5},{5,4},{6,7},{7,6},{8,9},{9,8},{10,11... | collective-permute-start | bytes 153608 | tf_op jit(solution)/shard_map/ppermute | solution.py:285
  11.8 4.1 %collective-permute-start.5 = (bf16[40,640]{1,0:T(8,128)(2,1)S(1)}, bf16[40,640]{1,0:T(8,128)(2,1)S(1)}, u32[]{:S(2)}, u32[]{:S(2)}) collective-permute-start(bf16[40,640]{1,0:T(8,128)(2,1)S(1)} %collective-permute-done.1.refs_7_), channel_id=1, source_target_pairs={{0,1},{1,0},{2,3},{3,2},{4,5},{5,4},{6,7},{7,6},{8,9},{9,8},{10,11... | collective-permute-start | bytes 153608 | tf_op jit(solution)/shard_map/ppermute | solution.py:285
  12.3 4.2 %collective-permute-start.6 = (bf16[40,640]{1,0:T(8,128)(2,1)S(1)}, bf16[40,640]{1,0:T(8,128)(2,1)S(1)}, u32[]{:S(2)}, u32[]{:S(2)}) collective-permute-start(bf16[40,640]{1,0:T(8,128)(2,1)S(1)} %collective-permute-done.2.refs_8_), channel_id=1, source_target_pairs={{0,1},{1,0},{2,3},{3,2},{4,5},{5,4},{6,7},{7,6},{8,9},{9,8},{10,11... | collective-permute-start | bytes 153608 | tf_op jit(solution)/shard_map/ppermute | solution.py:285
  17.9 1.9 %collective-permute-start.7 = (bf16[80,192]{1,0:T(8,128)(2,1)S(1)}, bf16[80,192]{1,0:T(8,128)(2,1)S(1)}, u32[]{:S(2)}, u32[]{:S(2)}) collective-permute-start(bf16[80,192]{1,0:T(8,128)(2,1)S(1)} %get-tuple-element.28), channel_id=1, source_target_pairs={{0,8},{8,0},{16,24},{24,16},{1,9},{9,1},{17,25},{25,17},{2,10},{10... | collective-permute-start | bytes 92168 | tf_op jit(solution)/shard_map/ppermute | solution.py:309
  17.9 4.1 %collective-permute-start.8 = (bf16[80,192]{1,0:T(8,128)(2,1)S(1)}, bf16[80,192]{1,0:T(8,128)(2,1)S(1)}, u32[]{:S(2)}, u32[]{:S(2)}) collective-permute-start(bf16[80,192]{1,0:T(8,128)(2,1)S(1)} %get-tuple-element.29), channel_id=1, source_target_pairs={{0,16},{8,24},{16,0},{24,8},{1,17},{9,25},{17,1},{25,9},{2,18},{10... | collective-permute-start | bytes 92168 | tf_op jit(solution)/shard_map/ppermute | solution.py:309
  19.5 3.5 %collective-permute-start.9 = (bf16[80,192]{1,0:T(8,128)(2,1)S(1)}, bf16[80,192]{1,0:T(8,128)(2,1)S(1)}, u32[]{:S(2)}, u32[]{:S(2)}) collective-permute-start(bf16[80,192]{1,0:T(8,128)(2,1)S(1)} %get-tuple-element.30), channel_id=1, source_target_pairs={{0,24},{8,16},{16,8},{24,0},{1,25},{9,17},{17,9},{25,1},{2,26},{10... | collective-permute-start | bytes 92168 | tf_op jit(solution)/shard_map/ppermute | solution.py:309

commit v3 on v2

--- a/solution.py
+++ b/solution.py
@@ -52,10 +52,10 @@
 
 
 def tables_kernel(
-    blocks, block, index_of, lat_ref, waves_hbm, coupling_hbm, tend_hbm, traj_hbm, *refs
+    blocks, block, held, index_of, lat_ref, waves_hbm, coupling_hbm, tend_hbm, traj_hbm, *refs
 ):
-    table_ref, phase_ref, mix_ref, kept_ref, own_ref, coriolis_ref = refs[:6]
-    waves_ref, coupling_ref, tend_ref, sems = refs[6:]
+    far_table_ref, own_table_ref, phase_ref, mix_ref, kept_ref, own_ref, coriolis_ref = refs[:7]
+    waves_ref, coupling_ref, tend_ref, sems = refs[7:]
     copies = [
         pltpu.make_async_copy(source_ref, target_ref, sems.at[i])
         for i, (source_ref, target_ref) in enumerate(
@@ -75,6 +75,18 @@
     waves_total = waves_ref.shape[0]
     points = jnp.full((1, 1), count, jnp.int32).astype(jnp.float32)
     waves = waves_ref[...].reshape(1, waves_total).astype(jnp.float32)
+    bands = len(held)
+    share = waves_total // bands
+    shares = [waves[:, d * share : (d + 1) * share] for d in range(bands)]
+    my_band = lax.axis_index("band")
+    ordered = []
+    for step in held:
+        goal = partner(my_band, step, bands)
+        chosen = shares[0]
+        for d in range(1, bands):
+            chosen = jnp.where(goal == d, shares[d], chosen)
+        ordered.append(chosen)
+    waves = jnp.concatenate(ordered, axis=1)
 
     coarse_rows = block // SUB
     coarse_pad = -(-coarse_rows // 8) * 8
@@ -86,12 +98,13 @@
         here_cos = coarse_cos[row : row + 1]
         here_sin = coarse_sin[row : row + 1]
         rows = pl.ds(row * SUB, SUB)
-        table_ref[rows, :waves_total] = (here_cos * fine_cos - here_sin * fine_sin).astype(
-            jnp.bfloat16
-        )
-        table_ref[rows, waves_total:] = (here_cos * fine_sin + here_sin * fine_cos).astype(
-            jnp.bfloat16
-        )
+        table_cos = (here_cos * fine_cos - here_sin * fine_sin).astype(jnp.bfloat16)
+        table_sin = (here_cos * fine_sin + here_sin * fine_cos).astype(jnp.bfloat16)
+        far = waves_total - share
+        far_table_ref[rows, :far] = table_cos[:, :far]
+        far_table_ref[rows, far:] = table_sin[:, :far]
+        own_table_ref[rows, :share] = table_cos[:, far:]
+        own_table_ref[rows, share:] = table_sin[:, far:]
 
     slot = lax.broadcasted_iota(jnp.int32, (blocks, 1), 0)
     first = jnp.zeros((blocks, 1), jnp.int32)
@@ -133,15 +146,40 @@
     copies[3].wait()
 
 
-def main_kernel(blocks, block, parts, index_of, *refs):
+def transform(flat, table_ref, phase_ref, first_wave, out_refs):
+    column_vars = out_refs[0].shape[0] // 2
+    blocks = flat.shape[0] // column_vars
+    wide = table_ref.shape[1]
+    waves = wide // 2
+    share = out_refs[0].shape[1]
+    near = jnp.concatenate(
+        [
+            jnp.dot(flat, table_ref[:, i : min(i + 256, wide)], preferred_element_type=jnp.float32)
+            for i in range(0, wide, 256)
+        ],
+        axis=1,
+    )
+    real = jnp.zeros((column_vars, waves), jnp.float32)
+    imag = jnp.zeros((column_vars, waves), jnp.float32)
+    for i in range(blocks):
+        rows = slice(i * column_vars, (i + 1) * column_vars)
+        near_cos, near_sin = near[rows, :waves], near[rows, waves:]
+        far_cos = phase_ref[0, i : i + 1, first_wave : first_wave + waves]
+        far_sin = phase_ref[1, i : i + 1, first_wave : first_wave + waves]
+        real = real + (far_cos * near_cos - far_sin * near_sin)
+        imag = imag + (far_cos * near_sin + far_sin * near_cos)
+    both = jnp.concatenate([real, imag], axis=0)
+    for k, out_ref in enumerate(out_refs):
+        out_ref[...] = both[:, k * share : (k + 1) * share].astype(jnp.bfloat16)
+
+
+def main_kernel(blocks, block, index_of, *refs):
     coriolis_ref, mix_ref, table_ref, phase_ref, tend_ref = refs[:5]
     traj_refs = refs[5 : 5 + blocks]
-    out_refs = refs[5 + blocks : 5 + blocks + parts]
-    grid_ref = refs[5 + blocks + parts]
+    flat_ref = refs[5 + blocks]
+    out_refs = refs[6 + blocks : -1]
+    grid_ref = refs[-1]
     column_vars = tend_ref.shape[0]
-    waves_total = phase_ref.shape[2]
-    share = waves_total // parts
-
     coriolis = coriolis_ref[:, :1]
     mix = mix_ref[...]
     for i, index in enumerate(index_of()):
@@ -159,43 +197,18 @@
             ],
             axis=0,
         )
-
     flat = grid_ref[...].astype(jnp.bfloat16)
-    reals = []
-    imags = []
-    width = math.gcd(waves_total, 256)
-    for first_wave in range(0, waves_total, width):
-        cols = slice(first_wave, first_wave + width)
-        near_cos = jnp.dot(flat, table_ref[:, cols], preferred_element_type=jnp.float32)
-        near_sin = jnp.dot(
-            flat,
-            table_ref[:, waves_total + first_wave : waves_total + first_wave + width],
-            preferred_element_type=jnp.float32,
-        )
-        real = jnp.zeros((column_vars, width), jnp.float32)
-        imag = jnp.zeros((column_vars, width), jnp.float32)
-        for i in range(blocks):
-            rows = slice(i * column_vars, (i + 1) * column_vars)
-            far_cos = phase_ref[0, i : i + 1, cols]
-            far_sin = phase_ref[1, i : i + 1, cols]
-            real = real + (far_cos * near_cos[rows] - far_sin * near_sin[rows])
-            imag = imag + (far_cos * near_sin[rows] + far_sin * near_cos[rows])
-        reals.append(real)
-        imags.append(imag)
-    both = jnp.concatenate(
-        [jnp.concatenate(reals, axis=1), jnp.concatenate(imags, axis=1)], axis=0
-    )
-    shares = [both[:, d * share : (d + 1) * share] for d in range(parts)]
-    my_band = lax.axis_index("band")
-    for k in range(parts):
-        goal = partner(my_band, k, parts)
-        chosen = shares[0]
-        for d in range(1, parts):
-            chosen = jnp.where(goal == d, shares[d], chosen)
-        out_refs[k][...] = chosen.astype(jnp.bfloat16)
-
-
-def place_kernel(parts, *refs):
+    flat_ref[...] = flat
+    transform(flat, table_ref, phase_ref, 0, out_refs)
+
+
+def own_kernel(flat_ref, table_ref, phase_ref, out_ref):
+    first_wave = phase_ref.shape[2] - out_ref.shape[1]
+    transform(flat_ref[...], table_ref, phase_ref, first_wave, [out_ref])
+
+
+def place_kernel(held, *refs):
+    parts = len(held)
     in_refs = refs[:parts]
     out_ref = refs[parts]
     column_vars = out_ref.shape[2]
@@ -209,7 +222,9 @@
     else:
         step = lax.axis_index("band") - slot
         step = jnp.where(step < 0, step + parts, step)
-    target = step * column_vars + variable
+    target = variable
+    for position, which in enumerate(held):
+        target = jnp.where(step == which, target + position * column_vars, target)
     choose = (target == lax.broadcasted_iota(jnp.int32, (total, total), 1)).astype(jnp.bfloat16)
     wide = [ref[...].astype(jnp.float32) for ref in in_refs]
     for half in range(2):
@@ -236,7 +251,12 @@
     inner = 2 if cols % 2 == 0 else 1
     outer = cols // inner
     direct = own % LANES == 0
+    order = sorted(range(1, outer), key=lambda step: (step > 2, -step))
+    moves = [(step, 0) for step in order]
+    if inner == 2:
+        moves += [(0, 1)] + [(step, 1) for step in order]
     blocks = cols if direct else 8
+    held = list(reversed(range(bands)))
     block = width // blocks
 
     def index_of():
@@ -244,14 +264,16 @@
             return list(range(blocks))
         my_col = lax.axis_index("col")
         far, near = my_col // inner, my_col % inner
-        indices = [source(far, step, outer) * inner + near for step in range(outer)]
-        return indices + [index ^ 1 for index in indices] if inner == 2 else indices
+        return [my_col] + [
+            source(far, step, outer) * inner + (near ^ turned) for step, turned in moves
+        ]
 
     operands = [wave_order, coupling, tend, traj]
-    table, phase, mix, kept, own_piece, coriolis = pl.pallas_call(
-        functools.partial(tables_kernel, blocks, block, index_of),
+    far_table, own_table, phase, mix, kept, own_piece, coriolis = pl.pallas_call(
+        functools.partial(tables_kernel, blocks, block, held, index_of),
         out_shape=[
-            jax.ShapeDtypeStruct((block, 2 * waves_total), jnp.bfloat16),
+            jax.ShapeDtypeStruct((block, 2 * (waves_total - share)), jnp.bfloat16),
+            jax.ShapeDtypeStruct((block, 2 * share), jnp.bfloat16),
             jax.ShapeDtypeStruct((2, blocks, waves_total), jnp.float32),
             jax.ShapeDtypeStruct((2 * column_vars, 3 * column_vars), jnp.bfloat16),
             jax.ShapeDtypeStruct((column_vars, width), jnp.bfloat16),
@@ -259,7 +281,7 @@
             jax.ShapeDtypeStruct((1, LANES), jnp.float32),
         ],
         in_specs=[SMEM_SPEC] + [HBM_SPEC] * len(operands),
-        out_specs=[VMEM_SPEC] * 6,
+        out_specs=[VMEM_SPEC] * 7,
         scratch_shapes=[
             pltpu.VMEM((waves_total,), jnp.int32),
             pltpu.VMEM((column_vars, column_vars), jnp.bfloat16),
@@ -275,40 +297,59 @@
 
     if direct:
         places = [(i // inner, i % inner) for i in range(cols)]
-        arrived = []
-        for step in range(1, outer):
-            pairs = [(f * inner + n, partner(f, step, outer) * inner + n) for f, n in places]
-            arrived.append(lax.ppermute(traj, "col", pairs))
-        if inner == 2:
-            pairs = [(i, i ^ 1) for i in range(cols)]
-            passed = [lax.optimization_barrier((piece, coriolis))[0] for piece in arrived]
-            arrived += [lax.ppermute(piece, "col", pairs) for piece in [traj] + passed]
+        moved = {}
+        for step, turned in moves:
+            if turned and step > 1:
+                pairs = [(i, i ^ 1) for i in range(cols)]
+                moved[step, turned] = lax.ppermute(moved[step, 0], "col", pairs)
+            else:
+                pairs = [
+                    (f * inner + n, partner(f, step, outer) * inner + (n ^ turned)) for f, n in places
+                ]
+                moved[step, turned] = lax.ppermute(traj, "col", pairs)
+        arrived = [moved[move] for move in moves]
     else:
         whole = lax.all_gather(traj, "col", axis=1, tiled=True)
         arrived = [whole[:, i * block : (i + 1) * block] for i in range(8)]
 
     pieces = [own_piece] + arrived if direct else arrived
-    parts = pl.pallas_call(
-        functools.partial(main_kernel, blocks, block, bands, index_of),
-        out_shape=[jax.ShapeDtypeStruct((2 * column_vars, share), jnp.bfloat16)] * bands,
+    spectra = jax.ShapeDtypeStruct((2 * column_vars, share), jnp.bfloat16)
+    flat, *parts = pl.pallas_call(
+        functools.partial(main_kernel, blocks, block, index_of),
+        out_shape=[jax.ShapeDtypeStruct((blocks * column_vars, block), jnp.bfloat16)]
+        + [spectra] * (bands - 1),
         in_specs=[VMEM_SPEC] * (5 + blocks),
         out_specs=[VMEM_SPEC] * bands,
         scratch_shapes=[pltpu.VMEM((blocks * column_vars, block), jnp.float32)],
         compiler_params=pltpu.CompilerParams(vmem_limit_bytes=24 * 1024 * 1024),
         cost_estimate=pl.CostEstimate(
-            flops=4 * column_vars * width * waves_total,
+            flops=4 * column_vars * width * (waves_total - share),
             bytes_accessed=4 * column_vars * width,
             transcendentals=0,
         ),
         name="column_and_waves",
-    )(coriolis, mix, table, phase, kept, *pieces)
-
-    ready = [parts[0]]
-    for step in range(1, bands):
+    )(coriolis, mix, far_table, phase, kept, *pieces)
+    ready = []
+    for step, part in zip(held, parts):
         pairs = [(i, partner(i, step, bands)) for i in range(bands)]
-        ready.append(lax.ppermute(parts[step], "band", pairs))
+        ready.append(lax.ppermute(part, "band", pairs))
+    ready.append(
+        pl.pallas_call(
+            own_kernel,
+            out_shape=spectra,
+            in_specs=[VMEM_SPEC] * 3,
+            out_specs=VMEM_SPEC,
+            compiler_params=pltpu.CompilerParams(vmem_limit_bytes=24 * 1024 * 1024),
+            cost_estimate=pl.CostEstimate(
+                flops=4 * column_vars * width * share,
+                bytes_accessed=4 * column_vars * width,
+                transcendentals=0,
+            ),
+            name="own_waves",
+        )(flat, own_table, phase)
+    )
     return pl.pallas_call(
-        functools.partial(place_kernel, bands),
+        functools.partial(place_kernel, held),
         out_shape=jax.ShapeDtypeStruct((1, 2, column_vars, bands, share), jnp.bfloat16),
         in_specs=[VMEM_SPEC] * bands,
         out_specs=VMEM_SPEC,

time: 24.1 us -> 21.3 us (0.88)
  waiting for transfers between devices: 6.34 us -> 2.18 us
  Pallas kernels: 4.04 us -> 4.74 us
  starting transfers between devices: 12.8 us -> 13.5 us
    ppermute x10, waiting for transfers between devices: 6.34 us -> 2.18 us  [the longest x3 1.95 us: body(): ready.append(lax.ppermute(part, 'band', pairs))]
    pallas_call x3 -> x4, Pallas kernels: 4.04 us -> 4.74 us  [the longest x1 2 us: body(): pl.pallas_call(functools.partial(tables_kernel, blocks, block, held, inde...]
    ppermute x10, starting transfers between devices: 12.8 us -> 13.5 us  [the longest x5 8.54 us: body(): moved[step, turned] = lax.ppermute(traj, 'col', pairs)]
  transfers between devices with their start and end apart: 10 -> 10, of which waited for: 6 -> 3; matrix products, arithmetic and copies ran while one was open for 0% -> 0% of each run, Pallas kernels for 7% -> 12%
where the time goes in v3:
time: 21.3 us; the launch traced here: 21.1 us
  starting transfers between devices  13.5 us (63%)
  Pallas kernels  4.74 us (22%)
  waiting for transfers between devices  2.18 us (10%)
  between operations  0.73 us (3%)
    ppermute x5, starting transfers between devices, body(): moved[step, turned] = lax.ppermute(traj, 'col', pairs)  8.54 us
    ppermute x2, starting transfers between devices, body(): moved[step, turned] = lax.ppermute(moved[step, 0], 'col', pairs)  3.03 us
    pallas_call x1, Pallas kernels, body(): pl.pallas_call(functools.partial(tables_kernel, blocks, block, held, inde...  2 us
    ppermute x3, waiting for transfers between devices, body(): ready.append(lax.ppermute(part, 'band', pairs))  1.95 us
    ppermute x3, starting transfers between devices, body(): ready.append(lax.ppermute(part, 'band', pairs))  1.92 us
    pallas_call x1, Pallas kernels, body(): pl.pallas_call(functools.partial(main_kernel, blocks, block, index_of), o...  1.28 us
    pallas_call x1, Pallas kernels, body(): pl.pallas_call(functools.partial(place_kernel, held), out_shape=jax.Shape...  0.88 us
    pallas_call x1, Pallas kernels, body(): pl.pallas_call(own_kernel, out_shape=spectra, in_specs=[VMEM_SPEC] * 3, o...  0.57 us
  transfers between devices with their start and end apart: 10, of which 3 were waited for; matrix products, arithmetic and copies ran while one was open for 0% of the time, Pallas kernels for 12%

profile of v3, /device:TPU:0, one launch (start us, length us, event | category | flops | bytes accessed | tf_op | source)
XLA Modules:
  0.0 21.1 jit_solution(12745985403890263789)
XLA Ops:
  0.0 5.0 %collective-permute-start.2 = (bf16[40,640]{1,0:T(8,128)(2,1)}, bf16[40,640]{1,0:T(8,128)(2,1)S(1)}, u32[]{:S(2)}, u32[]{:S(2)}) collective-permute-start(bf16[40,640]{1,0:T(8,128)(2,1)} %bitcast.3), channel_id=1, source_target_pairs={{0,6},{1,7},{2,4},{3,5},{4,2},{5,3},{6,0},{7,1},{8,14},{9,15},{10,... | collective-permute-start | bytes 153608 | tf_op jit(solution)/shard_map/ppermute | solution.py:309
  5.0 0.0 collective-permute-start
  5.1 1.7 %collective-permute-start.5 = (bf16[40,640]{1,0:T(8,128)(2,1)}, bf16[40,640]{1,0:T(8,128)(2,1)S(1)}, u32[]{:S(2)}, u32[]{:S(2)}) collective-permute-start(bf16[40,640]{1,0:T(8,128)(2,1)} %bitcast.5), channel_id=1, source_target_pairs={{0,3},{1,2},{2,1},{3,0},{4,7},{5,6},{6,5},{7,4},{8,11},{9,10},{10,... | collective-permute-start | bytes 153608 | tf_op jit(solution)/shard_map/ppermute | solution.py:309
  6.8 0.3 %collective-permute-start.3 = (bf16[40,640]{1,0:T(8,128)(2,1)}, bf16[40,640]{1,0:T(8,128)(2,1)S(1)}, u32[]{:S(2)}, u32[]{:S(2)}) collective-permute-start(bf16[40,640]{1,0:T(8,128)(2,1)} %bitcast.6), channel_id=1, source_target_pairs={{0,1},{1,0},{2,3},{3,2},{4,5},{5,4},{6,7},{7,6},{8,9},{9,8},{10,11... | collective-permute-start | bytes 153608 | tf_op jit(solution)/shard_map/ppermute | solution.py:309
  7.1 1.5 %collective-permute-start.1 = (bf16[40,640]{1,0:T(8,128)(2,1)}, bf16[40,640]{1,0:T(8,128)(2,1)S(1)}, u32[]{:S(2)}, u32[]{:S(2)}) collective-permute-start(bf16[40,640]{1,0:T(8,128)(2,1)} %bitcast.7), channel_id=1, source_target_pairs={{0,2},{1,3},{2,0},{3,1},{4,6},{5,7},{6,4},{7,5},{8,10},{9,11},{10,... | collective-permute-start | bytes 153608 | tf_op jit(solution)/shard_map/ppermute | solution.py:309
  8.5 0.0 collective-permute-done.2.refs_8_
  8.5 1.5 %collective-permute-start.6 = (bf16[40,640]{1,0:T(8,128)(2,1)S(1)}, bf16[40,640]{1,0:T(8,128)(2,1)S(1)}, u32[]{:S(2)}, u32[]{:S(2)}) collective-permute-start(bf16[40,640]{1,0:T(8,128)(2,1)S(1)} %collective-permute-done.2.refs_8_), channel_id=1, source_target_pairs={{0,1},{1,0},{2,3},{3,2},{4,5},{5,4},{6,7},{7,6},{8,9},{9,8},{10,11... | collective-permute-start | bytes 153608 | tf_op jit(solution)/shard_map/ppermute | solution.py:304
  10.1 0.2 collective-permute-done.refs_6_
  10.3 1.5 %collective-permute-start.4 = (bf16[40,640]{1,0:T(8,128)(2,1)S(1)}, bf16[40,640]{1,0:T(8,128)(2,1)S(1)}, u32[]{:S(2)}, u32[]{:S(2)}) collective-permute-start(bf16[40,640]{1,0:T(8,128)(2,1)S(1)} %collective-permute-done.refs_6_), channel_id=1, source_target_pairs={{0,1},{1,0},{2,3},{3,2},{4,5},{5,4},{6,7},{7,6},{8,9},{9,8},{10,11... | collective-permute-start | bytes 153608 | tf_op jit(solution)/shard_map/ppermute | solution.py:304
  12.4 2.0 %tables.1 = (bf16[640,1152]{1,0:T(8,128)(2,1)S(1)}, bf16[640,384]{1,0:T(8,128)(2,1)S(1)}, f32[2,8,768]{2,1,0:T(8,128)S(1)}, bf16[80,120]{1,0:T(8,128)(2,1)S(1)},...) custom-call(s32[1]{0:T(128)S(6)} %copy.6.lat_ref, s32[768]{0:T(1024)} %waves_hbm.1, ...), custom_call_target="tpu_custom_call" | custom-call | flops 209715200 | bytes 819200 | tf_op jit(solution)/shard_map/tables/pallas_call | solution.py:272
  14.5 0.0 collective-permute-done.5.refs_11_
  14.5 0.0 collective-permute-done.3.refs_9_
  14.5 0.0 collective-permute-done.1.refs_7_
  14.5 0.0 collective-permute-done.6.refs_12_
  14.5 0.0 collective-permute-done.4.refs_10_
  14.5 1.3 %column_and_waves.1 = (bf16[320,640]{1,0:T(8,128)(2,1)S(1)}, bf16[80,192]{1,0:T(8,128)(2,1)S(1)}, bf16[80,192]{1,0:T(8,128)(2,1)S(1)}, bf16[80,192]{1,0:T(8,128)(2,1)S(1)}) custom-call(f32[1,128]{1,0:T(1,128)S(1)} %get-tuple-element.16.refs_0_, bf16[80,120]{1,0:T(8,128)(2,1)S(1)} %get-tuple-element.17.refs_1_, ...), custom_call_target="tpu_custom_call" | custom-call | flops 471859200 | bytes 819200 | tf_op jit(solution)/shard_map/column_and_waves/pallas_call | solution.py:317
  15.8 0.1 collective-permute-start.7
  15.9 1.6 %collective-permute-start.8 = (bf16[80,192]{1,0:T(8,128)(2,1)S(1)}, bf16[80,192]{1,0:T(8,128)(2,1)S(1)}, u32[]{:S(2)}, u32[]{:S(2)}) collective-permute-start(bf16[80,192]{1,0:T(8,128)(2,1)S(1)} %get-tuple-element.23), channel_id=1, source_target_pairs={{0,16},{8,24},{16,0},{24,8},{1,17},{9,25},{17,1},{25,9},{2,18},{10... | collective-permute-start | bytes 92168 | tf_op jit(solution)/shard_map/ppermute | solution.py:335
  17.4 0.3 %collective-permute-start.9 = (bf16[80,192]{1,0:T(8,128)(2,1)S(1)}, bf16[80,192]{1,0:T(8,128)(2,1)S(1)}, u32[]{:S(2)}, u32[]{:S(2)}) collective-permute-start(bf16[80,192]{1,0:T(8,128)(2,1)S(1)} %get-tuple-element.24), channel_id=1, source_target_pairs={{0,8},{8,0},{16,24},{24,16},{1,9},{9,1},{17,25},{25,17},{2,10},{10... | collective-permute-start | bytes 92168 | tf_op jit(solution)/shard_map/ppermute | solution.py:335
  17.7 0.6 %own_waves.1.refs_3_ = bf16[80,192]{1,0:T(8,128)(2,1)S(1)} custom-call(bf16[320,640]{1,0:T(8,128)(2,1)S(1)} %get-tuple-element.25.flat_ref, bf16[640,384]{1,0:T(8,128)(2,1)S(1)} %get-tuple-element.26.table_ref, f32[2,8,768]{2,1,0:T(8,128)S(1)} %get-tuple-element.19.refs_3_.phase_ref), custom_call_target="tpu_custom_call" | custom-call | flops 157286400 | bytes 819200 | tf_op jit(solution)/shard_map/own_waves/pallas_call | solution.py:337
  18.3 1.4 %collective-permute-done.7.refs_0_ = bf16[80,192]{1,0:T(8,128)(2,1)S(1)} collective-permute-done((bf16[80,192]{1,0:T(8,128)(2,1)S(1)}, bf16[80,192]{1,0:T(8,128)(2,1)S(1)}, u32[]{:S(2)}, u32[]{:S(2)}) %collective-permute-start.7) | collective-permute-done | bytes 30752 | tf_op jit(solution)/shard_map/ppermute | solution.py:335
  19.7 0.6 %collective-permute-done.8.refs_1_ = bf16[80,192]{1,0:T(8,128)(2,1)S(1)} collective-permute-done((bf16[80,192]{1,0:T(8,128)(2,1)S(1)}, bf16[80,192]{1,0:T(8,128)(2,1)S(1)}, u32[]{:S(2)}, u32[]{:S(2)}) %collective-permute-start.8) | collective-permute-done | bytes 30752 | tf_op jit(solution)/shard_map/ppermute | solution.py:335
  20.3 0.0 collective-permute-done.9.refs_2_
  20.3 0.9 %row_slots.1 = bf16[1,2,40,4,192]{4,3,2,1,0:T(4,128)(2,1)} custom-call(bf16[80,192]{1,0:T(8,128)(2,1)S(1)} %collective-permute-done.7.refs_0_, bf16[80,192]{1,0:T(8,128)(2,1)S(1)} %collective-permute-done.8.refs_1_, bf16[80,192]{1,0:T(8,128)(2,1)S(1)} %collective-permute-done.9.refs_2_, bf16[80,192]{1,0:T(8,128)(2,1)S(1)} %own_waves.1.refs_3_), custom_call_target="tpu_custom_call" | custom-call | tf_op jit(solution)/shard_map/row_slots/pallas_call | solution.py:351
Async XLA Ops:
  0.0 8.5 %collective-permute-start.2 = (bf16[40,640]{1,0:T(8,128)(2,1)}, bf16[40,640]{1,0:T(8,128)(2,1)S(1)}, u32[]{:S(2)}, u32[]{:S(2)}) collective-permute-start(bf16[40,640]{1,0:T(8,128)(2,1)} %bitcast.3), channel_id=1, source_target_pairs={{0,6},{1,7},{2,4},{3,5},{4,2},{5,3},{6,0},{7,1},{8,14},{9,15},{10,... | collective-permute-start | bytes 153608 | tf_op jit(solution)/shard_map/ppermute | solution.py:309
  5.0 5.2 %collective-permute-start = (bf16[40,640]{1,0:T(8,128)(2,1)}, bf16[40,640]{1,0:T(8,128)(2,1)S(1)}, u32[]{:S(2)}, u32[]{:S(2)}) collective-permute-start(bf16[40,640]{1,0:T(8,128)(2,1)} %bitcast.4), channel_id=1, source_target_pairs={{0,4},{1,5},{2,6},{3,7},{4,0},{5,1},{6,2},{7,3},{8,12},{9,13},{10,... | collective-permute-start | bytes 153608 | tf_op jit(solution)/shard_map/ppermute | solution.py:309
  5.1 9.4 %collective-permute-start.5 = (bf16[40,640]{1,0:T(8,128)(2,1)}, bf16[40,640]{1,0:T(8,128)(2,1)S(1)}, u32[]{:S(2)}, u32[]{:S(2)}) collective-permute-start(bf16[40,640]{1,0:T(8,128)(2,1)} %bitcast.5), channel_id=1, source_target_pairs={{0,3},{1,2},{2,1},{3,0},{4,7},{5,6},{6,5},{7,4},{8,11},{9,10},{10,... | collective-permute-start | bytes 153608 | tf_op jit(solution)/shard_map/ppermute | solution.py:309
  6.8 7.7 %collective-permute-start.3 = (bf16[40,640]{1,0:T(8,128)(2,1)}, bf16[40,640]{1,0:T(8,128)(2,1)S(1)}, u32[]{:S(2)}, u32[]{:S(2)}) collective-permute-start(bf16[40,640]{1,0:T(8,128)(2,1)} %bitcast.6), channel_id=1, source_target_pairs={{0,1},{1,0},{2,3},{3,2},{4,5},{5,4},{6,7},{7,6},{8,9},{9,8},{10,11... | collective-permute-start | bytes 153608 | tf_op jit(solution)/shard_map/ppermute | solution.py:309
  7.1 7.4 %collective-permute-start.1 = (bf16[40,640]{1,0:T(8,128)(2,1)}, bf16[40,640]{1,0:T(8,128)(2,1)S(1)}, u32[]{:S(2)}, u32[]{:S(2)}) collective-permute-start(bf16[40,640]{1,0:T(8,128)(2,1)} %bitcast.7), channel_id=1, source_target_pairs={{0,2},{1,3},{2,0},{3,1},{4,6},{5,7},{6,4},{7,5},{8,10},{9,11},{10,... | collective-permute-start | bytes 153608 | tf_op jit(solution)/shard_map/ppermute | solution.py:309
  8.5 5.9 %collective-permute-start.6 = (bf16[40,640]{1,0:T(8,128)(2,1)S(1)}, bf16[40,640]{1,0:T(8,128)(2,1)S(1)}, u32[]{:S(2)}, u32[]{:S(2)}) collective-permute-start(bf16[40,640]{1,0:T(8,128)(2,1)S(1)} %collective-permute-done.2.refs_8_), channel_id=1, source_target_pairs={{0,1},{1,0},{2,3},{3,2},{4,5},{5,4},{6,7},{7,6},{8,9},{9,8},{10,11... | collective-permute-start | bytes 153608 | tf_op jit(solution)/shard_map/ppermute | solution.py:304
  10.3 4.2 %collective-permute-start.4 = (bf16[40,640]{1,0:T(8,128)(2,1)S(1)}, bf16[40,640]{1,0:T(8,128)(2,1)S(1)}, u32[]{:S(2)}, u32[]{:S(2)}) collective-permute-start(bf16[40,640]{1,0:T(8,128)(2,1)S(1)} %collective-permute-done.refs_6_), channel_id=1, source_target_pairs={{0,1},{1,0},{2,3},{3,2},{4,5},{5,4},{6,7},{7,6},{8,9},{9,8},{10,11... | collective-permute-start | bytes 153608 | tf_op jit(solution)/shard_map/ppermute | solution.py:304
  15.8 3.9 %collective-permute-start.7 = (bf16[80,192]{1,0:T(8,128)(2,1)S(1)}, bf16[80,192]{1,0:T(8,128)(2,1)S(1)}, u32[]{:S(2)}, u32[]{:S(2)}) collective-permute-start(bf16[80,192]{1,0:T(8,128)(2,1)S(1)} %get-tuple-element.22), channel_id=1, source_target_pairs={{0,24},{8,16},{16,8},{24,0},{1,25},{9,17},{17,9},{25,1},{2,26},{10... | collective-permute-start | bytes 92168 | tf_op jit(solution)/shard_map/ppermute | solution.py:335
  15.9 4.4 %collective-permute-start.8 = (bf16[80,192]{1,0:T(8,128)(2,1)S(1)}, bf16[80,192]{1,0:T(8,128)(2,1)S(1)}, u32[]{:S(2)}, u32[]{:S(2)}) collective-permute-start(bf16[80,192]{1,0:T(8,128)(2,1)S(1)} %get-tuple-element.23), channel_id=1, source_target_pairs={{0,16},{8,24},{16,0},{24,8},{1,17},{9,25},{17,1},{25,9},{2,18},{10... | collective-permute-start | bytes 92168 | tf_op jit(solution)/shard_map/ppermute | solution.py:335
  17.4 2.8 %collective-permute-start.9 = (bf16[80,192]{1,0:T(8,128)(2,1)S(1)}, bf16[80,192]{1,0:T(8,128)(2,1)S(1)}, u32[]{:S(2)}, u32[]{:S(2)}) collective-permute-start(bf16[80,192]{1,0:T(8,128)(2,1)S(1)} %get-tuple-element.24), channel_id=1, source_target_pairs={{0,8},{8,0},{16,24},{24,16},{1,9},{9,1},{17,25},{25,17},{2,10},{10... | collective-permute-start | bytes 92168 | tf_op jit(solution)/shard_map/ppermute | solution.py:335

commit v4 on v3

--- a/solution.py
+++ b/solution.py
@@ -100,11 +100,12 @@
         rows = pl.ds(row * SUB, SUB)
         table_cos = (here_cos * fine_cos - here_sin * fine_sin).astype(jnp.bfloat16)
         table_sin = (here_cos * fine_sin + here_sin * fine_cos).astype(jnp.bfloat16)
-        far = waves_total - share
+        far = far_table_ref.shape[1] // 2
+        near = own_table_ref.shape[1] // 2
         far_table_ref[rows, :far] = table_cos[:, :far]
         far_table_ref[rows, far:] = table_sin[:, :far]
-        own_table_ref[rows, :share] = table_cos[:, far:]
-        own_table_ref[rows, share:] = table_sin[:, far:]
+        own_table_ref[rows, :near] = table_cos[:, waves_total - near :]
+        own_table_ref[rows, near:] = table_sin[:, waves_total - near :]
 
     slot = lax.broadcasted_iota(jnp.int32, (blocks, 1), 0)
     first = jnp.zeros((blocks, 1), jnp.int32)
@@ -146,12 +147,9 @@
     copies[3].wait()
 
 
-def transform(flat, table_ref, phase_ref, first_wave, out_refs):
-    column_vars = out_refs[0].shape[0] // 2
-    blocks = flat.shape[0] // column_vars
+def transform(flat, column_vars, table_ref, phase_ref, first_wave):
     wide = table_ref.shape[1]
     waves = wide // 2
-    share = out_refs[0].shape[1]
     near = jnp.concatenate(
         [
             jnp.dot(flat, table_ref[:, i : min(i + 256, wide)], preferred_element_type=jnp.float32)
@@ -161,16 +159,14 @@
     )
     real = jnp.zeros((column_vars, waves), jnp.float32)
     imag = jnp.zeros((column_vars, waves), jnp.float32)
-    for i in range(blocks):
+    for i in range(flat.shape[0] // column_vars):
         rows = slice(i * column_vars, (i + 1) * column_vars)
         near_cos, near_sin = near[rows, :waves], near[rows, waves:]
         far_cos = phase_ref[0, i : i + 1, first_wave : first_wave + waves]
         far_sin = phase_ref[1, i : i + 1, first_wave : first_wave + waves]
         real = real + (far_cos * near_cos - far_sin * near_sin)
         imag = imag + (far_cos * near_sin + far_sin * near_cos)
-    both = jnp.concatenate([real, imag], axis=0)
-    for k, out_ref in enumerate(out_refs):
-        out_ref[...] = both[:, k * share : (k + 1) * share].astype(jnp.bfloat16)
+    return jnp.concatenate([real, imag], axis=0)
 
 
 def main_kernel(blocks, block, index_of, *refs):
@@ -199,12 +195,19 @@
         )
     flat = grid_ref[...].astype(jnp.bfloat16)
     flat_ref[...] = flat
-    transform(flat, table_ref, phase_ref, 0, out_refs)
+    both = transform(flat, column_vars, table_ref, phase_ref, 0)
+    share = out_refs[0].shape[1]
+    for k, out_ref in enumerate(out_refs):
+        out_ref[...] = both[:, k * share : (k + 1) * share].astype(jnp.bfloat16)
 
 
 def own_kernel(flat_ref, table_ref, phase_ref, out_ref):
-    first_wave = phase_ref.shape[2] - out_ref.shape[1]
-    transform(flat_ref[...], table_ref, phase_ref, first_wave, [out_ref])
+    near = table_ref.shape[1] // 2
+    column_vars, share = out_ref.shape[0] // 2, out_ref.shape[1]
+    both = transform(
+        flat_ref[...], column_vars, table_ref, phase_ref, phase_ref.shape[2] - near
+    )
+    out_ref[...] = both[:, near - share :].astype(jnp.bfloat16)
 
 
 def place_kernel(held, *refs):
@@ -248,13 +251,11 @@
     tend = adjoint_tend.reshape(column_vars, width)
     traj = trajectory.reshape(column_vars, own)
 
-    inner = 2 if cols % 2 == 0 else 1
-    outer = cols // inner
-    direct = own % LANES == 0
-    order = sorted(range(1, outer), key=lambda step: (step > 2, -step))
-    moves = [(step, 0) for step in order]
-    if inner == 2:
-        moves += [(0, 1)] + [(step, 1) for step in order]
+    direct = own % LANES == 0 and cols > 1 and cols & (cols - 1) == 0
+    across = cols // 2
+    swaps = [2, 3, 5, 4, 7, 1, 6] if cols == 8 else list(range(1, cols))
+    far = -(-(waves_total - share) // LANES) * LANES
+    near = waves_total - (waves_total - share) // LANES * LANES
     blocks = cols if direct else 8
     held = list(reversed(range(bands)))
     block = width // blocks
@@ -263,17 +264,14 @@
         if not direct:
             return list(range(blocks))
         my_col = lax.axis_index("col")
-        far, near = my_col // inner, my_col % inner
-        return [my_col] + [
-            source(far, step, outer) * inner + (near ^ turned) for step, turned in moves
-        ]
+        return [my_col] + [my_col ^ swap for swap in swaps]
 
     operands = [wave_order, coupling, tend, traj]
     far_table, own_table, phase, mix, kept, own_piece, coriolis = pl.pallas_call(
         functools.partial(tables_kernel, blocks, block, held, index_of),
         out_shape=[
-            jax.ShapeDtypeStruct((block, 2 * (waves_total - share)), jnp.bfloat16),
-            jax.ShapeDtypeStruct((block, 2 * share), jnp.bfloat16),
+            jax.ShapeDtypeStruct((block, 2 * far), jnp.bfloat16),
+            jax.ShapeDtypeStruct((block, 2 * near), jnp.bfloat16),
             jax.ShapeDtypeStruct((2, blocks, waves_total), jnp.float32),
             jax.ShapeDtypeStruct((2 * column_vars, 3 * column_vars), jnp.bfloat16),
             jax.ShapeDtypeStruct((column_vars, width), jnp.bfloat16),
@@ -296,18 +294,14 @@
     )(row_lat, *[pltpu.with_memory_space_constraint(x, pltpu.HBM) for x in operands])
 
     if direct:
-        places = [(i // inner, i % inner) for i in range(cols)]
-        moved = {}
-        for step, turned in moves:
-            if turned and step > 1:
-                pairs = [(i, i ^ 1) for i in range(cols)]
-                moved[step, turned] = lax.ppermute(moved[step, 0], "col", pairs)
-            else:
-                pairs = [
-                    (f * inner + n, partner(f, step, outer) * inner + (n ^ turned)) for f, n in places
-                ]
-                moved[step, turned] = lax.ppermute(traj, "col", pairs)
-        arrived = [moved[move] for move in moves]
+        swapped = lambda x, swap: lax.ppermute(x, "col", [(i, i ^ swap) for i in range(cols)])
+        moved = {across: swapped(traj, across)}
+        for swap in swaps:
+            if across < swap < cols - 1:
+                moved[swap] = swapped(moved[across], swap ^ across)
+            elif swap != across:
+                moved[swap] = swapped(traj, swap)
+        arrived = [moved[swap] for swap in swaps]
     else:
         whole = lax.all_gather(traj, "col", axis=1, tiled=True)
         arrived = [whole[:, i * block : (i + 1) * block] for i in range(8)]

time: 21.3 us -> 20.8 us (0.977)
  starting transfers between devices: 13.5 us -> 12.5 us
  waiting for transfers between devices: 2.18 us -> 2.65 us
    ppermute x7, starting transfers between devices: 11.6 us -> 10.6 us  [body(): lax.ppermute(x, 'col', [(i, i ^ swap) for i in range(cols)])]
    ppermute x7, waiting for transfers between devices: 0.23 us -> 0.62 us  [body(): lax.ppermute(x, 'col', [(i, i ^ swap) for i in range(cols)])]
  transfers between devices with their start and end apart: 10 -> 10, of which waited for: 3 -> 4; matrix products, arithmetic and copies ran while one was open for 0% -> 0% of each run, Pallas kernels for 12% -> 13%
where the time goes in v4:
time: 20.8 us; the launch traced here: 20.6 us
  starting transfers between devices  12.5 us (60%)
  Pallas kernels  4.73 us (23%)
  waiting for transfers between devices  2.65 us (13%)
  between operations  0.72 us (3%)
    ppermute x7, starting transfers between devices, body(): lax.ppermute(x, 'col', [(i, i ^ swap) for i in range(cols)])  10.6 us
    pallas_call x1, Pallas kernels, body(): pl.pallas_call(functools.partial(tables_kernel, blocks, block, held, inde...  2.09 us
    ppermute x3, waiting for transfers between devices, body(): ready.append(lax.ppermute(part, 'band', pairs))  2.02 us
    ppermute x3, starting transfers between devices, body(): ready.append(lax.ppermute(part, 'band', pairs))  1.92 us
    pallas_call x1, Pallas kernels, body(): pl.pallas_call(functools.partial(main_kernel, blocks, block, index_of), o...  1.27 us
    pallas_call x1, Pallas kernels, body(): pl.pallas_call(functools.partial(place_kernel, held), out_shape=jax.Shape...  0.88 us
    ppermute x7, waiting for transfers between devices, body(): lax.ppermute(x, 'col', [(i, i ^ swap) for i in range(cols)])  0.62 us
    pallas_call x1, Pallas kernels, body(): pl.pallas_call(own_kernel, out_shape=spectra, in_specs=[VMEM_SPEC] * 3, o...  0.49 us
  transfers between devices with their start and end apart: 10, of which 4 were waited for; matrix products, arithmetic and copies ran while one was open for 0% of the time, Pallas kernels for 13%

profile of v4, /device:TPU:0, one launch (start us, length us, event | category | flops | bytes accessed | tf_op | source)
XLA Modules:
  0.0 20.6 jit_solution(12266027303740469603)
XLA Ops:
  0.0 4.0 %collective-permute-start.2 = (bf16[40,640]{1,0:T(8,128)(2,1)}, bf16[40,640]{1,0:T(8,128)(2,1)S(1)}, u32[]{:S(2)}, u32[]{:S(2)}) collective-permute-start(bf16[40,640]{1,0:T(8,128)(2,1)} %bitcast.3), channel_id=1, source_target_pairs={{0,4},{1,5},{2,6},{3,7},{4,0},{5,1},{6,2},{7,3},{8,12},{9,13},{10,... | collective-permute-start | bytes 153608 | tf_op jit(solution)/shard_map/ppermute | solution.py:297
  4.0 1.5 %collective-permute-start.5 = (bf16[40,640]{1,0:T(8,128)(2,1)}, bf16[40,640]{1,0:T(8,128)(2,1)S(1)}, u32[]{:S(2)}, u32[]{:S(2)}) collective-permute-start(bf16[40,640]{1,0:T(8,128)(2,1)} %bitcast.4), channel_id=1, source_target_pairs={{0,1},{1,0},{2,3},{3,2},{4,5},{5,4},{6,7},{7,6},{8,9},{9,8},{10,11... | collective-permute-start | bytes 153608 | tf_op jit(solution)/shard_map/ppermute | solution.py:297
  5.6 1.3 %collective-permute-start.4 = (bf16[40,640]{1,0:T(8,128)(2,1)}, bf16[40,640]{1,0:T(8,128)(2,1)S(1)}, u32[]{:S(2)}, u32[]{:S(2)}) collective-permute-start(bf16[40,640]{1,0:T(8,128)(2,1)} %bitcast.5), channel_id=1, source_target_pairs={{0,7},{1,6},{2,5},{3,4},{4,3},{5,2},{6,1},{7,0},{8,15},{9,14},{10,... | collective-permute-start | bytes 153608 | tf_op jit(solution)/shard_map/ppermute | solution.py:297
  6.8 0.5 %collective-permute-start.1 = (bf16[40,640]{1,0:T(8,128)(2,1)}, bf16[40,640]{1,0:T(8,128)(2,1)S(1)}, u32[]{:S(2)}, u32[]{:S(2)}) collective-permute-start(bf16[40,640]{1,0:T(8,128)(2,1)} %bitcast.6), channel_id=1, source_target_pairs={{0,3},{1,2},{2,1},{3,0},{4,7},{5,6},{6,5},{7,4},{8,11},{9,10},{10,... | collective-permute-start | bytes 153608 | tf_op jit(solution)/shard_map/ppermute | solution.py:297
  7.4 2.5 %collective-permute-start = (bf16[40,640]{1,0:T(8,128)(2,1)}, bf16[40,640]{1,0:T(8,128)(2,1)S(1)}, u32[]{:S(2)}, u32[]{:S(2)}) collective-permute-start(bf16[40,640]{1,0:T(8,128)(2,1)} %bitcast.7), channel_id=1, source_target_pairs={{0,2},{1,3},{2,0},{3,1},{4,6},{5,7},{6,4},{7,5},{8,10},{9,11},{10,... | collective-permute-start | bytes 153608 | tf_op jit(solution)/shard_map/ppermute | solution.py:297
  9.8 0.0 collective-permute-done.2.refs_9_
  9.8 0.0 collective-permute-start.6
  9.9 0.0 collective-permute-done.5.refs_11_
  9.9 0.8 %collective-permute-start.3 = (bf16[40,640]{1,0:T(8,128)(2,1)S(1)}, bf16[40,640]{1,0:T(8,128)(2,1)S(1)}, u32[]{:S(2)}, u32[]{:S(2)}) collective-permute-start(bf16[40,640]{1,0:T(8,128)(2,1)S(1)} %collective-permute-done.2.refs_9_), channel_id=1, source_target_pairs={{0,1},{1,0},{2,3},{3,2},{4,5},{5,4},{6,7},{7,6},{8,9},{9,8},{10,11... | collective-permute-start | bytes 153608 | tf_op jit(solution)/shard_map/ppermute | solution.py:297
  11.3 2.1 %tables.1 = (bf16[640,1280]{1,0:T(8,128)(2,1)S(1)}, bf16[640,512]{1,0:T(8,128)(2,1)S(1)}, f32[2,8,768]{2,1,0:T(8,128)S(1)}, bf16[80,120]{1,0:T(8,128)(2,1)S(1)},...) custom-call(s32[1]{0:T(128)S(6)} %copy.6.lat_ref, s32[768]{0:T(1024)} %waves_hbm.1, ...), custom_call_target="tpu_custom_call" | custom-call | flops 209715200 | bytes 819200 | tf_op jit(solution)/shard_map/tables/pallas_call | solution.py:270
  13.4 0.0 collective-permute-done.4.refs_10_
  13.4 0.0 collective-permute-done.1.refs_7_
  13.4 0.0 collective-permute-done.refs_6_
  13.4 0.5 %collective-permute-done.6.refs_12_ = bf16[40,640]{1,0:T(8,128)(2,1)S(1)} collective-permute-done((bf16[40,640]{1,0:T(8,128)(2,1)S(1)}, bf16[40,640]{1,0:T(8,128)(2,1)S(1)}, u32[]{:S(2)}, u32[]{:S(2)}) %collective-permute-start.6) | collective-permute-done | bytes 51232 | tf_op jit(solution)/shard_map/ppermute | solution.py:297
  13.9 0.1 collective-permute-done.3.refs_8_
  14.0 1.3 %column_and_waves.1 = (bf16[320,640]{1,0:T(8,128)(2,1)S(1)}, bf16[80,192]{1,0:T(8,128)(2,1)S(1)}, bf16[80,192]{1,0:T(8,128)(2,1)S(1)}, bf16[80,192]{1,0:T(8,128)(2,1)S(1)}) custom-call(f32[1,128]{1,0:T(1,128)S(1)} %get-tuple-element.16.refs_0_, bf16[80,120]{1,0:T(8,128)(2,1)S(1)} %get-tuple-element.17.refs_1_, ...), custom_call_target="tpu_custom_call" | custom-call | flops 471859200 | bytes 819200 | tf_op jit(solution)/shard_map/column_and_waves/pallas_call | solution.py:311
  15.3 0.1 collective-permute-start.7
  15.4 1.6 %collective-permute-start.8 = (bf16[80,192]{1,0:T(8,128)(2,1)S(1)}, bf16[80,192]{1,0:T(8,128)(2,1)S(1)}, u32[]{:S(2)}, u32[]{:S(2)}) collective-permute-start(bf16[80,192]{1,0:T(8,128)(2,1)S(1)} %get-tuple-element.23), channel_id=1, source_target_pairs={{0,16},{8,24},{16,0},{24,8},{1,17},{9,25},{17,1},{25,9},{2,18},{10... | collective-permute-start | bytes 92168 | tf_op jit(solution)/shard_map/ppermute | solution.py:329
  16.9 0.3 %collective-permute-start.9 = (bf16[80,192]{1,0:T(8,128)(2,1)S(1)}, bf16[80,192]{1,0:T(8,128)(2,1)S(1)}, u32[]{:S(2)}, u32[]{:S(2)}) collective-permute-start(bf16[80,192]{1,0:T(8,128)(2,1)S(1)} %get-tuple-element.24), channel_id=1, source_target_pairs={{0,8},{8,0},{16,24},{24,16},{1,9},{9,1},{17,25},{25,17},{2,10},{10... | collective-permute-start | bytes 92168 | tf_op jit(solution)/shard_map/ppermute | solution.py:329
  17.2 0.5 %own_waves.1.refs_3_ = bf16[80,192]{1,0:T(8,128)(2,1)S(1)} custom-call(bf16[320,640]{1,0:T(8,128)(2,1)S(1)} %get-tuple-element.25.flat_ref, bf16[640,512]{1,0:T(8,128)(2,1)S(1)} %get-tuple-element.26.table_ref, f32[2,8,768]{2,1,0:T(8,128)S(1)} %get-tuple-element.19.refs_3_.phase_ref), custom_call_target="tpu_custom_call" | custom-call | flops 157286400 | bytes 819200 | tf_op jit(solution)/shard_map/own_waves/pallas_call | solution.py:331
  17.7 1.5 %collective-permute-done.7.refs_0_ = bf16[80,192]{1,0:T(8,128)(2,1)S(1)} collective-permute-done((bf16[80,192]{1,0:T(8,128)(2,1)S(1)}, bf16[80,192]{1,0:T(8,128)(2,1)S(1)}, u32[]{:S(2)}, u32[]{:S(2)}) %collective-permute-start.7) | collective-permute-done | bytes 30752 | tf_op jit(solution)/shard_map/ppermute | solution.py:329
  19.2 0.6 %collective-permute-done.8.refs_1_ = bf16[80,192]{1,0:T(8,128)(2,1)S(1)} collective-permute-done((bf16[80,192]{1,0:T(8,128)(2,1)S(1)}, bf16[80,192]{1,0:T(8,128)(2,1)S(1)}, u32[]{:S(2)}, u32[]{:S(2)}) %collective-permute-start.8) | collective-permute-done | bytes 30752 | tf_op jit(solution)/shard_map/ppermute | solution.py:329
  19.8 0.0 collective-permute-done.9.refs_2_
  19.8 0.9 %row_slots.1 = bf16[1,2,40,4,192]{4,3,2,1,0:T(4,128)(2,1)} custom-call(bf16[80,192]{1,0:T(8,128)(2,1)S(1)} %collective-permute-done.7.refs_0_, bf16[80,192]{1,0:T(8,128)(2,1)S(1)} %collective-permute-done.8.refs_1_, bf16[80,192]{1,0:T(8,128)(2,1)S(1)} %collective-permute-done.9.refs_2_, bf16[80,192]{1,0:T(8,128)(2,1)S(1)} %own_waves.1.refs_3_), custom_call_target="tpu_custom_call" | custom-call | tf_op jit(solution)/shard_map/row_slots/pallas_call | solution.py:345
Async XLA Ops:
  0.0 9.8 %collective-permute-start.2 = (bf16[40,640]{1,0:T(8,128)(2,1)}, bf16[40,640]{1,0:T(8,128)(2,1)S(1)}, u32[]{:S(2)}, u32[]{:S(2)}) collective-permute-start(bf16[40,640]{1,0:T(8,128)(2,1)} %bitcast.3), channel_id=1, source_target_pairs={{0,4},{1,5},{2,6},{3,7},{4,0},{5,1},{6,2},{7,3},{8,12},{9,13},{10,... | collective-permute-start | bytes 153608 | tf_op jit(solution)/shard_map/ppermute | solution.py:297
  4.0 5.8 %collective-permute-start.5 = (bf16[40,640]{1,0:T(8,128)(2,1)}, bf16[40,640]{1,0:T(8,128)(2,1)S(1)}, u32[]{:S(2)}, u32[]{:S(2)}) collective-permute-start(bf16[40,640]{1,0:T(8,128)(2,1)} %bitcast.4), channel_id=1, source_target_pairs={{0,1},{1,0},{2,3},{3,2},{4,5},{5,4},{6,7},{7,6},{8,9},{9,8},{10,11... | collective-permute-start | bytes 153608 | tf_op jit(solution)/shard_map/ppermute | solution.py:297
  5.6 7.8 %collective-permute-start.4 = (bf16[40,640]{1,0:T(8,128)(2,1)}, bf16[40,640]{1,0:T(8,128)(2,1)S(1)}, u32[]{:S(2)}, u32[]{:S(2)}) collective-permute-start(bf16[40,640]{1,0:T(8,128)(2,1)} %bitcast.5), channel_id=1, source_target_pairs={{0,7},{1,6},{2,5},{3,4},{4,3},{5,2},{6,1},{7,0},{8,15},{9,14},{10,... | collective-permute-start | bytes 153608 | tf_op jit(solution)/shard_map/ppermute | solution.py:297
  6.8 6.5 %collective-permute-start.1 = (bf16[40,640]{1,0:T(8,128)(2,1)}, bf16[40,640]{1,0:T(8,128)(2,1)S(1)}, u32[]{:S(2)}, u32[]{:S(2)}) collective-permute-start(bf16[40,640]{1,0:T(8,128)(2,1)} %bitcast.6), channel_id=1, source_target_pairs={{0,3},{1,2},{2,1},{3,0},{4,7},{5,6},{6,5},{7,4},{8,11},{9,10},{10,... | collective-permute-start | bytes 153608 | tf_op jit(solution)/shard_map/ppermute | solution.py:297
  7.4 6.0 %collective-permute-start = (bf16[40,640]{1,0:T(8,128)(2,1)}, bf16[40,640]{1,0:T(8,128)(2,1)S(1)}, u32[]{:S(2)}, u32[]{:S(2)}) collective-permute-start(bf16[40,640]{1,0:T(8,128)(2,1)} %bitcast.7), channel_id=1, source_target_pairs={{0,2},{1,3},{2,0},{3,1},{4,6},{5,7},{6,4},{7,5},{8,10},{9,11},{10,... | collective-permute-start | bytes 153608 | tf_op jit(solution)/shard_map/ppermute | solution.py:297
  9.8 4.1 %collective-permute-start.6 = (bf16[40,640]{1,0:T(8,128)(2,1)S(1)}, bf16[40,640]{1,0:T(8,128)(2,1)S(1)}, u32[]{:S(2)}, u32[]{:S(2)}) collective-permute-start(bf16[40,640]{1,0:T(8,128)(2,1)S(1)} %collective-permute-done.2.refs_9_), channel_id=1, source_target_pairs={{0,2},{1,3},{2,0},{3,1},{4,6},{5,7},{6,4},{7,5},{8,10},{9,11},{10,... | collective-permute-start | bytes 153608 | tf_op jit(solution)/shard_map/ppermute | solution.py:297
  9.9 4.2 %collective-permute-start.3 = (bf16[40,640]{1,0:T(8,128)(2,1)S(1)}, bf16[40,640]{1,0:T(8,128)(2,1)S(1)}, u32[]{:S(2)}, u32[]{:S(2)}) collective-permute-start(bf16[40,640]{1,0:T(8,128)(2,1)S(1)} %collective-permute-done.2.refs_9_), channel_id=1, source_target_pairs={{0,1},{1,0},{2,3},{3,2},{4,5},{5,4},{6,7},{7,6},{8,9},{9,8},{10,11... | collective-permute-start | bytes 153608 | tf_op jit(solution)/shard_map/ppermute | solution.py:297
  15.3 3.9 %collective-permute-start.7 = (bf16[80,192]{1,0:T(8,128)(2,1)S(1)}, bf16[80,192]{1,0:T(8,128)(2,1)S(1)}, u32[]{:S(2)}, u32[]{:S(2)}) collective-permute-start(bf16[80,192]{1,0:T(8,128)(2,1)S(1)} %get-tuple-element.22), channel_id=1, source_target_pairs={{0,24},{8,16},{16,8},{24,0},{1,25},{9,17},{17,9},{25,1},{2,26},{10... | collective-permute-start | bytes 92168 | tf_op jit(solution)/shard_map/ppermute | solution.py:329
  15.4 4.4 %collective-permute-start.8 = (bf16[80,192]{1,0:T(8,128)(2,1)S(1)}, bf16[80,192]{1,0:T(8,128)(2,1)S(1)}, u32[]{:S(2)}, u32[]{:S(2)}) collective-permute-start(bf16[80,192]{1,0:T(8,128)(2,1)S(1)} %get-tuple-element.23), channel_id=1, source_target_pairs={{0,16},{8,24},{16,0},{24,8},{1,17},{9,25},{17,1},{25,9},{2,18},{10... | collective-permute-start | bytes 92168 | tf_op jit(solution)/shard_map/ppermute | solution.py:329
  16.9 2.8 %collective-permute-start.9 = (bf16[80,192]{1,0:T(8,128)(2,1)S(1)}, bf16[80,192]{1,0:T(8,128)(2,1)S(1)}, u32[]{:S(2)}, u32[]{:S(2)}) collective-permute-start(bf16[80,192]{1,0:T(8,128)(2,1)S(1)} %get-tuple-element.24), channel_id=1, source_target_pairs={{0,8},{8,0},{16,24},{24,16},{1,9},{9,1},{17,25},{25,17},{2,10},{10... | collective-permute-start | bytes 92168 | tf_op jit(solution)/shard_map/ppermute | solution.py:329

commit v5 on v4

--- a/solution.py
+++ b/solution.py
@@ -51,11 +51,31 @@
     return first, -second
 
 
+def column_step(block, indices, mix, coriolis, tend_ref, traj_refs, grid_ref):
+    column_vars = tend_ref.shape[0]
+    for i, (index, traj_ref) in enumerate(zip(indices, traj_refs)):
+        start = pl.multiple_of(index * block, LANES)
+        traj = traj_ref[...].astype(jnp.float32)
+        tend = tend_ref[:, pl.ds(start, block)].astype(jnp.float32)
+        stacked = jnp.concatenate([traj, tend, tend * traj], axis=0).astype(jnp.bfloat16)
+        mixed = jnp.dot(mix, stacked, preferred_element_type=jnp.float32)
+        total = mixed[column_vars:] + tend * mixed[:column_vars]
+        grid_ref[pl.ds(i * column_vars, column_vars), :] = jnp.concatenate(
+            [
+                total[:LEVELS] - coriolis * tend[LEVELS : 2 * LEVELS],
+                total[LEVELS : 2 * LEVELS] + coriolis * tend[:LEVELS],
+                total[2 * LEVELS :],
+            ],
+            axis=0,
+        )
+
+
 def tables_kernel(
-    blocks, block, held, index_of, lat_ref, waves_hbm, coupling_hbm, tend_hbm, traj_hbm, *refs
+    blocks, block, early, held, index_of, lat_ref, waves_hbm, coupling_hbm, tend_hbm, traj_hbm, *refs
 ):
-    far_table_ref, own_table_ref, phase_ref, mix_ref, kept_ref, own_ref, coriolis_ref = refs[:7]
-    waves_ref, coupling_ref, tend_ref, sems = refs[7:]
+    early_refs, refs = refs[: max(early - 1, 0)], refs[max(early - 1, 0) :]
+    far_table_ref, own_table_ref, phase_ref, mix_ref, kept_ref, coriolis_ref = refs[:6]
+    waves_ref, coupling_ref, tend_ref, own_ref, sems = refs[6 + (early > 0) :]
     copies = [
         pltpu.make_async_copy(source_ref, target_ref, sems.at[i])
         for i, (source_ref, target_ref) in enumerate(
@@ -145,6 +165,16 @@
             place < count, tend_ref[:, cols].astype(jnp.float32), 0.0
         ).astype(jnp.bfloat16)
     copies[3].wait()
+    if early:
+        column_step(
+            block,
+            index_of()[:early],
+            mix_ref[...],
+            coriolis_ref[:, :1],
+            kept_ref,
+            [own_ref, *early_refs],
+            refs[6],
+        )
 
 
 def transform(flat, column_vars, table_ref, phase_ref, first_wave):
@@ -169,31 +199,24 @@
     return jnp.concatenate([real, imag], axis=0)
 
 
-def main_kernel(blocks, block, index_of, *refs):
+def main_kernel(blocks, block, early, index_of, *refs):
     coriolis_ref, mix_ref, table_ref, phase_ref, tend_ref = refs[:5]
-    traj_refs = refs[5 : 5 + blocks]
-    flat_ref = refs[5 + blocks]
-    out_refs = refs[6 + blocks : -1]
-    grid_ref = refs[-1]
+    before, refs = refs[5 : 5 + (early > 0)], refs[5 + (early > 0) :]
+    late = blocks - early
+    flat_ref = refs[late]
+    out_refs = refs[late + 1 : -1]
     column_vars = tend_ref.shape[0]
-    coriolis = coriolis_ref[:, :1]
-    mix = mix_ref[...]
-    for i, index in enumerate(index_of()):
-        start = pl.multiple_of(index * block, LANES)
-        traj = traj_refs[i][...].astype(jnp.float32)
-        tend = tend_ref[:, pl.ds(start, block)].astype(jnp.float32)
-        stacked = jnp.concatenate([traj, tend, tend * traj], axis=0).astype(jnp.bfloat16)
-        mixed = jnp.dot(mix, stacked, preferred_element_type=jnp.float32)
-        total = mixed[column_vars:] + tend * mixed[:column_vars]
-        grid_ref[pl.ds(i * column_vars, column_vars), :] = jnp.concatenate(
-            [
-                total[:LEVELS] - coriolis * tend[LEVELS : 2 * LEVELS],
-                total[LEVELS : 2 * LEVELS] + coriolis * tend[:LEVELS],
-                total[2 * LEVELS :],
-            ],
-            axis=0,
-        )
-    flat = grid_ref[...].astype(jnp.bfloat16)
+    column_step(
+        block,
+        index_of()[early:],
+        mix_ref[...],
+        coriolis_ref[:, :1],
+        tend_ref,
+        refs[:late],
+        refs[-1],
+    )
+    flat = jnp.concatenate([ref[...] for ref in before] + [refs[-1][...]], axis=0)
+    flat = flat.astype(jnp.bfloat16)
     flat_ref[...] = flat
     both = transform(flat, column_vars, table_ref, phase_ref, 0)
     share = out_refs[0].shape[1]
@@ -253,7 +276,8 @@
 
     direct = own % LANES == 0 and cols > 1 and cols & (cols - 1) == 0
     across = cols // 2
-    swaps = [2, 3, 5, 4, 7, 1, 6] if cols == 8 else list(range(1, cols))
+    swaps = [1, across]
+    late_swaps = [2, 3, 5, 7, 6] if cols == 8 else [q for q in range(2, cols) if q != across]
     far = -(-(waves_total - share) // LANES) * LANES
     near = waves_total - (waves_total - share) // LANES * LANES
     blocks = cols if direct else 8
@@ -264,26 +288,47 @@
         if not direct:
             return list(range(blocks))
         my_col = lax.axis_index("col")
-        return [my_col] + [my_col ^ swap for swap in swaps]
+        return [my_col] + [my_col ^ swap for swap in [*swaps, *late_swaps]]
+
+    if direct:
+        swapped = lambda x, swap: lax.ppermute(x, "col", [(i, i ^ swap) for i in range(cols)])
+        moved = {across: swapped(traj, across)}
+        for swap in swaps:
+            if swap != across:
+                moved[swap] = swapped(traj, swap)
+        first = [moved[swap] for swap in swaps]
+        pieces = [
+            swapped(moved[across], swap ^ across)
+            if across < swap < cols - 1
+            else swapped(traj, swap)
+            for swap in late_swaps
+        ]
+        early = 1 + len(first)
+    else:
+        whole = lax.all_gather(traj, "col", axis=1, tiled=True)
+        first = []
+        pieces = [whole[:, i * block : (i + 1) * block] for i in range(8)]
+        early = 0
 
     operands = [wave_order, coupling, tend, traj]
-    far_table, own_table, phase, mix, kept, own_piece, coriolis = pl.pallas_call(
-        functools.partial(tables_kernel, blocks, block, held, index_of),
+    far_table, own_table, phase, mix, kept, coriolis, *before = pl.pallas_call(
+        functools.partial(tables_kernel, blocks, block, early, held, index_of),
         out_shape=[
             jax.ShapeDtypeStruct((block, 2 * far), jnp.bfloat16),
             jax.ShapeDtypeStruct((block, 2 * near), jnp.bfloat16),
             jax.ShapeDtypeStruct((2, blocks, waves_total), jnp.float32),
             jax.ShapeDtypeStruct((2 * column_vars, 3 * column_vars), jnp.bfloat16),
             jax.ShapeDtypeStruct((column_vars, width), jnp.bfloat16),
-            jax.ShapeDtypeStruct((column_vars, own), jnp.bfloat16),
             jax.ShapeDtypeStruct((1, LANES), jnp.float32),
-        ],
-        in_specs=[SMEM_SPEC] + [HBM_SPEC] * len(operands),
-        out_specs=[VMEM_SPEC] * 7,
+        ]
+        + [jax.ShapeDtypeStruct((early * column_vars, block), jnp.float32)] * (early > 0),
+        in_specs=[SMEM_SPEC] + [HBM_SPEC] * len(operands) + [VMEM_SPEC] * len(first),
+        out_specs=[VMEM_SPEC] * (6 + (early > 0)),
         scratch_shapes=[
             pltpu.VMEM((waves_total,), jnp.int32),
             pltpu.VMEM((column_vars, column_vars), jnp.bfloat16),
             pltpu.VMEM((column_vars, width), jnp.bfloat16),
+            pltpu.VMEM((column_vars, own), jnp.bfloat16),
             pltpu.SemaphoreType.DMA((len(operands),)),
         ],
         compiler_params=pltpu.CompilerParams(vmem_limit_bytes=16 * 1024 * 1024),
@@ -291,30 +336,16 @@
             flops=1024 * column_vars * width, bytes_accessed=4 * column_vars * width, transcendentals=0
         ),
         name="tables",
-    )(row_lat, *[pltpu.with_memory_space_constraint(x, pltpu.HBM) for x in operands])
-
-    if direct:
-        swapped = lambda x, swap: lax.ppermute(x, "col", [(i, i ^ swap) for i in range(cols)])
-        moved = {across: swapped(traj, across)}
-        for swap in swaps:
-            if across < swap < cols - 1:
-                moved[swap] = swapped(moved[across], swap ^ across)
-            elif swap != across:
-                moved[swap] = swapped(traj, swap)
-        arrived = [moved[swap] for swap in swaps]
-    else:
-        whole = lax.all_gather(traj, "col", axis=1, tiled=True)
-        arrived = [whole[:, i * block : (i + 1) * block] for i in range(8)]
-
-    pieces = [own_piece] + arrived if direct else arrived
+    )(row_lat, *[pltpu.with_memory_space_constraint(x, pltpu.HBM) for x in operands], *first)
+
     spectra = jax.ShapeDtypeStruct((2 * column_vars, share), jnp.bfloat16)
     flat, *parts = pl.pallas_call(
-        functools.partial(main_kernel, blocks, block, index_of),
+        functools.partial(main_kernel, blocks, block, early, index_of),
         out_shape=[jax.ShapeDtypeStruct((blocks * column_vars, block), jnp.bfloat16)]
         + [spectra] * (bands - 1),
-        in_specs=[VMEM_SPEC] * (5 + blocks),
+        in_specs=[VMEM_SPEC] * (5 + len(before) + len(pieces)),
         out_specs=[VMEM_SPEC] * bands,
-        scratch_shapes=[pltpu.VMEM((blocks * column_vars, block), jnp.float32)],
+        scratch_shapes=[pltpu.VMEM(((blocks - early) * column_vars, block), jnp.float32)],
         compiler_params=pltpu.CompilerParams(vmem_limit_bytes=24 * 1024 * 1024),
         cost_estimate=pl.CostEstimate(
             flops=4 * column_vars * width * (waves_total - share),
@@ -322,7 +353,7 @@
             transcendentals=0,
         ),
         name="column_and_waves",
-    )(coriolis, mix, far_table, phase, kept, *pieces)
+    )(coriolis, mix, far_table, phase, kept, *before, *pieces)
     ready = []
     for step, part in zip(held, parts):
         pairs = [(i, partner(i, step, bands)) for i in range(bands)]

time: 20.8 us -> 20.6 us (level)
  waiting for transfers between devices: 2.65 us -> 2.38 us
    ppermute x7, waiting for transfers between devices: 0.62 us -> 0.37 us  [body(): lax.ppermute(x, 'col', [(i, i ^ swap) for i in range(cols)])]
  transfers between devices with their start and end apart: 10 -> 10, of which waited for: 4 -> 4; matrix products, arithmetic and copies ran while one was open for 0% -> 0% of each run, Pallas kernels for 13% -> 14%
where the time goes in v5:
time: 20.6 us; the launch traced here: 20.4 us
  starting transfers between devices  12.5 us (61%)
  Pallas kernels  4.78 us (23%)
  waiting for transfers between devices  2.38 us (12%)
  between operations  0.71 us (3%)
    ppermute x7, starting transfers between devices, body(): lax.ppermute(x, 'col', [(i, i ^ swap) for i in range(cols)])  10.6 us
    pallas_call x1, Pallas kernels, body(): pl.pallas_call(functools.partial(tables_kernel, blocks, block, early, hel...  2.34 us
    ppermute x3, waiting for transfers between devices, body(): ready.append(lax.ppermute(part, 'band', pairs))  2.01 us
    ppermute x3, starting transfers between devices, body(): ready.append(lax.ppermute(part, 'band', pairs))  1.92 us
    pallas_call x1, Pallas kernels, body(): pl.pallas_call(functools.partial(main_kernel, blocks, block, early, index...  1.07 us
    pallas_call x1, Pallas kernels, body(): pl.pallas_call(functools.partial(place_kernel, held), out_shape=jax.Shape...  0.88 us
    pallas_call x1, Pallas kernels, body(): pl.pallas_call(own_kernel, out_shape=spectra, in_specs=[VMEM_SPEC] * 3, o...  0.49 us
  transfers between devices with their start and end apart: 10, of which 4 were waited for; matrix products, arithmetic and copies ran while one was open for 0% of the time, Pallas kernels for 14%

profile of v5, /device:TPU:0, one launch (start us, length us, event | category | flops | bytes accessed | tf_op | source)
XLA Modules:
  0.0 20.4 jit_solution(16162384018016622021)
XLA Ops:
  0.0 4.0 %collective-permute-start.1 = (bf16[40,640]{1,0:T(8,128)(2,1)}, bf16[40,640]{1,0:T(8,128)(2,1)S(1)}, u32[]{:S(2)}, u32[]{:S(2)}) collective-permute-start(bf16[40,640]{1,0:T(8,128)(2,1)} %bitcast.3), channel_id=1, source_target_pairs={{0,4},{1,5},{2,6},{3,7},{4,0},{5,1},{6,2},{7,3},{8,12},{9,13},{10,... | collective-permute-start | bytes 153608 | tf_op jit(solution)/shard_map/ppermute | solution.py:294
  4.0 1.5 %collective-permute-start = (bf16[40,640]{1,0:T(8,128)(2,1)}, bf16[40,640]{1,0:T(8,128)(2,1)S(1)}, u32[]{:S(2)}, u32[]{:S(2)}) collective-permute-start(bf16[40,640]{1,0:T(8,128)(2,1)} %bitcast.4), channel_id=1, source_target_pairs={{0,1},{1,0},{2,3},{3,2},{4,5},{5,4},{6,7},{7,6},{8,9},{9,8},{10,11... | collective-permute-start | bytes 153608 | tf_op jit(solution)/shard_map/ppermute | solution.py:294
  5.6 1.3 %collective-permute-start.5 = (bf16[40,640]{1,0:T(8,128)(2,1)}, bf16[40,640]{1,0:T(8,128)(2,1)S(1)}, u32[]{:S(2)}, u32[]{:S(2)}) collective-permute-start(bf16[40,640]{1,0:T(8,128)(2,1)} %bitcast.5), channel_id=1, source_target_pairs={{0,7},{1,6},{2,5},{3,4},{4,3},{5,2},{6,1},{7,0},{8,15},{9,14},{10,... | collective-permute-start | bytes 153608 | tf_op jit(solution)/shard_map/ppermute | solution.py:294
  6.8 0.5 %collective-permute-start.3 = (bf16[40,640]{1,0:T(8,128)(2,1)}, bf16[40,640]{1,0:T(8,128)(2,1)S(1)}, u32[]{:S(2)}, u32[]{:S(2)}) collective-permute-start(bf16[40,640]{1,0:T(8,128)(2,1)} %bitcast.6), channel_id=1, source_target_pairs={{0,3},{1,2},{2,1},{3,0},{4,7},{5,6},{6,5},{7,4},{8,11},{9,10},{10,... | collective-permute-start | bytes 153608 | tf_op jit(solution)/shard_map/ppermute | solution.py:294
  7.4 2.5 %collective-permute-start.2 = (bf16[40,640]{1,0:T(8,128)(2,1)}, bf16[40,640]{1,0:T(8,128)(2,1)S(1)}, u32[]{:S(2)}, u32[]{:S(2)}) collective-permute-start(bf16[40,640]{1,0:T(8,128)(2,1)} %bitcast.7), channel_id=1, source_target_pairs={{0,2},{1,3},{2,0},{3,1},{4,6},{5,7},{6,4},{7,5},{8,10},{9,11},{10,... | collective-permute-start | bytes 153608 | tf_op jit(solution)/shard_map/ppermute | solution.py:294
  9.8 0.0 collective-permute-done.1.refs_1_
  9.8 0.0 collective-permute-start.6
  9.9 0.0 collective-permute-done.refs_0_
  9.9 0.8 %collective-permute-start.4 = (bf16[40,640]{1,0:T(8,128)(2,1)S(1)}, bf16[40,640]{1,0:T(8,128)(2,1)S(1)}, u32[]{:S(2)}, u32[]{:S(2)}) collective-permute-start(bf16[40,640]{1,0:T(8,128)(2,1)S(1)} %collective-permute-done.1.refs_1_), channel_id=1, source_target_pairs={{0,1},{1,0},{2,3},{3,2},{4,5},{5,4},{6,7},{7,6},{8,9},{9,8},{10,11... | collective-permute-start | bytes 153608 | tf_op jit(solution)/shard_map/ppermute | solution.py:294
  11.3 2.3 %tables.1 = (bf16[640,1280]{1,0:T(8,128)(2,1)S(1)}, bf16[640,512]{1,0:T(8,128)(2,1)S(1)}, f32[2,8,768]{2,1,0:T(8,128)S(1)}, bf16[80,120]{1,0:T(8,128)(2,1)S(1)},...) custom-call(s32[1]{0:T(128)S(6)} %copy.6.lat_ref, s32[768]{0:T(1024)} %waves_hbm.1, ...), custom_call_target="tpu_custom_call" | custom-call | flops 209715200 | bytes 819200 | tf_op jit(solution)/shard_map/tables/pallas_call | solution.py:314
  13.6 0.0 collective-permute-done.5.refs_9_
  13.6 0.0 collective-permute-done.3.refs_7_
  13.7 0.0 collective-permute-done.2.refs_6_
  13.7 0.3 %collective-permute-done.6.refs_10_ = bf16[40,640]{1,0:T(8,128)(2,1)S(1)} collective-permute-done((bf16[40,640]{1,0:T(8,128)(2,1)S(1)}, bf16[40,640]{1,0:T(8,128)(2,1)S(1)}, u32[]{:S(2)}, u32[]{:S(2)}) %collective-permute-start.6) | collective-permute-done | bytes 51232 | tf_op jit(solution)/shard_map/ppermute | solution.py:294
  13.9 0.1 collective-permute-done.4.refs_8_
  14.0 1.1 %column_and_waves.1 = (bf16[320,640]{1,0:T(8,128)(2,1)S(1)}, bf16[80,192]{1,0:T(8,128)(2,1)S(1)}, bf16[80,192]{1,0:T(8,128)(2,1)S(1)}, bf16[80,192]{1,0:T(8,128)(2,1)S(1)}) custom-call(f32[1,128]{1,0:T(1,128)S(1)} %get-tuple-element.16.refs_0_, bf16[80,120]{1,0:T(8,128)(2,1)S(1)} %get-tuple-element.17.refs_1_, ...), custom_call_target="tpu_custom_call" | custom-call | flops 471859200 | bytes 819200 | tf_op jit(solution)/shard_map/column_and_waves/pallas_call | solution.py:342
  15.1 0.1 collective-permute-start.7
  15.2 1.6 %collective-permute-start.8 = (bf16[80,192]{1,0:T(8,128)(2,1)S(1)}, bf16[80,192]{1,0:T(8,128)(2,1)S(1)}, u32[]{:S(2)}, u32[]{:S(2)}) collective-permute-start(bf16[80,192]{1,0:T(8,128)(2,1)S(1)} %get-tuple-element.23), channel_id=1, source_target_pairs={{0,16},{8,24},{16,0},{24,8},{1,17},{9,25},{17,1},{25,9},{2,18},{10... | collective-permute-start | bytes 92168 | tf_op jit(solution)/shard_map/ppermute | solution.py:360
  16.7 0.3 %collective-permute-start.9 = (bf16[80,192]{1,0:T(8,128)(2,1)S(1)}, bf16[80,192]{1,0:T(8,128)(2,1)S(1)}, u32[]{:S(2)}, u32[]{:S(2)}) collective-permute-start(bf16[80,192]{1,0:T(8,128)(2,1)S(1)} %get-tuple-element.24), channel_id=1, source_target_pairs={{0,8},{8,0},{16,24},{24,16},{1,9},{9,1},{17,25},{25,17},{2,10},{10... | collective-permute-start | bytes 92168 | tf_op jit(solution)/shard_map/ppermute | solution.py:360
  17.0 0.5 %own_waves.1.refs_3_ = bf16[80,192]{1,0:T(8,128)(2,1)S(1)} custom-call(bf16[320,640]{1,0:T(8,128)(2,1)S(1)} %get-tuple-element.25.flat_ref, bf16[640,512]{1,0:T(8,128)(2,1)S(1)} %get-tuple-element.26.table_ref, f32[2,8,768]{2,1,0:T(8,128)S(1)} %get-tuple-element.19.refs_3_.phase_ref), custom_call_target="tpu_custom_call" | custom-call | flops 157286400 | bytes 819200 | tf_op jit(solution)/shard_map/own_waves/pallas_call | solution.py:362
  17.5 1.4 %collective-permute-done.7.refs_0_ = bf16[80,192]{1,0:T(8,128)(2,1)S(1)} collective-permute-done((bf16[80,192]{1,0:T(8,128)(2,1)S(1)}, bf16[80,192]{1,0:T(8,128)(2,1)S(1)}, u32[]{:S(2)}, u32[]{:S(2)}) %collective-permute-start.7) | collective-permute-done | bytes 30752 | tf_op jit(solution)/shard_map/ppermute | solution.py:360
  19.0 0.6 %collective-permute-done.8.refs_1_ = bf16[80,192]{1,0:T(8,128)(2,1)S(1)} collective-permute-done((bf16[80,192]{1,0:T(8,128)(2,1)S(1)}, bf16[80,192]{1,0:T(8,128)(2,1)S(1)}, u32[]{:S(2)}, u32[]{:S(2)}) %collective-permute-start.8) | collective-permute-done | bytes 30752 | tf_op jit(solution)/shard_map/ppermute | solution.py:360
  19.5 0.0 collective-permute-done.9.refs_2_
  19.5 0.9 %row_slots.1 = bf16[1,2,40,4,192]{4,3,2,1,0:T(4,128)(2,1)} custom-call(bf16[80,192]{1,0:T(8,128)(2,1)S(1)} %collective-permute-done.7.refs_0_, bf16[80,192]{1,0:T(8,128)(2,1)S(1)} %collective-permute-done.8.refs_1_, bf16[80,192]{1,0:T(8,128)(2,1)S(1)} %collective-permute-done.9.refs_2_, bf16[80,192]{1,0:T(8,128)(2,1)S(1)} %own_waves.1.refs_3_), custom_call_target="tpu_custom_call" | custom-call | tf_op jit(solution)/shard_map/row_slots/pallas_call | solution.py:376
Async XLA Ops:
  0.0 9.8 %collective-permute-start.1 = (bf16[40,640]{1,0:T(8,128)(2,1)}, bf16[40,640]{1,0:T(8,128)(2,1)S(1)}, u32[]{:S(2)}, u32[]{:S(2)}) collective-permute-start(bf16[40,640]{1,0:T(8,128)(2,1)} %bitcast.3), channel_id=1, source_target_pairs={{0,4},{1,5},{2,6},{3,7},{4,0},{5,1},{6,2},{7,3},{8,12},{9,13},{10,... | collective-permute-start | bytes 153608 | tf_op jit(solution)/shard_map/ppermute | solution.py:294
  4.0 5.8 %collective-permute-start = (bf16[40,640]{1,0:T(8,128)(2,1)}, bf16[40,640]{1,0:T(8,128)(2,1)S(1)}, u32[]{:S(2)}, u32[]{:S(2)}) collective-permute-start(bf16[40,640]{1,0:T(8,128)(2,1)} %bitcast.4), channel_id=1, source_target_pairs={{0,1},{1,0},{2,3},{3,2},{4,5},{5,4},{6,7},{7,6},{8,9},{9,8},{10,11... | collective-permute-start | bytes 153608 | tf_op jit(solution)/shard_map/ppermute | solution.py:294
  5.6 8.1 %collective-permute-start.5 = (bf16[40,640]{1,0:T(8,128)(2,1)}, bf16[40,640]{1,0:T(8,128)(2,1)S(1)}, u32[]{:S(2)}, u32[]{:S(2)}) collective-permute-start(bf16[40,640]{1,0:T(8,128)(2,1)} %bitcast.5), channel_id=1, source_target_pairs={{0,7},{1,6},{2,5},{3,4},{4,3},{5,2},{6,1},{7,0},{8,15},{9,14},{10,... | collective-permute-start | bytes 153608 | tf_op jit(solution)/shard_map/ppermute | solution.py:294
  6.8 6.8 %collective-permute-start.3 = (bf16[40,640]{1,0:T(8,128)(2,1)}, bf16[40,640]{1,0:T(8,128)(2,1)S(1)}, u32[]{:S(2)}, u32[]{:S(2)}) collective-permute-start(bf16[40,640]{1,0:T(8,128)(2,1)} %bitcast.6), channel_id=1, source_target_pairs={{0,3},{1,2},{2,1},{3,0},{4,7},{5,6},{6,5},{7,4},{8,11},{9,10},{10,... | collective-permute-start | bytes 153608 | tf_op jit(solution)/shard_map/ppermute | solution.py:294
  7.4 6.3 %collective-permute-start.2 = (bf16[40,640]{1,0:T(8,128)(2,1)}, bf16[40,640]{1,0:T(8,128)(2,1)S(1)}, u32[]{:S(2)}, u32[]{:S(2)}) collective-permute-start(bf16[40,640]{1,0:T(8,128)(2,1)} %bitcast.7), channel_id=1, source_target_pairs={{0,2},{1,3},{2,0},{3,1},{4,6},{5,7},{6,4},{7,5},{8,10},{9,11},{10,... | collective-permute-start | bytes 153608 | tf_op jit(solution)/shard_map/ppermute | solution.py:294
  9.8 4.1 %collective-permute-start.6 = (bf16[40,640]{1,0:T(8,128)(2,1)S(1)}, bf16[40,640]{1,0:T(8,128)(2,1)S(1)}, u32[]{:S(2)}, u32[]{:S(2)}) collective-permute-start(bf16[40,640]{1,0:T(8,128)(2,1)S(1)} %collective-permute-done.1.refs_1_), channel_id=1, source_target_pairs={{0,2},{1,3},{2,0},{3,1},{4,6},{5,7},{6,4},{7,5},{8,10},{9,11},{10,... | collective-permute-start | bytes 153608 | tf_op jit(solution)/shard_map/ppermute | solution.py:294
  9.9 4.2 %collective-permute-start.4 = (bf16[40,640]{1,0:T(8,128)(2,1)S(1)}, bf16[40,640]{1,0:T(8,128)(2,1)S(1)}, u32[]{:S(2)}, u32[]{:S(2)}) collective-permute-start(bf16[40,640]{1,0:T(8,128)(2,1)S(1)} %collective-permute-done.1.refs_1_), channel_id=1, source_target_pairs={{0,1},{1,0},{2,3},{3,2},{4,5},{5,4},{6,7},{7,6},{8,9},{9,8},{10,11... | collective-permute-start | bytes 153608 | tf_op jit(solution)/shard_map/ppermute | solution.py:294
  15.1 3.9 %collective-permute-start.7 = (bf16[80,192]{1,0:T(8,128)(2,1)S(1)}, bf16[80,192]{1,0:T(8,128)(2,1)S(1)}, u32[]{:S(2)}, u32[]{:S(2)}) collective-permute-start(bf16[80,192]{1,0:T(8,128)(2,1)S(1)} %get-tuple-element.22), channel_id=1, source_target_pairs={{0,24},{8,16},{16,8},{24,0},{1,25},{9,17},{17,9},{25,1},{2,26},{10... | collective-permute-start | bytes 92168 | tf_op jit(solution)/shard_map/ppermute | solution.py:360
  15.2 4.4 %collective-permute-start.8 = (bf16[80,192]{1,0:T(8,128)(2,1)S(1)}, bf16[80,192]{1,0:T(8,128)(2,1)S(1)}, u32[]{:S(2)}, u32[]{:S(2)}) collective-permute-start(bf16[80,192]{1,0:T(8,128)(2,1)S(1)} %get-tuple-element.23), channel_id=1, source_target_pairs={{0,16},{8,24},{16,0},{24,8},{1,17},{9,25},{17,1},{25,9},{2,18},{10... | collective-permute-start | bytes 92168 | tf_op jit(solution)/shard_map/ppermute | solution.py:360
  16.7 2.8 %collective-permute-start.9 = (bf16[80,192]{1,0:T(8,128)(2,1)S(1)}, bf16[80,192]{1,0:T(8,128)(2,1)S(1)}, u32[]{:S(2)}, u32[]{:S(2)}) collective-permute-start(bf16[80,192]{1,0:T(8,128)(2,1)S(1)} %get-tuple-element.24), channel_id=1, source_target_pairs={{0,8},{8,0},{16,24},{24,16},{1,9},{9,1},{17,25},{25,17},{2,10},{10... | collective-permute-start | bytes 92168 | tf_op jit(solution)/shard_map/ppermute | solution.py:360

commit v6 on v5

--- a/solution.py
+++ b/solution.py
@@ -224,7 +224,7 @@
         out_ref[...] = both[:, k * share : (k + 1) * share].astype(jnp.bfloat16)
 
 
-def own_kernel(flat_ref, table_ref, phase_ref, out_ref):
+def own_kernel(held, flat_ref, table_ref, phase_ref, out_ref, choose_ref):
     near = table_ref.shape[1] // 2
     column_vars, share = out_ref.shape[0] // 2, out_ref.shape[1]
     both = transform(
@@ -232,14 +232,8 @@
     )
     out_ref[...] = both[:, near - share :].astype(jnp.bfloat16)
 
-
-def place_kernel(held, *refs):
     parts = len(held)
-    in_refs = refs[:parts]
-    out_ref = refs[parts]
-    column_vars = out_ref.shape[2]
-    share = out_ref.shape[4]
-    total = parts * column_vars
+    total = choose_ref.shape[0]
     row = lax.broadcasted_iota(jnp.int32, (total, 1), 0)
     variable = jnp.floor((row.astype(jnp.float32) + 0.5) * (1.0 / parts)).astype(jnp.int32)
     slot = row - variable * parts
@@ -251,7 +245,15 @@
     target = variable
     for position, which in enumerate(held):
         target = jnp.where(step == which, target + position * column_vars, target)
-    choose = (target == lax.broadcasted_iota(jnp.int32, (total, total), 1)).astype(jnp.bfloat16)
+    choose_ref[...] = (target == lax.broadcasted_iota(jnp.int32, (total, total), 1)).astype(
+        jnp.bfloat16
+    )
+
+
+def place_kernel(choose_ref, *refs):
+    in_refs, out_ref = refs[:-1], refs[-1]
+    _, _, column_vars, parts, share = out_ref.shape
+    choose = choose_ref[...]
     wide = [ref[...].astype(jnp.float32) for ref in in_refs]
     for half in range(2):
         rows = slice(half * column_vars, (half + 1) * column_vars)
@@ -274,7 +276,7 @@
     tend = adjoint_tend.reshape(column_vars, width)
     traj = trajectory.reshape(column_vars, own)
 
-    direct = own % LANES == 0 and cols > 1 and cols & (cols - 1) == 0
+    direct = own % LANES == 0 and cols > 2 and cols & (cols - 1) == 0
     across = cols // 2
     swaps = [1, across]
     late_swaps = [2, 3, 5, 7, 6] if cols == 8 else [q for q in range(2, cols) if q != across]
@@ -358,29 +360,28 @@
     for step, part in zip(held, parts):
         pairs = [(i, partner(i, step, bands)) for i in range(bands)]
         ready.append(lax.ppermute(part, "band", pairs))
-    ready.append(
-        pl.pallas_call(
-            own_kernel,
-            out_shape=spectra,
-            in_specs=[VMEM_SPEC] * 3,
-            out_specs=VMEM_SPEC,
-            compiler_params=pltpu.CompilerParams(vmem_limit_bytes=24 * 1024 * 1024),
-            cost_estimate=pl.CostEstimate(
-                flops=4 * column_vars * width * share,
-                bytes_accessed=4 * column_vars * width,
-                transcendentals=0,
-            ),
-            name="own_waves",
-        )(flat, own_table, phase)
-    )
+    total = bands * column_vars
+    own_part, choose = pl.pallas_call(
+        functools.partial(own_kernel, held),
+        out_shape=[spectra, jax.ShapeDtypeStruct((total, total), jnp.bfloat16)],
+        in_specs=[VMEM_SPEC] * 3,
+        out_specs=[VMEM_SPEC] * 2,
+        compiler_params=pltpu.CompilerParams(vmem_limit_bytes=24 * 1024 * 1024),
+        cost_estimate=pl.CostEstimate(
+            flops=4 * column_vars * width * share,
+            bytes_accessed=4 * column_vars * width,
+            transcendentals=0,
+        ),
+        name="own_waves",
+    )(flat, own_table, phase)
     return pl.pallas_call(
-        functools.partial(place_kernel, held),
+        place_kernel,
         out_shape=jax.ShapeDtypeStruct((1, 2, column_vars, bands, share), jnp.bfloat16),
-        in_specs=[VMEM_SPEC] * bands,
+        in_specs=[VMEM_SPEC] * (1 + bands),
         out_specs=VMEM_SPEC,
         compiler_params=pltpu.CompilerParams(vmem_limit_bytes=16 * 1024 * 1024),
         name="row_slots",
-    )(*ready)
+    )(choose, *ready, own_part)
 
 
 def solution(mesh):

time: 20.6 us -> 20.6 us (level)
  no operation moved by 1% of the time
where the time goes in v6:
time: 20.6 us; the launch traced here: 20.4 us
  starting transfers between devices  12.5 us (61%)
  Pallas kernels  4.77 us (23%)
  waiting for transfers between devices  2.38 us (12%)
  between operations  0.71 us (3%)
    ppermute x7, starting transfers between devices, body(): lax.ppermute(x, 'col', [(i, i ^ swap) for i in range(cols)])  10.6 us
    pallas_call x1, Pallas kernels, body(): pl.pallas_call(functools.partial(tables_kernel, blocks, block, early, hel...  2.34 us
    ppermute x3, waiting for transfers between devices, body(): ready.append(lax.ppermute(part, 'band', pairs))  2.01 us
    ppermute x3, starting transfers between devices, body(): ready.append(lax.ppermute(part, 'band', pairs))  1.92 us
    pallas_call x1, Pallas kernels, body(): pl.pallas_call(functools.partial(main_kernel, blocks, block, early, index...  1.07 us
    pallas_call x1, Pallas kernels, body(): pl.pallas_call(place_kernel, out_shape=jax.ShapeDtypeStruct((1, 2, column...  0.87 us
    pallas_call x1, Pallas kernels, body(): pl.pallas_call(functools.partial(own_kernel, held), out_shape=[spectra, j...  0.49 us
  transfers between devices with their start and end apart: 10, of which 4 were waited for; matrix products, arithmetic and copies ran while one was open for 0% of the time, Pallas kernels for 14%

profile of v6, /device:TPU:0, one launch (start us, length us, event | category | flops | bytes accessed | tf_op | source)
XLA Modules:
  0.0 20.4 jit_solution(9850464365758773459)
XLA Ops:
  0.0 4.0 %collective-permute-start.1 = (bf16[40,640]{1,0:T(8,128)(2,1)}, bf16[40,640]{1,0:T(8,128)(2,1)S(1)}, u32[]{:S(2)}, u32[]{:S(2)}) collective-permute-start(bf16[40,640]{1,0:T(8,128)(2,1)} %bitcast.3), channel_id=1, source_target_pairs={{0,4},{1,5},{2,6},{3,7},{4,0},{5,1},{6,2},{7,3},{8,12},{9,13},{10,... | collective-permute-start | bytes 153608 | tf_op jit(solution)/shard_map/ppermute | solution.py:296
  4.0 1.5 %collective-permute-start = (bf16[40,640]{1,0:T(8,128)(2,1)}, bf16[40,640]{1,0:T(8,128)(2,1)S(1)}, u32[]{:S(2)}, u32[]{:S(2)}) collective-permute-start(bf16[40,640]{1,0:T(8,128)(2,1)} %bitcast.4), channel_id=1, source_target_pairs={{0,1},{1,0},{2,3},{3,2},{4,5},{5,4},{6,7},{7,6},{8,9},{9,8},{10,11... | collective-permute-start | bytes 153608 | tf_op jit(solution)/shard_map/ppermute | solution.py:296
  5.6 1.3 %collective-permute-start.5 = (bf16[40,640]{1,0:T(8,128)(2,1)}, bf16[40,640]{1,0:T(8,128)(2,1)S(1)}, u32[]{:S(2)}, u32[]{:S(2)}) collective-permute-start(bf16[40,640]{1,0:T(8,128)(2,1)} %bitcast.5), channel_id=1, source_target_pairs={{0,7},{1,6},{2,5},{3,4},{4,3},{5,2},{6,1},{7,0},{8,15},{9,14},{10,... | collective-permute-start | bytes 153608 | tf_op jit(solution)/shard_map/ppermute | solution.py:296
  6.8 0.5 %collective-permute-start.3 = (bf16[40,640]{1,0:T(8,128)(2,1)}, bf16[40,640]{1,0:T(8,128)(2,1)S(1)}, u32[]{:S(2)}, u32[]{:S(2)}) collective-permute-start(bf16[40,640]{1,0:T(8,128)(2,1)} %bitcast.6), channel_id=1, source_target_pairs={{0,3},{1,2},{2,1},{3,0},{4,7},{5,6},{6,5},{7,4},{8,11},{9,10},{10,... | collective-permute-start | bytes 153608 | tf_op jit(solution)/shard_map/ppermute | solution.py:296
  7.4 2.5 %collective-permute-start.2 = (bf16[40,640]{1,0:T(8,128)(2,1)}, bf16[40,640]{1,0:T(8,128)(2,1)S(1)}, u32[]{:S(2)}, u32[]{:S(2)}) collective-permute-start(bf16[40,640]{1,0:T(8,128)(2,1)} %bitcast.7), channel_id=1, source_target_pairs={{0,2},{1,3},{2,0},{3,1},{4,6},{5,7},{6,4},{7,5},{8,10},{9,11},{10,... | collective-permute-start | bytes 153608 | tf_op jit(solution)/shard_map/ppermute | solution.py:296
  9.8 0.0 collective-permute-done.1.refs_1_
  9.8 0.0 collective-permute-start.6
  9.9 0.0 collective-permute-done.refs_0_
  9.9 0.8 %collective-permute-start.4 = (bf16[40,640]{1,0:T(8,128)(2,1)S(1)}, bf16[40,640]{1,0:T(8,128)(2,1)S(1)}, u32[]{:S(2)}, u32[]{:S(2)}) collective-permute-start(bf16[40,640]{1,0:T(8,128)(2,1)S(1)} %collective-permute-done.1.refs_1_), channel_id=1, source_target_pairs={{0,1},{1,0},{2,3},{3,2},{4,5},{5,4},{6,7},{7,6},{8,9},{9,8},{10,11... | collective-permute-start | bytes 153608 | tf_op jit(solution)/shard_map/ppermute | solution.py:296
  11.3 2.3 %tables.1 = (bf16[640,1280]{1,0:T(8,128)(2,1)S(1)}, bf16[640,512]{1,0:T(8,128)(2,1)S(1)}, f32[2,8,768]{2,1,0:T(8,128)S(1)}, bf16[80,120]{1,0:T(8,128)(2,1)S(1)},...) custom-call(s32[1]{0:T(128)S(6)} %copy.6.lat_ref, s32[768]{0:T(1024)} %waves_hbm.1, ...), custom_call_target="tpu_custom_call" | custom-call | flops 209715200 | bytes 819200 | tf_op jit(solution)/shard_map/tables/pallas_call | solution.py:316
  13.6 0.0 collective-permute-done.5.refs_9_
  13.6 0.0 collective-permute-done.3.refs_7_
  13.7 0.0 collective-permute-done.2.refs_6_
  13.7 0.3 %collective-permute-done.6.refs_10_ = bf16[40,640]{1,0:T(8,128)(2,1)S(1)} collective-permute-done((bf16[40,640]{1,0:T(8,128)(2,1)S(1)}, bf16[40,640]{1,0:T(8,128)(2,1)S(1)}, u32[]{:S(2)}, u32[]{:S(2)}) %collective-permute-start.6) | collective-permute-done | bytes 51232 | tf_op jit(solution)/shard_map/ppermute | solution.py:296
  13.9 0.1 collective-permute-done.4.refs_8_
  14.0 1.1 %column_and_waves.1 = (bf16[320,640]{1,0:T(8,128)(2,1)S(1)}, bf16[80,192]{1,0:T(8,128)(2,1)S(1)}, bf16[80,192]{1,0:T(8,128)(2,1)S(1)}, bf16[80,192]{1,0:T(8,128)(2,1)S(1)}) custom-call(f32[1,128]{1,0:T(1,128)S(1)} %get-tuple-element.18.refs_0_, bf16[80,120]{1,0:T(8,128)(2,1)S(1)} %get-tuple-element.19.refs_1_, ...), custom_call_target="tpu_custom_call" | custom-call | flops 471859200 | bytes 819200 | tf_op jit(solution)/shard_map/column_and_waves/pallas_call | solution.py:344
  15.1 0.1 collective-permute-start.7
  15.2 1.6 %collective-permute-start.8 = (bf16[80,192]{1,0:T(8,128)(2,1)S(1)}, bf16[80,192]{1,0:T(8,128)(2,1)S(1)}, u32[]{:S(2)}, u32[]{:S(2)}) collective-permute-start(bf16[80,192]{1,0:T(8,128)(2,1)S(1)} %get-tuple-element.28), channel_id=1, source_target_pairs={{0,16},{8,24},{16,0},{24,8},{1,17},{9,25},{17,1},{25,9},{2,18},{10... | collective-permute-start | bytes 92168 | tf_op jit(solution)/shard_map/ppermute | solution.py:362
  16.7 0.3 %collective-permute-start.9 = (bf16[80,192]{1,0:T(8,128)(2,1)S(1)}, bf16[80,192]{1,0:T(8,128)(2,1)S(1)}, u32[]{:S(2)}, u32[]{:S(2)}) collective-permute-start(bf16[80,192]{1,0:T(8,128)(2,1)S(1)} %get-tuple-element.29), channel_id=1, source_target_pairs={{0,8},{8,0},{16,24},{24,16},{1,9},{9,1},{17,25},{25,17},{2,10},{10... | collective-permute-start | bytes 92168 | tf_op jit(solution)/shard_map/ppermute | solution.py:362
  17.0 0.5 %own_waves.1 = (bf16[80,192]{1,0:T(8,128)(2,1)S(1)}, bf16[160,160]{1,0:T(8,128)(2,1)S(1)}) custom-call(bf16[320,640]{1,0:T(8,128)(2,1)S(1)} %get-tuple-element.24.flat_ref, bf16[640,512]{1,0:T(8,128)(2,1)S(1)} %get-tuple-element.25.table_ref, f32[2,8,768]{2,1,0:T(8,128)S(1)} %get-tuple-element.21.refs_3_.phase_ref), custom_call_target="tpu_custom_call" | custom-call | flops 157286400 | bytes 819200 | tf_op jit(solution)/shard_map/own_waves/pallas_call | solution.py:364
  17.5 1.4 %collective-permute-done.7.refs_0_ = bf16[80,192]{1,0:T(8,128)(2,1)S(1)} collective-permute-done((bf16[80,192]{1,0:T(8,128)(2,1)S(1)}, bf16[80,192]{1,0:T(8,128)(2,1)S(1)}, u32[]{:S(2)}, u32[]{:S(2)}) %collective-permute-start.7) | collective-permute-done | bytes 30752 | tf_op jit(solution)/shard_map/ppermute | solution.py:362
  19.0 0.6 %collective-permute-done.8.refs_1_ = bf16[80,192]{1,0:T(8,128)(2,1)S(1)} collective-permute-done((bf16[80,192]{1,0:T(8,128)(2,1)S(1)}, bf16[80,192]{1,0:T(8,128)(2,1)S(1)}, u32[]{:S(2)}, u32[]{:S(2)}) %collective-permute-start.8) | collective-permute-done | bytes 30752 | tf_op jit(solution)/shard_map/ppermute | solution.py:362
  19.5 0.0 collective-permute-done.9.refs_2_
  19.5 0.9 %row_slots.1 = bf16[1,2,40,4,192]{4,3,2,1,0:T(4,128)(2,1)} custom-call(bf16[160,160]{1,0:T(8,128)(2,1)S(1)} %get-tuple-element.26.choose_ref, bf16[80,192]{1,0:T(8,128)(2,1)S(1)} %collective-permute-done.7.refs_0_, bf16[80,192]{1,0:T(8,128)(2,1)S(1)} %collective-permute-done.8.refs_1_, bf16[80,192]{1,0:T(8,128)(2,1)S(1)} %collective-permute-done.9.refs_2_, ...), custom_call_target="tpu_custom_call" | custom-call | tf_op jit(solution)/shard_map/row_slots/pallas_call | solution.py:377
Async XLA Ops:
  0.0 9.8 %collective-permute-start.1 = (bf16[40,640]{1,0:T(8,128)(2,1)}, bf16[40,640]{1,0:T(8,128)(2,1)S(1)}, u32[]{:S(2)}, u32[]{:S(2)}) collective-permute-start(bf16[40,640]{1,0:T(8,128)(2,1)} %bitcast.3), channel_id=1, source_target_pairs={{0,4},{1,5},{2,6},{3,7},{4,0},{5,1},{6,2},{7,3},{8,12},{9,13},{10,... | collective-permute-start | bytes 153608 | tf_op jit(solution)/shard_map/ppermute | solution.py:296
  4.0 5.8 %collective-permute-start = (bf16[40,640]{1,0:T(8,128)(2,1)}, bf16[40,640]{1,0:T(8,128)(2,1)S(1)}, u32[]{:S(2)}, u32[]{:S(2)}) collective-permute-start(bf16[40,640]{1,0:T(8,128)(2,1)} %bitcast.4), channel_id=1, source_target_pairs={{0,1},{1,0},{2,3},{3,2},{4,5},{5,4},{6,7},{7,6},{8,9},{9,8},{10,11... | collective-permute-start | bytes 153608 | tf_op jit(solution)/shard_map/ppermute | solution.py:296
  5.6 8.1 %collective-permute-start.5 = (bf16[40,640]{1,0:T(8,128)(2,1)}, bf16[40,640]{1,0:T(8,128)(2,1)S(1)}, u32[]{:S(2)}, u32[]{:S(2)}) collective-permute-start(bf16[40,640]{1,0:T(8,128)(2,1)} %bitcast.5), channel_id=1, source_target_pairs={{0,7},{1,6},{2,5},{3,4},{4,3},{5,2},{6,1},{7,0},{8,15},{9,14},{10,... | collective-permute-start | bytes 153608 | tf_op jit(solution)/shard_map/ppermute | solution.py:296
  6.8 6.8 %collective-permute-start.3 = (bf16[40,640]{1,0:T(8,128)(2,1)}, bf16[40,640]{1,0:T(8,128)(2,1)S(1)}, u32[]{:S(2)}, u32[]{:S(2)}) collective-permute-start(bf16[40,640]{1,0:T(8,128)(2,1)} %bitcast.6), channel_id=1, source_target_pairs={{0,3},{1,2},{2,1},{3,0},{4,7},{5,6},{6,5},{7,4},{8,11},{9,10},{10,... | collective-permute-start | bytes 153608 | tf_op jit(solution)/shard_map/ppermute | solution.py:296
  7.4 6.3 %collective-permute-start.2 = (bf16[40,640]{1,0:T(8,128)(2,1)}, bf16[40,640]{1,0:T(8,128)(2,1)S(1)}, u32[]{:S(2)}, u32[]{:S(2)}) collective-permute-start(bf16[40,640]{1,0:T(8,128)(2,1)} %bitcast.7), channel_id=1, source_target_pairs={{0,2},{1,3},{2,0},{3,1},{4,6},{5,7},{6,4},{7,5},{8,10},{9,11},{10,... | collective-permute-start | bytes 153608 | tf_op jit(solution)/shard_map/ppermute | solution.py:296
  9.8 4.1 %collective-permute-start.6 = (bf16[40,640]{1,0:T(8,128)(2,1)S(1)}, bf16[40,640]{1,0:T(8,128)(2,1)S(1)}, u32[]{:S(2)}, u32[]{:S(2)}) collective-permute-start(bf16[40,640]{1,0:T(8,128)(2,1)S(1)} %collective-permute-done.1.refs_1_), channel_id=1, source_target_pairs={{0,2},{1,3},{2,0},{3,1},{4,6},{5,7},{6,4},{7,5},{8,10},{9,11},{10,... | collective-permute-start | bytes 153608 | tf_op jit(solution)/shard_map/ppermute | solution.py:296
  9.9 4.2 %collective-permute-start.4 = (bf16[40,640]{1,0:T(8,128)(2,1)S(1)}, bf16[40,640]{1,0:T(8,128)(2,1)S(1)}, u32[]{:S(2)}, u32[]{:S(2)}) collective-permute-start(bf16[40,640]{1,0:T(8,128)(2,1)S(1)} %collective-permute-done.1.refs_1_), channel_id=1, source_target_pairs={{0,1},{1,0},{2,3},{3,2},{4,5},{5,4},{6,7},{7,6},{8,9},{9,8},{10,11... | collective-permute-start | bytes 153608 | tf_op jit(solution)/shard_map/ppermute | solution.py:296
  15.1 3.9 %collective-permute-start.7 = (bf16[80,192]{1,0:T(8,128)(2,1)S(1)}, bf16[80,192]{1,0:T(8,128)(2,1)S(1)}, u32[]{:S(2)}, u32[]{:S(2)}) collective-permute-start(bf16[80,192]{1,0:T(8,128)(2,1)S(1)} %get-tuple-element.27), channel_id=1, source_target_pairs={{0,24},{8,16},{16,8},{24,0},{1,25},{9,17},{17,9},{25,1},{2,26},{10... | collective-permute-start | bytes 92168 | tf_op jit(solution)/shard_map/ppermute | solution.py:362
  15.2 4.4 %collective-permute-start.8 = (bf16[80,192]{1,0:T(8,128)(2,1)S(1)}, bf16[80,192]{1,0:T(8,128)(2,1)S(1)}, u32[]{:S(2)}, u32[]{:S(2)}) collective-permute-start(bf16[80,192]{1,0:T(8,128)(2,1)S(1)} %get-tuple-element.28), channel_id=1, source_target_pairs={{0,16},{8,24},{16,0},{24,8},{1,17},{9,25},{17,1},{25,9},{2,18},{10... | collective-permute-start | bytes 92168 | tf_op jit(solution)/shard_map/ppermute | solution.py:362
  16.7 2.8 %collective-permute-start.9 = (bf16[80,192]{1,0:T(8,128)(2,1)S(1)}, bf16[80,192]{1,0:T(8,128)(2,1)S(1)}, u32[]{:S(2)}, u32[]{:S(2)}) collective-permute-start(bf16[80,192]{1,0:T(8,128)(2,1)S(1)} %get-tuple-element.29), channel_id=1, source_target_pairs={{0,8},{8,0},{16,24},{24,16},{1,9},{9,1},{17,25},{25,17},{2,10},{10... | collective-permute-start | bytes 92168 | tf_op jit(solution)/shard_map/ppermute | solution.py:362

commit v7 on v5

--- a/solution.py
+++ b/solution.py
@@ -120,12 +120,14 @@
         rows = pl.ds(row * SUB, SUB)
         table_cos = (here_cos * fine_cos - here_sin * fine_sin).astype(jnp.bfloat16)
         table_sin = (here_cos * fine_sin + here_sin * fine_cos).astype(jnp.bfloat16)
-        far = far_table_ref.shape[1] // 2
-        near = own_table_ref.shape[1] // 2
-        far_table_ref[rows, :far] = table_cos[:, :far]
-        far_table_ref[rows, far:] = table_sin[:, :far]
-        own_table_ref[rows, :near] = table_cos[:, waves_total - near :]
-        own_table_ref[rows, near:] = table_sin[:, waves_total - near :]
+        for ref, skip in [
+            (far_table_ref, 0),
+            (own_table_ref, waves_total - own_table_ref.shape[1] // 2),
+        ]:
+            for i in range(0, ref.shape[1] // 2, LANES):
+                cols = slice(skip + i, skip + i + LANES)
+                ref[rows, 2 * i : 2 * i + LANES] = table_cos[:, cols]
+                ref[rows, 2 * i + LANES : 2 * (i + LANES)] = table_sin[:, cols]
 
     slot = lax.broadcasted_iota(jnp.int32, (blocks, 1), 0)
     first = jnp.zeros((blocks, 1), jnp.int32)
@@ -178,25 +180,25 @@
 
 
 def transform(flat, column_vars, table_ref, phase_ref, first_wave):
-    wide = table_ref.shape[1]
-    waves = wide // 2
-    near = jnp.concatenate(
-        [
-            jnp.dot(flat, table_ref[:, i : min(i + 256, wide)], preferred_element_type=jnp.float32)
-            for i in range(0, wide, 256)
-        ],
-        axis=1,
-    )
-    real = jnp.zeros((column_vars, waves), jnp.float32)
-    imag = jnp.zeros((column_vars, waves), jnp.float32)
-    for i in range(flat.shape[0] // column_vars):
-        rows = slice(i * column_vars, (i + 1) * column_vars)
-        near_cos, near_sin = near[rows, :waves], near[rows, waves:]
-        far_cos = phase_ref[0, i : i + 1, first_wave : first_wave + waves]
-        far_sin = phase_ref[1, i : i + 1, first_wave : first_wave + waves]
-        real = real + (far_cos * near_cos - far_sin * near_sin)
-        imag = imag + (far_cos * near_sin + far_sin * near_cos)
-    return jnp.concatenate([real, imag], axis=0)
+    reals, imags = [], []
+    for i in range(0, table_ref.shape[1] // 2, LANES):
+        near = jnp.dot(
+            flat, table_ref[:, 2 * i : 2 * (i + LANES)], preferred_element_type=jnp.float32
+        )
+        cols = slice(first_wave + i, first_wave + i + LANES)
+        real = jnp.zeros((column_vars, LANES), jnp.float32)
+        imag = jnp.zeros((column_vars, LANES), jnp.float32)
+        for k in range(flat.shape[0] // column_vars):
+            rows = slice(k * column_vars, (k + 1) * column_vars)
+            near_cos, near_sin = near[rows, :LANES], near[rows, LANES:]
+            far_cos, far_sin = phase_ref[0, k : k + 1, cols], phase_ref[1, k : k + 1, cols]
+            real = real + (far_cos * near_cos - far_sin * near_sin)
+            imag = imag + (far_cos * near_sin + far_sin * near_cos)
+        reals.append(real)
+        imags.append(imag)
+    return jnp.concatenate(
+        [jnp.concatenate(reals, axis=1), jnp.concatenate(imags, axis=1)], axis=0
+    )
 
 
 def main_kernel(blocks, block, early, index_of, *refs):

time: 20.6 us -> 20.5 us (level)
  no operation moved by 1% of the time
where the time goes in v7:
time: 20.5 us; the launch traced here: 20.4 us
  starting transfers between devices  12.5 us (61%)
  Pallas kernels  4.74 us (23%)
  waiting for transfers between devices  2.36 us (12%)
  between operations  0.71 us (3%)
    ppermute x7, starting transfers between devices, body(): lax.ppermute(x, 'col', [(i, i ^ swap) for i in range(cols)])  10.6 us
    pallas_call x1, Pallas kernels, body(): pl.pallas_call(functools.partial(tables_kernel, blocks, block, early, hel...  2.36 us
    ppermute x3, waiting for transfers between devices, body(): ready.append(lax.ppermute(part, 'band', pairs))  2.01 us
    ppermute x3, starting transfers between devices, body(): ready.append(lax.ppermute(part, 'band', pairs))  1.92 us
    pallas_call x1, Pallas kernels, body(): pl.pallas_call(functools.partial(main_kernel, blocks, block, early, index...  1.01 us
    pallas_call x1, Pallas kernels, body(): pl.pallas_call(functools.partial(place_kernel, held), out_shape=jax.Shape...  0.88 us
    pallas_call x1, Pallas kernels, body(): pl.pallas_call(own_kernel, out_shape=spectra, in_specs=[VMEM_SPEC] * 3, o...  0.49 us
  transfers between devices with their start and end apart: 10, of which 4 were waited for; matrix products, arithmetic and copies ran while one was open for 0% of the time, Pallas kernels for 14%

profile of v7, /device:TPU:0, one launch (start us, length us, event | category | flops | bytes accessed | tf_op | source)
XLA Modules:
  0.0 20.4 jit_solution(693761389864800336)
XLA Ops:
  0.0 4.0 %collective-permute-start.1 = (bf16[40,640]{1,0:T(8,128)(2,1)}, bf16[40,640]{1,0:T(8,128)(2,1)S(1)}, u32[]{:S(2)}, u32[]{:S(2)}) collective-permute-start(bf16[40,640]{1,0:T(8,128)(2,1)} %bitcast.3), channel_id=1, source_target_pairs={{0,4},{1,5},{2,6},{3,7},{4,0},{5,1},{6,2},{7,3},{8,12},{9,13},{10,... | collective-permute-start | bytes 153608 | tf_op jit(solution)/shard_map/ppermute | solution.py:296
  4.0 1.5 %collective-permute-start = (bf16[40,640]{1,0:T(8,128)(2,1)}, bf16[40,640]{1,0:T(8,128)(2,1)S(1)}, u32[]{:S(2)}, u32[]{:S(2)}) collective-permute-start(bf16[40,640]{1,0:T(8,128)(2,1)} %bitcast.4), channel_id=1, source_target_pairs={{0,1},{1,0},{2,3},{3,2},{4,5},{5,4},{6,7},{7,6},{8,9},{9,8},{10,11... | collective-permute-start | bytes 153608 | tf_op jit(solution)/shard_map/ppermute | solution.py:296
  5.6 1.3 %collective-permute-start.5 = (bf16[40,640]{1,0:T(8,128)(2,1)}, bf16[40,640]{1,0:T(8,128)(2,1)S(1)}, u32[]{:S(2)}, u32[]{:S(2)}) collective-permute-start(bf16[40,640]{1,0:T(8,128)(2,1)} %bitcast.5), channel_id=1, source_target_pairs={{0,7},{1,6},{2,5},{3,4},{4,3},{5,2},{6,1},{7,0},{8,15},{9,14},{10,... | collective-permute-start | bytes 153608 | tf_op jit(solution)/shard_map/ppermute | solution.py:296
  6.8 0.5 %collective-permute-start.3 = (bf16[40,640]{1,0:T(8,128)(2,1)}, bf16[40,640]{1,0:T(8,128)(2,1)S(1)}, u32[]{:S(2)}, u32[]{:S(2)}) collective-permute-start(bf16[40,640]{1,0:T(8,128)(2,1)} %bitcast.6), channel_id=1, source_target_pairs={{0,3},{1,2},{2,1},{3,0},{4,7},{5,6},{6,5},{7,4},{8,11},{9,10},{10,... | collective-permute-start | bytes 153608 | tf_op jit(solution)/shard_map/ppermute | solution.py:296
  7.4 2.5 %collective-permute-start.2 = (bf16[40,640]{1,0:T(8,128)(2,1)}, bf16[40,640]{1,0:T(8,128)(2,1)S(1)}, u32[]{:S(2)}, u32[]{:S(2)}) collective-permute-start(bf16[40,640]{1,0:T(8,128)(2,1)} %bitcast.7), channel_id=1, source_target_pairs={{0,2},{1,3},{2,0},{3,1},{4,6},{5,7},{6,4},{7,5},{8,10},{9,11},{10,... | collective-permute-start | bytes 153608 | tf_op jit(solution)/shard_map/ppermute | solution.py:296
  9.8 0.0 collective-permute-done.1.refs_1_
  9.8 0.0 collective-permute-start.6
  9.9 0.0 collective-permute-done.refs_0_
  9.9 0.8 %collective-permute-start.4 = (bf16[40,640]{1,0:T(8,128)(2,1)S(1)}, bf16[40,640]{1,0:T(8,128)(2,1)S(1)}, u32[]{:S(2)}, u32[]{:S(2)}) collective-permute-start(bf16[40,640]{1,0:T(8,128)(2,1)S(1)} %collective-permute-done.1.refs_1_), channel_id=1, source_target_pairs={{0,1},{1,0},{2,3},{3,2},{4,5},{5,4},{6,7},{7,6},{8,9},{9,8},{10,11... | collective-permute-start | bytes 153608 | tf_op jit(solution)/shard_map/ppermute | solution.py:296
  11.3 2.4 %tables.1 = (bf16[640,1280]{1,0:T(8,128)(2,1)S(1)}, bf16[640,512]{1,0:T(8,128)(2,1)S(1)}, f32[2,8,768]{2,1,0:T(8,128)S(1)}, bf16[80,120]{1,0:T(8,128)(2,1)S(1)},...) custom-call(s32[1]{0:T(128)S(6)} %copy.6.lat_ref, s32[768]{0:T(1024)} %waves_hbm.1, ...), custom_call_target="tpu_custom_call" | custom-call | flops 209715200 | bytes 819200 | tf_op jit(solution)/shard_map/tables/pallas_call | solution.py:316
  13.7 0.0 collective-permute-done.5.refs_9_
  13.7 0.0 collective-permute-done.3.refs_7_
  13.7 0.0 collective-permute-done.2.refs_6_
  13.7 0.3 %collective-permute-done.6.refs_10_ = bf16[40,640]{1,0:T(8,128)(2,1)S(1)} collective-permute-done((bf16[40,640]{1,0:T(8,128)(2,1)S(1)}, bf16[40,640]{1,0:T(8,128)(2,1)S(1)}, u32[]{:S(2)}, u32[]{:S(2)}) %collective-permute-start.6) | collective-permute-done | bytes 51232 | tf_op jit(solution)/shard_map/ppermute | solution.py:296
  13.9 0.1 collective-permute-done.4.refs_8_
  14.0 1.0 %column_and_waves.1 = (bf16[320,640]{1,0:T(8,128)(2,1)S(1)}, bf16[80,192]{1,0:T(8,128)(2,1)S(1)}, bf16[80,192]{1,0:T(8,128)(2,1)S(1)}, bf16[80,192]{1,0:T(8,128)(2,1)S(1)}) custom-call(f32[1,128]{1,0:T(1,128)S(1)} %get-tuple-element.16.refs_0_, bf16[80,120]{1,0:T(8,128)(2,1)S(1)} %get-tuple-element.17.refs_1_, ...), custom_call_target="tpu_custom_call" | custom-call | flops 471859200 | bytes 819200 | tf_op jit(solution)/shard_map/column_and_waves/pallas_call | solution.py:344
  15.0 0.1 collective-permute-start.7
  15.1 1.6 %collective-permute-start.8 = (bf16[80,192]{1,0:T(8,128)(2,1)S(1)}, bf16[80,192]{1,0:T(8,128)(2,1)S(1)}, u32[]{:S(2)}, u32[]{:S(2)}) collective-permute-start(bf16[80,192]{1,0:T(8,128)(2,1)S(1)} %get-tuple-element.23), channel_id=1, source_target_pairs={{0,16},{8,24},{16,0},{24,8},{1,17},{9,25},{17,1},{25,9},{2,18},{10... | collective-permute-start | bytes 92168 | tf_op jit(solution)/shard_map/ppermute | solution.py:362
  16.7 0.3 %collective-permute-start.9 = (bf16[80,192]{1,0:T(8,128)(2,1)S(1)}, bf16[80,192]{1,0:T(8,128)(2,1)S(1)}, u32[]{:S(2)}, u32[]{:S(2)}) collective-permute-start(bf16[80,192]{1,0:T(8,128)(2,1)S(1)} %get-tuple-element.24), channel_id=1, source_target_pairs={{0,8},{8,0},{16,24},{24,16},{1,9},{9,1},{17,25},{25,17},{2,10},{10... | collective-permute-start | bytes 92168 | tf_op jit(solution)/shard_map/ppermute | solution.py:362
  17.0 0.5 %own_waves.1.refs_3_ = bf16[80,192]{1,0:T(8,128)(2,1)S(1)} custom-call(bf16[320,640]{1,0:T(8,128)(2,1)S(1)} %get-tuple-element.25.flat_ref, bf16[640,512]{1,0:T(8,128)(2,1)S(1)} %get-tuple-element.26.table_ref, f32[2,8,768]{2,1,0:T(8,128)S(1)} %get-tuple-element.19.refs_3_.phase_ref), custom_call_target="tpu_custom_call" | custom-call | flops 157286400 | bytes 819200 | tf_op jit(solution)/shard_map/own_waves/pallas_call | solution.py:364
  17.5 1.4 %collective-permute-done.7.refs_0_ = bf16[80,192]{1,0:T(8,128)(2,1)S(1)} collective-permute-done((bf16[80,192]{1,0:T(8,128)(2,1)S(1)}, bf16[80,192]{1,0:T(8,128)(2,1)S(1)}, u32[]{:S(2)}, u32[]{:S(2)}) %collective-permute-start.7) | collective-permute-done | bytes 30752 | tf_op jit(solution)/shard_map/ppermute | solution.py:362
  18.9 0.6 %collective-permute-done.8.refs_1_ = bf16[80,192]{1,0:T(8,128)(2,1)S(1)} collective-permute-done((bf16[80,192]{1,0:T(8,128)(2,1)S(1)}, bf16[80,192]{1,0:T(8,128)(2,1)S(1)}, u32[]{:S(2)}, u32[]{:S(2)}) %collective-permute-start.8) | collective-permute-done | bytes 30752 | tf_op jit(solution)/shard_map/ppermute | solution.py:362
  19.5 0.0 collective-permute-done.9.refs_2_
  19.5 0.9 %row_slots.1 = bf16[1,2,40,4,192]{4,3,2,1,0:T(4,128)(2,1)} custom-call(bf16[80,192]{1,0:T(8,128)(2,1)S(1)} %collective-permute-done.7.refs_0_, bf16[80,192]{1,0:T(8,128)(2,1)S(1)} %collective-permute-done.8.refs_1_, bf16[80,192]{1,0:T(8,128)(2,1)S(1)} %collective-permute-done.9.refs_2_, bf16[80,192]{1,0:T(8,128)(2,1)S(1)} %own_waves.1.refs_3_), custom_call_target="tpu_custom_call" | custom-call | tf_op jit(solution)/shard_map/row_slots/pallas_call | solution.py:378
Async XLA Ops:
  0.0 9.8 %collective-permute-start.1 = (bf16[40,640]{1,0:T(8,128)(2,1)}, bf16[40,640]{1,0:T(8,128)(2,1)S(1)}, u32[]{:S(2)}, u32[]{:S(2)}) collective-permute-start(bf16[40,640]{1,0:T(8,128)(2,1)} %bitcast.3), channel_id=1, source_target_pairs={{0,4},{1,5},{2,6},{3,7},{4,0},{5,1},{6,2},{7,3},{8,12},{9,13},{10,... | collective-permute-start | bytes 153608 | tf_op jit(solution)/shard_map/ppermute | solution.py:296
  4.0 5.8 %collective-permute-start = (bf16[40,640]{1,0:T(8,128)(2,1)}, bf16[40,640]{1,0:T(8,128)(2,1)S(1)}, u32[]{:S(2)}, u32[]{:S(2)}) collective-permute-start(bf16[40,640]{1,0:T(8,128)(2,1)} %bitcast.4), channel_id=1, source_target_pairs={{0,1},{1,0},{2,3},{3,2},{4,5},{5,4},{6,7},{7,6},{8,9},{9,8},{10,11... | collective-permute-start | bytes 153608 | tf_op jit(solution)/shard_map/ppermute | solution.py:296
  5.6 8.1 %collective-permute-start.5 = (bf16[40,640]{1,0:T(8,128)(2,1)}, bf16[40,640]{1,0:T(8,128)(2,1)S(1)}, u32[]{:S(2)}, u32[]{:S(2)}) collective-permute-start(bf16[40,640]{1,0:T(8,128)(2,1)} %bitcast.5), channel_id=1, source_target_pairs={{0,7},{1,6},{2,5},{3,4},{4,3},{5,2},{6,1},{7,0},{8,15},{9,14},{10,... | collective-permute-start | bytes 153608 | tf_op jit(solution)/shard_map/ppermute | solution.py:296
  6.8 6.8 %collective-permute-start.3 = (bf16[40,640]{1,0:T(8,128)(2,1)}, bf16[40,640]{1,0:T(8,128)(2,1)S(1)}, u32[]{:S(2)}, u32[]{:S(2)}) collective-permute-start(bf16[40,640]{1,0:T(8,128)(2,1)} %bitcast.6), channel_id=1, source_target_pairs={{0,3},{1,2},{2,1},{3,0},{4,7},{5,6},{6,5},{7,4},{8,11},{9,10},{10,... | collective-permute-start | bytes 153608 | tf_op jit(solution)/shard_map/ppermute | solution.py:296
  7.4 6.3 %collective-permute-start.2 = (bf16[40,640]{1,0:T(8,128)(2,1)}, bf16[40,640]{1,0:T(8,128)(2,1)S(1)}, u32[]{:S(2)}, u32[]{:S(2)}) collective-permute-start(bf16[40,640]{1,0:T(8,128)(2,1)} %bitcast.7), channel_id=1, source_target_pairs={{0,2},{1,3},{2,0},{3,1},{4,6},{5,7},{6,4},{7,5},{8,10},{9,11},{10,... | collective-permute-start | bytes 153608 | tf_op jit(solution)/shard_map/ppermute | solution.py:296
  9.8 4.1 %collective-permute-start.6 = (bf16[40,640]{1,0:T(8,128)(2,1)S(1)}, bf16[40,640]{1,0:T(8,128)(2,1)S(1)}, u32[]{:S(2)}, u32[]{:S(2)}) collective-permute-start(bf16[40,640]{1,0:T(8,128)(2,1)S(1)} %collective-permute-done.1.refs_1_), channel_id=1, source_target_pairs={{0,2},{1,3},{2,0},{3,1},{4,6},{5,7},{6,4},{7,5},{8,10},{9,11},{10,... | collective-permute-start | bytes 153608 | tf_op jit(solution)/shard_map/ppermute | solution.py:296
  9.9 4.2 %collective-permute-start.4 = (bf16[40,640]{1,0:T(8,128)(2,1)S(1)}, bf16[40,640]{1,0:T(8,128)(2,1)S(1)}, u32[]{:S(2)}, u32[]{:S(2)}) collective-permute-start(bf16[40,640]{1,0:T(8,128)(2,1)S(1)} %collective-permute-done.1.refs_1_), channel_id=1, source_target_pairs={{0,1},{1,0},{2,3},{3,2},{4,5},{5,4},{6,7},{7,6},{8,9},{9,8},{10,11... | collective-permute-start | bytes 153608 | tf_op jit(solution)/shard_map/ppermute | solution.py:296
  15.0 3.9 %collective-permute-start.7 = (bf16[80,192]{1,0:T(8,128)(2,1)S(1)}, bf16[80,192]{1,0:T(8,128)(2,1)S(1)}, u32[]{:S(2)}, u32[]{:S(2)}) collective-permute-start(bf16[80,192]{1,0:T(8,128)(2,1)S(1)} %get-tuple-element.22), channel_id=1, source_target_pairs={{0,24},{8,16},{16,8},{24,0},{1,25},{9,17},{17,9},{25,1},{2,26},{10... | collective-permute-start | bytes 92168 | tf_op jit(solution)/shard_map/ppermute | solution.py:362
  15.1 4.4 %collective-permute-start.8 = (bf16[80,192]{1,0:T(8,128)(2,1)S(1)}, bf16[80,192]{1,0:T(8,128)(2,1)S(1)}, u32[]{:S(2)}, u32[]{:S(2)}) collective-permute-start(bf16[80,192]{1,0:T(8,128)(2,1)S(1)} %get-tuple-element.23), channel_id=1, source_target_pairs={{0,16},{8,24},{16,0},{24,8},{1,17},{9,25},{17,1},{25,9},{2,18},{10... | collective-permute-start | bytes 92168 | tf_op jit(solution)/shard_map/ppermute | solution.py:362
  16.7 2.8 %collective-permute-start.9 = (bf16[80,192]{1,0:T(8,128)(2,1)S(1)}, bf16[80,192]{1,0:T(8,128)(2,1)S(1)}, u32[]{:S(2)}, u32[]{:S(2)}) collective-permute-start(bf16[80,192]{1,0:T(8,128)(2,1)S(1)} %get-tuple-element.24), channel_id=1, source_target_pairs={{0,8},{8,0},{16,24},{24,16},{1,9},{9,1},{17,25},{25,17},{2,10},{10... | collective-permute-start | bytes 92168 | tf_op jit(solution)/shard_map/ppermute | solution.py:362

commit v8 on v7

--- a/solution.py
+++ b/solution.py
@@ -226,7 +226,7 @@
         out_ref[...] = both[:, k * share : (k + 1) * share].astype(jnp.bfloat16)
 
 
-def own_kernel(flat_ref, table_ref, phase_ref, out_ref):
+def own_kernel(held, flat_ref, table_ref, phase_ref, out_ref, choose_ref):
     near = table_ref.shape[1] // 2
     column_vars, share = out_ref.shape[0] // 2, out_ref.shape[1]
     both = transform(
@@ -234,14 +234,8 @@
     )
     out_ref[...] = both[:, near - share :].astype(jnp.bfloat16)
 
-
-def place_kernel(held, *refs):
     parts = len(held)
-    in_refs = refs[:parts]
-    out_ref = refs[parts]
-    column_vars = out_ref.shape[2]
-    share = out_ref.shape[4]
-    total = parts * column_vars
+    total = choose_ref.shape[0]
     row = lax.broadcasted_iota(jnp.int32, (total, 1), 0)
     variable = jnp.floor((row.astype(jnp.float32) + 0.5) * (1.0 / parts)).astype(jnp.int32)
     slot = row - variable * parts
@@ -253,13 +247,26 @@
     target = variable
     for position, which in enumerate(held):
         target = jnp.where(step == which, target + position * column_vars, target)
-    choose = (target == lax.broadcasted_iota(jnp.int32, (total, total), 1)).astype(jnp.bfloat16)
+    choose_ref[...] = (target == lax.broadcasted_iota(jnp.int32, (total, total), 1)).astype(
+        jnp.bfloat16
+    )
+
+
+def place_kernel(choose_ref, *refs):
+    in_refs, (out_hbm, out_ref, sems) = refs[:-3], refs[-3:]
+    _, column_vars, parts, share = out_ref.shape
+    copies = []
+    choose = choose_ref[...]
     wide = [ref[...].astype(jnp.float32) for ref in in_refs]
     for half in range(2):
         rows = slice(half * column_vars, (half + 1) * column_vars)
         stacked = jnp.concatenate([w[rows] for w in wide], axis=0).astype(jnp.bfloat16)
         placed = jnp.dot(choose, stacked, preferred_element_type=jnp.float32)
-        out_ref[0, half] = placed.reshape(column_vars, parts, share).astype(jnp.bfloat16)
+        out_ref[half] = placed.reshape(column_vars, parts, share).astype(jnp.bfloat16)
+        copies.append(pltpu.make_async_copy(out_ref.at[half], out_hbm.at[0, half], sems.at[half]))
+        copies[half].start()
+    for copy in copies:
+        copy.wait()
 
 
 VMEM_SPEC = pl.BlockSpec(memory_space=pltpu.VMEM)
@@ -276,7 +283,7 @@
     tend = adjoint_tend.reshape(column_vars, width)
     traj = trajectory.reshape(column_vars, own)
 
-    direct = own % LANES == 0 and cols > 1 and cols & (cols - 1) == 0
+    direct = own % LANES == 0 and cols > 2 and cols & (cols - 1) == 0
     across = cols // 2
     swaps = [1, across]
     late_swaps = [2, 3, 5, 7, 6] if cols == 8 else [q for q in range(2, cols) if q != across]
@@ -360,29 +367,32 @@
     for step, part in zip(held, parts):
         pairs = [(i, partner(i, step, bands)) for i in range(bands)]
         ready.append(lax.ppermute(part, "band", pairs))
-    ready.append(
-        pl.pallas_call(
-            own_kernel,
-            out_shape=spectra,
-            in_specs=[VMEM_SPEC] * 3,
-            out_specs=VMEM_SPEC,
-            compiler_params=pltpu.CompilerParams(vmem_limit_bytes=24 * 1024 * 1024),
-            cost_estimate=pl.CostEstimate(
-                flops=4 * column_vars * width * share,
-                bytes_accessed=4 * column_vars * width,
-                transcendentals=0,
-            ),
-            name="own_waves",
-        )(flat, own_table, phase)
-    )
+    total = bands * column_vars
+    own_part, choose = pl.pallas_call(
+        functools.partial(own_kernel, held),
+        out_shape=[spectra, jax.ShapeDtypeStruct((total, total), jnp.bfloat16)],
+        in_specs=[VMEM_SPEC] * 3,
+        out_specs=[VMEM_SPEC] * 2,
+        compiler_params=pltpu.CompilerParams(vmem_limit_bytes=24 * 1024 * 1024),
+        cost_estimate=pl.CostEstimate(
+            flops=4 * column_vars * width * share,
+            bytes_accessed=4 * column_vars * width,
+            transcendentals=0,
+        ),
+        name="own_waves",
+    )(flat, own_table, phase)
     return pl.pallas_call(
-        functools.partial(place_kernel, held),
+        place_kernel,
         out_shape=jax.ShapeDtypeStruct((1, 2, column_vars, bands, share), jnp.bfloat16),
-        in_specs=[VMEM_SPEC] * bands,
-        out_specs=VMEM_SPEC,
+        in_specs=[VMEM_SPEC] * (1 + bands),
+        out_specs=HBM_SPEC,
+        scratch_shapes=[
+            pltpu.VMEM((2, column_vars, bands, share), jnp.bfloat16),
+            pltpu.SemaphoreType.DMA((2,)),
+        ],
         compiler_params=pltpu.CompilerParams(vmem_limit_bytes=16 * 1024 * 1024),
         name="row_slots",
-    )(*ready)
+    )(choose, *ready, own_part)
 
 
 def solution(mesh):

time: 20.5 us -> 20.5 us (level)
  no operation moved by 1% of the time
where the time goes in v8:
time: 20.5 us; the launch traced here: 20.4 us
  starting transfers between devices  12.5 us (61%)
  Pallas kernels  4.73 us (23%)
  waiting for transfers between devices  2.36 us (12%)
  between operations  0.71 us (3%)
    ppermute x7, starting transfers between devices, body(): lax.ppermute(x, 'col', [(i, i ^ swap) for i in range(cols)])  10.6 us
    pallas_call x1, Pallas kernels, body(): pl.pallas_call(functools.partial(tables_kernel, blocks, block, early, hel...  2.36 us
    ppermute x3, waiting for transfers between devices, body(): ready.append(lax.ppermute(part, 'band', pairs))  2.01 us
    ppermute x3, starting transfers between devices, body(): ready.append(lax.ppermute(part, 'band', pairs))  1.92 us
    pallas_call x1, Pallas kernels, body(): pl.pallas_call(functools.partial(main_kernel, blocks, block, early, index...  1.01 us
    pallas_call x1, Pallas kernels, body(): pl.pallas_call(place_kernel, out_shape=jax.ShapeDtypeStruct((1, 2, column...  0.87 us
    pallas_call x1, Pallas kernels, body(): pl.pallas_call(functools.partial(own_kernel, held), out_shape=[spectra, j...  0.49 us
  transfers between devices with their start and end apart: 10, of which 4 were waited for; matrix products, arithmetic and copies ran while one was open for 0% of the time, Pallas kernels for 14%

profile of v8, /device:TPU:0, one launch (start us, length us, event | category | flops | bytes accessed | tf_op | source)
XLA Modules:
  0.0 20.4 jit_solution(12130422669851572895)
XLA Ops:
  0.0 4.0 %collective-permute-start.1 = (bf16[40,640]{1,0:T(8,128)(2,1)}, bf16[40,640]{1,0:T(8,128)(2,1)S(1)}, u32[]{:S(2)}, u32[]{:S(2)}) collective-permute-start(bf16[40,640]{1,0:T(8,128)(2,1)} %bitcast.3), channel_id=1, source_target_pairs={{0,4},{1,5},{2,6},{3,7},{4,0},{5,1},{6,2},{7,3},{8,12},{9,13},{10,... | collective-permute-start | bytes 153608 | tf_op jit(solution)/shard_map/ppermute | solution.py:303
  4.0 1.5 %collective-permute-start = (bf16[40,640]{1,0:T(8,128)(2,1)}, bf16[40,640]{1,0:T(8,128)(2,1)S(1)}, u32[]{:S(2)}, u32[]{:S(2)}) collective-permute-start(bf16[40,640]{1,0:T(8,128)(2,1)} %bitcast.4), channel_id=1, source_target_pairs={{0,1},{1,0},{2,3},{3,2},{4,5},{5,4},{6,7},{7,6},{8,9},{9,8},{10,11... | collective-permute-start | bytes 153608 | tf_op jit(solution)/shard_map/ppermute | solution.py:303
  5.6 1.3 %collective-permute-start.5 = (bf16[40,640]{1,0:T(8,128)(2,1)}, bf16[40,640]{1,0:T(8,128)(2,1)S(1)}, u32[]{:S(2)}, u32[]{:S(2)}) collective-permute-start(bf16[40,640]{1,0:T(8,128)(2,1)} %bitcast.5), channel_id=1, source_target_pairs={{0,7},{1,6},{2,5},{3,4},{4,3},{5,2},{6,1},{7,0},{8,15},{9,14},{10,... | collective-permute-start | bytes 153608 | tf_op jit(solution)/shard_map/ppermute | solution.py:303
  6.8 0.5 %collective-permute-start.3 = (bf16[40,640]{1,0:T(8,128)(2,1)}, bf16[40,640]{1,0:T(8,128)(2,1)S(1)}, u32[]{:S(2)}, u32[]{:S(2)}) collective-permute-start(bf16[40,640]{1,0:T(8,128)(2,1)} %bitcast.6), channel_id=1, source_target_pairs={{0,3},{1,2},{2,1},{3,0},{4,7},{5,6},{6,5},{7,4},{8,11},{9,10},{10,... | collective-permute-start | bytes 153608 | tf_op jit(solution)/shard_map/ppermute | solution.py:303
  7.4 2.5 %collective-permute-start.2 = (bf16[40,640]{1,0:T(8,128)(2,1)}, bf16[40,640]{1,0:T(8,128)(2,1)S(1)}, u32[]{:S(2)}, u32[]{:S(2)}) collective-permute-start(bf16[40,640]{1,0:T(8,128)(2,1)} %bitcast.7), channel_id=1, source_target_pairs={{0,2},{1,3},{2,0},{3,1},{4,6},{5,7},{6,4},{7,5},{8,10},{9,11},{10,... | collective-permute-start | bytes 153608 | tf_op jit(solution)/shard_map/ppermute | solution.py:303
  9.8 0.0 collective-permute-done.1.refs_1_
  9.8 0.0 collective-permute-start.6
  9.9 0.0 collective-permute-done.refs_0_
  9.9 0.8 %collective-permute-start.4 = (bf16[40,640]{1,0:T(8,128)(2,1)S(1)}, bf16[40,640]{1,0:T(8,128)(2,1)S(1)}, u32[]{:S(2)}, u32[]{:S(2)}) collective-permute-start(bf16[40,640]{1,0:T(8,128)(2,1)S(1)} %collective-permute-done.1.refs_1_), channel_id=1, source_target_pairs={{0,1},{1,0},{2,3},{3,2},{4,5},{5,4},{6,7},{7,6},{8,9},{9,8},{10,11... | collective-permute-start | bytes 153608 | tf_op jit(solution)/shard_map/ppermute | solution.py:303
  11.3 2.4 %tables.1 = (bf16[640,1280]{1,0:T(8,128)(2,1)S(1)}, bf16[640,512]{1,0:T(8,128)(2,1)S(1)}, f32[2,8,768]{2,1,0:T(8,128)S(1)}, bf16[80,120]{1,0:T(8,128)(2,1)S(1)},...) custom-call(s32[1]{0:T(128)S(6)} %copy.6.lat_ref, s32[768]{0:T(1024)} %waves_hbm.1, ...), custom_call_target="tpu_custom_call" | custom-call | flops 209715200 | bytes 819200 | tf_op jit(solution)/shard_map/tables/pallas_call | solution.py:323
  13.7 0.0 collective-permute-done.5.refs_9_
  13.7 0.0 collective-permute-done.3.refs_7_
  13.7 0.0 collective-permute-done.2.refs_6_
  13.7 0.3 %collective-permute-done.6.refs_10_ = bf16[40,640]{1,0:T(8,128)(2,1)S(1)} collective-permute-done((bf16[40,640]{1,0:T(8,128)(2,1)S(1)}, bf16[40,640]{1,0:T(8,128)(2,1)S(1)}, u32[]{:S(2)}, u32[]{:S(2)}) %collective-permute-start.6) | collective-permute-done | bytes 51232 | tf_op jit(solution)/shard_map/ppermute | solution.py:303
  13.9 0.1 collective-permute-done.4.refs_8_
  14.0 1.0 %column_and_waves.1 = (bf16[320,640]{1,0:T(8,128)(2,1)S(1)}, bf16[80,192]{1,0:T(8,128)(2,1)S(1)}, bf16[80,192]{1,0:T(8,128)(2,1)S(1)}, bf16[80,192]{1,0:T(8,128)(2,1)S(1)}) custom-call(f32[1,128]{1,0:T(1,128)S(1)} %get-tuple-element.18.refs_0_, bf16[80,120]{1,0:T(8,128)(2,1)S(1)} %get-tuple-element.19.refs_1_, ...), custom_call_target="tpu_custom_call" | custom-call | flops 471859200 | bytes 819200 | tf_op jit(solution)/shard_map/column_and_waves/pallas_call | solution.py:351
  15.0 0.1 collective-permute-start.7
  15.1 1.6 %collective-permute-start.8 = (bf16[80,192]{1,0:T(8,128)(2,1)S(1)}, bf16[80,192]{1,0:T(8,128)(2,1)S(1)}, u32[]{:S(2)}, u32[]{:S(2)}) collective-permute-start(bf16[80,192]{1,0:T(8,128)(2,1)S(1)} %get-tuple-element.28), channel_id=1, source_target_pairs={{0,16},{8,24},{16,0},{24,8},{1,17},{9,25},{17,1},{25,9},{2,18},{10... | collective-permute-start | bytes 92168 | tf_op jit(solution)/shard_map/ppermute | solution.py:369
  16.7 0.3 %collective-permute-start.9 = (bf16[80,192]{1,0:T(8,128)(2,1)S(1)}, bf16[80,192]{1,0:T(8,128)(2,1)S(1)}, u32[]{:S(2)}, u32[]{:S(2)}) collective-permute-start(bf16[80,192]{1,0:T(8,128)(2,1)S(1)} %get-tuple-element.29), channel_id=1, source_target_pairs={{0,8},{8,0},{16,24},{24,16},{1,9},{9,1},{17,25},{25,17},{2,10},{10... | collective-permute-start | bytes 92168 | tf_op jit(solution)/shard_map/ppermute | solution.py:369
  17.0 0.5 %own_waves.1 = (bf16[80,192]{1,0:T(8,128)(2,1)S(1)}, bf16[160,160]{1,0:T(8,128)(2,1)S(1)}) custom-call(bf16[320,640]{1,0:T(8,128)(2,1)S(1)} %get-tuple-element.24.flat_ref, bf16[640,512]{1,0:T(8,128)(2,1)S(1)} %get-tuple-element.25.table_ref, f32[2,8,768]{2,1,0:T(8,128)S(1)} %get-tuple-element.21.refs_3_.phase_ref), custom_call_target="tpu_custom_call" | custom-call | flops 157286400 | bytes 819200 | tf_op jit(solution)/shard_map/own_waves/pallas_call | solution.py:371
  17.5 1.4 %collective-permute-done.7.refs_0_ = bf16[80,192]{1,0:T(8,128)(2,1)S(1)} collective-permute-done((bf16[80,192]{1,0:T(8,128)(2,1)S(1)}, bf16[80,192]{1,0:T(8,128)(2,1)S(1)}, u32[]{:S(2)}, u32[]{:S(2)}) %collective-permute-start.7) | collective-permute-done | bytes 30752 | tf_op jit(solution)/shard_map/ppermute | solution.py:369
  18.9 0.6 %collective-permute-done.8.refs_1_ = bf16[80,192]{1,0:T(8,128)(2,1)S(1)} collective-permute-done((bf16[80,192]{1,0:T(8,128)(2,1)S(1)}, bf16[80,192]{1,0:T(8,128)(2,1)S(1)}, u32[]{:S(2)}, u32[]{:S(2)}) %collective-permute-start.8) | collective-permute-done | bytes 30752 | tf_op jit(solution)/shard_map/ppermute | solution.py:369
  19.5 0.0 collective-permute-done.9.refs_2_
  19.5 0.9 %row_slots.1 = bf16[1,2,40,4,192]{4,3,2,1,0:T(4,128)(2,1)} custom-call(bf16[160,160]{1,0:T(8,128)(2,1)S(1)} %get-tuple-element.26.choose_ref, bf16[80,192]{1,0:T(8,128)(2,1)S(1)} %collective-permute-done.7.refs_0_, bf16[80,192]{1,0:T(8,128)(2,1)S(1)} %collective-permute-done.8.refs_1_, bf16[80,192]{1,0:T(8,128)(2,1)S(1)} %collective-permute-done.9.refs_2_, ...), custom_call_target="tpu_custom_call" | custom-call | tf_op jit(solution)/shard_map/row_slots/pallas_call | solution.py:384
Async XLA Ops:
  0.0 9.8 %collective-permute-start.1 = (bf16[40,640]{1,0:T(8,128)(2,1)}, bf16[40,640]{1,0:T(8,128)(2,1)S(1)}, u32[]{:S(2)}, u32[]{:S(2)}) collective-permute-start(bf16[40,640]{1,0:T(8,128)(2,1)} %bitcast.3), channel_id=1, source_target_pairs={{0,4},{1,5},{2,6},{3,7},{4,0},{5,1},{6,2},{7,3},{8,12},{9,13},{10,... | collective-permute-start | bytes 153608 | tf_op jit(solution)/shard_map/ppermute | solution.py:303
  4.0 5.8 %collective-permute-start = (bf16[40,640]{1,0:T(8,128)(2,1)}, bf16[40,640]{1,0:T(8,128)(2,1)S(1)}, u32[]{:S(2)}, u32[]{:S(2)}) collective-permute-start(bf16[40,640]{1,0:T(8,128)(2,1)} %bitcast.4), channel_id=1, source_target_pairs={{0,1},{1,0},{2,3},{3,2},{4,5},{5,4},{6,7},{7,6},{8,9},{9,8},{10,11... | collective-permute-start | bytes 153608 | tf_op jit(solution)/shard_map/ppermute | solution.py:303
  5.6 8.1 %collective-permute-start.5 = (bf16[40,640]{1,0:T(8,128)(2,1)}, bf16[40,640]{1,0:T(8,128)(2,1)S(1)}, u32[]{:S(2)}, u32[]{:S(2)}) collective-permute-start(bf16[40,640]{1,0:T(8,128)(2,1)} %bitcast.5), channel_id=1, source_target_pairs={{0,7},{1,6},{2,5},{3,4},{4,3},{5,2},{6,1},{7,0},{8,15},{9,14},{10,... | collective-permute-start | bytes 153608 | tf_op jit(solution)/shard_map/ppermute | solution.py:303
  6.8 6.8 %collective-permute-start.3 = (bf16[40,640]{1,0:T(8,128)(2,1)}, bf16[40,640]{1,0:T(8,128)(2,1)S(1)}, u32[]{:S(2)}, u32[]{:S(2)}) collective-permute-start(bf16[40,640]{1,0:T(8,128)(2,1)} %bitcast.6), channel_id=1, source_target_pairs={{0,3},{1,2},{2,1},{3,0},{4,7},{5,6},{6,5},{7,4},{8,11},{9,10},{10,... | collective-permute-start | bytes 153608 | tf_op jit(solution)/shard_map/ppermute | solution.py:303
  7.4 6.3 %collective-permute-start.2 = (bf16[40,640]{1,0:T(8,128)(2,1)}, bf16[40,640]{1,0:T(8,128)(2,1)S(1)}, u32[]{:S(2)}, u32[]{:S(2)}) collective-permute-start(bf16[40,640]{1,0:T(8,128)(2,1)} %bitcast.7), channel_id=1, source_target_pairs={{0,2},{1,3},{2,0},{3,1},{4,6},{5,7},{6,4},{7,5},{8,10},{9,11},{10,... | collective-permute-start | bytes 153608 | tf_op jit(solution)/shard_map/ppermute | solution.py:303
  9.8 4.1 %collective-permute-start.6 = (bf16[40,640]{1,0:T(8,128)(2,1)S(1)}, bf16[40,640]{1,0:T(8,128)(2,1)S(1)}, u32[]{:S(2)}, u32[]{:S(2)}) collective-permute-start(bf16[40,640]{1,0:T(8,128)(2,1)S(1)} %collective-permute-done.1.refs_1_), channel_id=1, source_target_pairs={{0,2},{1,3},{2,0},{3,1},{4,6},{5,7},{6,4},{7,5},{8,10},{9,11},{10,... | collective-permute-start | bytes 153608 | tf_op jit(solution)/shard_map/ppermute | solution.py:303
  9.9 4.2 %collective-permute-start.4 = (bf16[40,640]{1,0:T(8,128)(2,1)S(1)}, bf16[40,640]{1,0:T(8,128)(2,1)S(1)}, u32[]{:S(2)}, u32[]{:S(2)}) collective-permute-start(bf16[40,640]{1,0:T(8,128)(2,1)S(1)} %collective-permute-done.1.refs_1_), channel_id=1, source_target_pairs={{0,1},{1,0},{2,3},{3,2},{4,5},{5,4},{6,7},{7,6},{8,9},{9,8},{10,11... | collective-permute-start | bytes 153608 | tf_op jit(solution)/shard_map/ppermute | solution.py:303
  15.0 3.9 %collective-permute-start.7 = (bf16[80,192]{1,0:T(8,128)(2,1)S(1)}, bf16[80,192]{1,0:T(8,128)(2,1)S(1)}, u32[]{:S(2)}, u32[]{:S(2)}) collective-permute-start(bf16[80,192]{1,0:T(8,128)(2,1)S(1)} %get-tuple-element.27), channel_id=1, source_target_pairs={{0,24},{8,16},{16,8},{24,0},{1,25},{9,17},{17,9},{25,1},{2,26},{10... | collective-permute-start | bytes 92168 | tf_op jit(solution)/shard_map/ppermute | solution.py:369
  15.1 4.4 %collective-permute-start.8 = (bf16[80,192]{1,0:T(8,128)(2,1)S(1)}, bf16[80,192]{1,0:T(8,128)(2,1)S(1)}, u32[]{:S(2)}, u32[]{:S(2)}) collective-permute-start(bf16[80,192]{1,0:T(8,128)(2,1)S(1)} %get-tuple-element.28), channel_id=1, source_target_pairs={{0,16},{8,24},{16,0},{24,8},{1,17},{9,25},{17,1},{25,9},{2,18},{10... | collective-permute-start | bytes 92168 | tf_op jit(solution)/shard_map/ppermute | solution.py:369
  16.7 2.8 %collective-permute-start.9 = (bf16[80,192]{1,0:T(8,128)(2,1)S(1)}, bf16[80,192]{1,0:T(8,128)(2,1)S(1)}, u32[]{:S(2)}, u32[]{:S(2)}) collective-permute-start(bf16[80,192]{1,0:T(8,128)(2,1)S(1)} %get-tuple-element.29), channel_id=1, source_target_pairs={{0,8},{8,0},{16,24},{24,16},{1,9},{9,1},{17,25},{25,17},{2,10},{10... | collective-permute-start | bytes 92168 | tf_op jit(solution)/shard_map/ppermute | solution.py:369
